TPU v7x, 256 devices: a whole 4x4x8 slice. The times are simulated.
256 devices in a mesh: expert: 32 (over z, y), hidden: 8 (over x, core).
Axes of the slice: x: 4, y: 4, z: 8, core: 2. Of those that a mesh axis runs over, the one named last changes fastest.
Arguments:
- tokens: bfloat16 [1024, 7168], P('expert'), may hold values from -6 to 6
- grad_out: bfloat16 [1024, 7168], P('expert'), may hold values from -1.5 to 1.5
- routes: int32 [1024, 8], P('expert'), may hold values from 0 to 31, all different within a row; in each aligned block of 32 rows (0 to 31, 32 to 63, ...) at most 16 rows name the same one
- gating: bfloat16 [1024, 8], P('expert'), may hold values from 0.19921875 to 1
- w_gate: bfloat16 [32, 7168, 1024], P('expert', None, 'hidden'), may hold values from -0.0625 to 0.0625
- w_up: bfloat16 [32, 7168, 1024], P('expert', None, 'hidden'), may hold values from -0.0625 to 0.0625
- w_down: bfloat16 [32, 1024, 7168], P('expert', 'hidden'), may hold values from -0.1875 to 0.1875
Outputs:
- grad_tokens: bfloat16 [1024, 7168], P('expert', 'hidden')
- grad_gating: float32 [1024, 8], P('expert')
- grad_w_gate: bfloat16 [32, 7168, 1024], P('expert', None, 'hidden')
- grad_w_up: bfloat16 [32, 7168, 1024], P('expert', None, 'hidden')
- grad_w_down: bfloat16 [32, 1024, 7168], P('expert', 'hidden')
Inputs may be any that keep to these rules, and one draw needn't show every extreme that they name: `routes`: each row names 8 different experts; in the rows of one token owner no expert is named by more than 16 rows, and in some owners' rows an expert is named by exactly 16 rows. Every expert is named somewhere.
All inputs are finite; a program needn't handle non-finite values.
Results may differ from a plain program's by a relative error of at most 0.019.
Values may be sent and summed in bfloat16 or wider, within the bound.
No kernel may reach another device: no remote copies, remote signals or barrier semaphores. Data moves between devices by JAX's collectives and lax.ppermute only.
A program may use at most 192 MiB of HBM per device.

v0:
```python
import jax
import jax.numpy as jnp
from jax import lax
from jax.sharding import PartitionSpec as P


def silu_parts(pre):
    sig = jax.nn.sigmoid(pre)
    return (pre * sig, sig * (1.0 + pre * (1.0 - sig)))


def build_sends(x_src, dy_src, gating, target, token_index, slot_rows, groups):
    send_x = jnp.zeros((slot_rows, x_src.shape[1]), jnp.bfloat16).at[target].set(x_src[token_index])
    send_dy = (
        jnp.zeros((slot_rows, dy_src.shape[1]), jnp.bfloat16).at[target].set(dy_src[token_index])
    )
    send_gate = jnp.zeros((slot_rows,), jnp.bfloat16).at[target].set(gating.reshape(-1))
    return (
        send_x.reshape(groups, -1, x_src.shape[1]),
        send_dy.reshape(groups, -1, dy_src.shape[1]),
        send_gate.reshape(groups, -1),
    )


def local(tokens, grad_out, routes, gating, w_gate, w_up, w_down):
    groups = lax.axis_size("expert")
    members = w_gate.shape[0]
    experts_all = groups * members
    tok_count = tokens.shape[0]
    topk = routes.shape[1]
    width = tokens.shape[1]
    capacity = min(
        tok_count, 8 * ((5 * tok_count * topk + 32 * experts_all - 1) // (32 * experts_all))
    )
    slot_rows = experts_all * capacity
    flat_routes = routes.reshape(-1)
    onehot = (flat_routes[:, None] == jnp.arange(experts_all, dtype=jnp.int32)[None, :]).astype(
        jnp.int32
    )
    before = jnp.cumsum(onehot, axis=0) - onehot
    slots = jnp.sum(before * onehot, axis=1)
    target = flat_routes * capacity + slots
    token_index = jnp.arange(tok_count * topk, dtype=jnp.int32) // topk
    sends = build_sends(tokens, grad_out, gating, target, token_index, slot_rows, groups)
    recv_x, recv_dy, recv_gate = (
        lax.all_to_all(sends[0], "expert", split_axis=0, concat_axis=0, tiled=True),
        lax.all_to_all(sends[1], "expert", split_axis=0, concat_axis=0, tiled=True),
        lax.all_to_all(sends[2], "expert", split_axis=0, concat_axis=0, tiled=True),
    )
    rows_x = recv_x.reshape(-1, width)
    rows_dy = recv_dy.reshape(-1, width)
    weight_col = recv_gate.reshape(-1, 1).astype(jnp.float32)
    wgate = w_gate[0]
    wup = w_up[0]
    wdown = w_down[0]
    pre_gate = jnp.dot(rows_x, wgate, preferred_element_type=jnp.float32)
    pre_up = jnp.dot(rows_x, wup, preferred_element_type=jnp.float32)
    back = lax.dot_general(
        rows_dy, wdown, (((1,), (1,)), ((), ())), preferred_element_type=jnp.float32
    )
    silu_val, silu_grad = silu_parts(pre_gate)
    act = silu_val * pre_up
    gate_list = jnp.sum(act * back, axis=1).reshape(groups, capacity)
    weighted = (weight_col * act).astype(jnp.bfloat16)
    grads_down = [
        lax.dot_general(
            weighted, rows_dy, (((0,), (0,)), ((), ())), preferred_element_type=jnp.float32
        ).astype(jnp.bfloat16)
    ]
    dact = weight_col * back
    d_up = (dact * silu_val).astype(jnp.bfloat16)
    d_gate = (dact * pre_up * silu_grad).astype(jnp.bfloat16)
    grads_gate = [
        lax.dot_general(
            rows_x, d_gate, (((0,), (0,)), ((), ())), preferred_element_type=jnp.float32
        ).astype(jnp.bfloat16)
    ]
    grads_up = [
        lax.dot_general(
            rows_x, d_up, (((0,), (0,)), ((), ())), preferred_element_type=jnp.float32
        ).astype(jnp.bfloat16)
    ]
    partial_value = lax.dot_general(
        d_gate, wgate, (((1,), (1,)), ((), ())), preferred_element_type=jnp.float32
    )
    partial_value = partial_value + lax.dot_general(
        d_up, wup, (((1,), (1,)), ((), ())), preferred_element_type=jnp.float32
    )
    partial_list = partial_value.reshape(groups, capacity, width)
    gate_all = gate_list
    reduced = lax.psum_scatter(
        partial_list.astype(jnp.bfloat16), "hidden", scatter_dimension=2, tiled=True
    ).astype(jnp.float32)
    gate_all = lax.psum(gate_all, "hidden")
    back_rows, back_gate = (
        lax.all_to_all(
            reduced.astype(jnp.bfloat16), "expert", split_axis=0, concat_axis=0, tiled=True
        ).astype(reduced.dtype),
        lax.all_to_all(
            gate_all.astype(jnp.bfloat16), "expert", split_axis=0, concat_axis=0, tiled=True
        ).astype(gate_all.dtype),
    )
    flat_rows = back_rows.reshape(slot_rows, -1)
    picked = flat_rows[target].reshape(tok_count, topk, -1)
    grad_tokens = jnp.sum(picked, axis=1).astype(jnp.bfloat16)
    gate_vals = back_gate.reshape(-1)[target].reshape(tok_count, topk)
    return (
        grad_tokens,
        gate_vals,
        jnp.stack(grads_gate),
        jnp.stack(grads_up),
        jnp.stack(grads_down),
    )


def solution(mesh):
    placed = (
        P("expert", None),
        P("expert", None),
        P("expert", None),
        P("expert", None),
        P("expert", None, "hidden"),
        P("expert", None, "hidden"),
        P("expert", "hidden", None),
    )
    return jax.shard_map(
        local,
        mesh=mesh,
        in_specs=placed,
        out_specs=(
            P("expert", "hidden"),
            P("expert", None),
            P("expert", None, "hidden"),
            P("expert", None, "hidden"),
            P("expert", "hidden", None),
        ),
        check_vma=False,
    )
```

profile of v0, /device:TPU:17, one launch (start us, length us, event | category | flops | bytes accessed | tf_op | source)
XLA Modules:
  0.0 675.3 jit_solution(15762545007012533419)
XLA Ops:
  13.8 11.3 %all-to-all-start = ((bf16[32,1,16]{2,1,0:T(2,128)(2,1)}), bf16[32,1,16]{2,1,0:T(2,128)(2,1)S(1)}, u32[]{:S(2)}, u32[]{:S(2)}) async-start(bf16[32,1,16]{2,1,0:T(2,128)(2,1)} %all_to_all.28), calls=%async_computation | async-start | bytes 32768 | tf_op jit(solution)/shard_map/all_to_all | solution.py:48
  25.2 20.1 %scatter_custom_fusion.2 = bf16[512,7168]{1,0:T(8,128)(2,1)} fusion(s32[256]{0:T(256)S(1)} %bitcast.78, bf16[32,7168]{1,0:T(8,128)(2,1)} %param.7, s32[1024]{0:T(1024)S(1)} %pad_clamp_fusion.1, bf16[]{:T(256)} %constant.26.clone.1), kind=kCustom, calls=%fused_computation.14 | custom fusion | bytes 7340544 | tf_op jit(solution)/shard_map/scatter | solution.py:13
  45.3 9.3 %all-to-all-start.2 = ((bf16[32,16,7168]{2,1,0:T(8,128)(2,1)}), bf16[32,16,7168]{2,1,0:T(8,128)(2,1)}, u32[]{:S(2)}, u32[]{:S(2)}) async-start(bf16[32,16,7168]{2,1,0:T(8,128)(2,1)} %bitcast.73), calls=%async_computation.2 | async-start | bytes 14680064 | tf_op jit(solution)/shard_map/all_to_all | solution.py:46
  54.6 19.8 %scatter_custom_fusion.1 = bf16[512,7168]{1,0:T(8,128)(2,1)} fusion(s32[256]{0:T(256)S(1)} %bitcast.79, bf16[32,7168]{1,0:T(8,128)(2,1)} %param.8, s32[1024]{0:T(1024)S(1)} %pad_clamp_fusion.1, bf16[]{:T(256)} %constant.26.clone.1), kind=kCustom, calls=%fused_computation.16 | custom fusion | bytes 7340544 | tf_op jit(solution)/shard_map/scatter | solution.py:15
  74.4 140.4 %all-to-all-done.2 = bf16[32,16,7168]{2,1,0:T(8,128)(2,1)} async-done(((bf16[32,16,7168]{2,1,0:T(8,128)(2,1)}), bf16[32,16,7168]{2,1,0:T(8,128)(2,1)}, u32[]{:S(2)}, u32[]{:S(2)}) %all-to-all-start.2) | async-done | bytes 7340064 | tf_op jit(solution)/shard_map/all_to_all | solution.py:46
  214.8 12.6 %all-to-all-start.1 = ((bf16[32,16,7168]{2,1,0:T(8,128)(2,1)}), bf16[32,16,7168]{2,1,0:T(8,128)(2,1)}, u32[]{:S(2)}, u32[]{:S(2)}) async-start(bf16[32,16,7168]{2,1,0:T(8,128)(2,1)} %bitcast.72), calls=%async_computation.1 | async-start | bytes 14680064 | tf_op jit(solution)/shard_map/all_to_all | solution.py:47
  227.6 5.8 fusion.11
  233.3 5.7 fusion.14
  239.0 148.1 %all-to-all-done.1 = bf16[32,16,7168]{2,1,0:T(8,128)(2,1)} async-done(((bf16[32,16,7168]{2,1,0:T(8,128)(2,1)}), bf16[32,16,7168]{2,1,0:T(8,128)(2,1)}, u32[]{:S(2)}, u32[]{:S(2)}) %all-to-all-start.1) | async-done | bytes 7340064 | tf_op jit(solution)/shard_map/all_to_all | solution.py:47
  387.1 6.2 multiply_reduce_fusion
  393.3 7.3 %fusion.9 = f32[512,7168]{1,0:T(8,128)} fusion(bf16[512,128]{0,1:T(8,128)(2,1)S(1)} %get-tuple-element.16, bf16[1,7168,128]{2,1,0:T(8,128)(2,1)S(1)} %copy-done), kind=kOutput, calls=%fused_computation.20 | convolution fusion | flops 939524096 | bytes 16646144 | tf_op jit(solution)/shard_map/dot_general | solution.py:83
  400.6 10.4 %add_convert_fusion = bf16[512,7168]{1,0:T(8,128)(2,1)} fusion(f32[512,7168]{1,0:T(8,128)} %fusion.9, bf16[512,128]{0,1:T(8,128)(2,1)S(1)} %get-tuple-element.17, bf16[1,7168,128]{2,1,0:T(8,128)(2,1)S(1)} %copy-done.3), kind=kOutput, calls=%fused_computation.7 | convolution fusion | flops 946864128 | bytes 23986176 | tf_op jit(solution)/shard_map/dot_general | solution.py:86
  411.0 49.3 %copy.26 = bf16[32,16,7168]{1,0,2:T(8,128)(2,1)} copy(bf16[32,16,7168]{2,1,0:T(8,128)(2,1)} %bitcast.75) | data formatting | bytes 14680064
  460.3 95.8 %reshape.223 = bf16[7168,512]{1,0:T(8,128)(2,1)} reshape(bf16[7168,32,16]{2,1,0:T(8,128)(2,1)} %bitcast.71) | data formatting | bytes 14680064
  556.2 22.7 %psum.7 = bf16[32,16]{1,0:T(8,128)(2,1)S(1)} all-reduce(f32[32,16]{1,0:T(8,128)S(1)} %reshape.161), channel_id=1, replica_groups=mesh['expert'=32,'hidden'=8] {'hidden'}, use_global_device_ids=true, to_apply=%region_9.10 | all-reduce | flops 512 | bytes 3072 | tf_op jit(solution)/shard_map/psum | solution.py:94
  579.5 13.4 %all-to-all-start.4 = ((bf16[32,1,16]{2,1,0:T(2,128)(2,1)}), bf16[32,1,16]{2,1,0:T(2,128)(2,1)S(1)}, u32[]{:S(2)}, u32[]{:S(2)}) async-start(bf16[32,1,16]{2,1,0:T(2,128)(2,1)} %copy.24), calls=%async_computation.4 | async-start | bytes 32768 | tf_op jit(solution)/shard_map/all_to_all | solution.py:99
  593.0 18.7 %reduce-scatter.4.cloned.1.call-done = bf16[896,512]{1,0:T(8,128)(2,1)} async-done(((bf16[7168,512]{1,0:T(8,128)(2,1)}), bf16[896,512]{1,0:T(8,128)(2,1)}) %reduce-scatter.4.cloned.1.call-update) | async-done | bytes 917520
  611.7 8.5 %reshape.224 = bf16[896,32,16]{2,1,0:T(8,128)(2,1)} reshape(bf16[896,512]{1,0:T(8,128)(2,1)} %reduce-scatter.4.cloned.1.call-done) | data formatting | bytes 1835008
  620.2 9.6 %copy.27 = bf16[32,16,896]{2,1,0:T(8,128)(2,1)} copy(bf16[32,16,896]{1,0,2:T(8,128)(2,1)} %bitcast.74) | data formatting | bytes 1835008
  629.8 9.9 %all-to-all-start.3 = ((bf16[32,16,896]{2,1,0:T(8,128)(2,1)}), bf16[32,16,896]{2,1,0:T(8,128)(2,1)S(1)}, u32[]{:S(2)}, u32[]{:S(2)}) async-start(bf16[32,16,896]{2,1,0:T(8,128)(2,1)} %copy.27), calls=%async_computation.3 | async-start | bytes 1835008 | tf_op jit(solution)/shard_map/all_to_all | solution.py:96
  639.7 5.5 fusion.2
  645.2 6.4 fusion
  651.6 6.4 fusion.1
  664.3 3.0 gather_fusion
  (44 shorter events, 14.6 us)
Async XLA Ops:
  7.2 220.4 %copy-start = (bf16[1,7168,128]{2,1,0:T(8,128)(2,1)S(1)}, bf16[1,7168,128]{2,1,0:T(8,128)(2,1)}, u32[]{:S(2)}) copy-start(bf16[1,7168,128]{2,1,0:T(8,128)(2,1)} %param.11) | copy-start | bytes 5505028
  13.8 31.5 %all-to-all-start = ((bf16[32,1,16]{2,1,0:T(2,128)(2,1)}), bf16[32,1,16]{2,1,0:T(2,128)(2,1)S(1)}, u32[]{:S(2)}, u32[]{:S(2)}) async-start(bf16[32,1,16]{2,1,0:T(2,128)(2,1)} %all_to_all.28), calls=%async_computation | async-start | bytes 32768 | tf_op jit(solution)/shard_map/all_to_all | solution.py:48
  45.3 169.5 %all-to-all-start.2 = ((bf16[32,16,7168]{2,1,0:T(8,128)(2,1)}), bf16[32,16,7168]{2,1,0:T(8,128)(2,1)}, u32[]{:S(2)}, u32[]{:S(2)}) async-start(bf16[32,16,7168]{2,1,0:T(8,128)(2,1)} %bitcast.73), calls=%async_computation.2 | async-start | bytes 14680064 | tf_op jit(solution)/shard_map/all_to_all | solution.py:46
  214.8 172.3 %all-to-all-start.1 = ((bf16[32,16,7168]{2,1,0:T(8,128)(2,1)}), bf16[32,16,7168]{2,1,0:T(8,128)(2,1)}, u32[]{:S(2)}, u32[]{:S(2)}) async-start(bf16[32,16,7168]{2,1,0:T(8,128)(2,1)} %bitcast.72), calls=%async_computation.1 | async-start | bytes 14680064 | tf_op jit(solution)/shard_map/all_to_all | solution.py:47
  227.4 384.3 %reduce-scatter.4.cloned.1.call-start = ((), (), s32[]{:S(2)}) async-start(), calls=%async_computation.6 | async-start | bytes 8257536
  227.5 5.8 copy-start.2
  393.3 7.3 %copy-start.3 = (bf16[1,7168,128]{2,1,0:T(8,128)(2,1)S(1)}, bf16[1,7168,128]{2,1,0:T(8,128)(2,1)}, u32[]{:S(2)}) copy-start(bf16[1,7168,128]{2,1,0:T(8,128)(2,1)} %param.12) | copy-start | bytes 5505028
  579.5 50.3 %all-to-all-start.4 = ((bf16[32,1,16]{2,1,0:T(2,128)(2,1)}), bf16[32,1,16]{2,1,0:T(2,128)(2,1)S(1)}, u32[]{:S(2)}, u32[]{:S(2)}) async-start(bf16[32,1,16]{2,1,0:T(2,128)(2,1)} %copy.24), calls=%async_computation.4 | async-start | bytes 32768 | tf_op jit(solution)/shard_map/all_to_all | solution.py:99
  629.8 33.1 %all-to-all-start.3 = ((bf16[32,16,896]{2,1,0:T(8,128)(2,1)}), bf16[32,16,896]{2,1,0:T(8,128)(2,1)S(1)}, u32[]{:S(2)}, u32[]{:S(2)}) async-start(bf16[32,16,896]{2,1,0:T(8,128)(2,1)} %copy.27), calls=%async_computation.3 | async-start | bytes 1835008 | tf_op jit(solution)/shard_map/all_to_all | solution.py:96
  662.9 5.3 copy-start.1
Sparse Core Ops, SparseCore 0:
  556.2 55.4 reduce-scatter.3
where the time goes:
time: 683 us; the launch traced here: 675 us
  waiting for transfers between devices  309 us (45%)
  local copies, waits for them, and re-layouts  215 us (31%)
  starting transfers between devices  56.5 us (8%)
  matrix products  53.7 us (8%)
  blocking collectives  22.7 us (3%)
  between operations  14.5 us (2%)
    unnamed x15, local copies, waits for them, and re-layouts  165 us
    all_to_all x1, waiting for transfers between devices, local(): lax.all_to_all(sends[1], 'expert', split_axis=0, concat_axis=0, tiled=True)  148 us
    all_to_all x1, waiting for transfers between devices, local(): lax.all_to_all(sends[0], 'expert', split_axis=0, concat_axis=0, tiled=True)  140 us
    psum x1, blocking collectives, local(): gate_all = lax.psum(gate_all, 'hidden')  22.7 us
    scatter x1, local copies, waits for them, and re-layouts, build_sends(): jnp.zeros((slot_rows, x_src.shape[1]), jnp.bfloat16).at[target]  20.1 us
    scatter x1, local copies, waits for them, and re-layouts, build_sends(): jnp.zeros((slot_rows, dy_src.shape[1]), jnp.bfloat16).at[target]  19.8 us
    unnamed x2, waiting for transfers between devices  18.7 us
  transfers between devices with their start and end apart: 6, of which 4 were waited for; matrix products, arithmetic and copies ran while one was open for 14% of the time, Pallas kernels for 0%

commit v1 on v0

v1 whole, which is shorter than its diff:
```python
import functools

import jax
import jax.numpy as jnp
from jax import lax
from jax.experimental import pallas as pl
from jax.experimental.pallas import tpu as pltpu
from jax.sharding import PartitionSpec as P

CAP = 16
CHIPS = 4
BF = jnp.bfloat16
F32 = jnp.float32
VMEM_LIMIT = 40 * 1024 * 1024

NN = (((1,), (0,)), ((), ()))
NT = (((1,), (1,)), ((), ()))
TN = (((0,), (0,)), ((), ()))


def mm(a, b, dims):
    return lax.dot_general(a, b, dims, preferred_element_type=F32)


def call(body, out_shape, flops=0, moved=0, **kw):
    return pl.pallas_call(
        body,
        out_shape=out_shape,
        compiler_params=pltpu.CompilerParams(vmem_limit_bytes=VMEM_LIMIT),
        cost_estimate=pl.CostEstimate(flops=flops, bytes_accessed=moved, transcendentals=0),
        **kw,
    )


def shape(dims, dtype):
    return jax.ShapeDtypeStruct(dims, dtype)


VM = pl.BlockSpec(memory_space=pltpu.VMEM)
SM = pl.BlockSpec(memory_space=pltpu.SMEM)


def select_rows(routes, gates, rows, experts):
    count, topk = routes.shape
    lane = lax.broadcasted_iota(jnp.int32, (count, experts), 1)
    named = jnp.zeros((count, experts), F32)
    weight = jnp.zeros((count, experts), F32)
    for k in range(topk):
        hit = routes[:, k : k + 1] == lane
        named = jnp.where(hit, 1.0, named)
        weight = jnp.where(hit, gates[:, k : k + 1].astype(F32), weight)
    earlier = (
        lax.broadcasted_iota(jnp.int32, (count, count), 1) < lax.broadcasted_iota(jnp.int32, (count, count), 0)
    ).astype(F32)
    slot = mm(earlier.astype(BF), named.astype(BF), NN)
    slot = jnp.where(named > 0, slot, 2.0 * CAP)
    row = lax.broadcasted_iota(jnp.int32, (rows, experts), 0)
    owner = (row // CAP == lax.broadcasted_iota(jnp.int32, (rows, experts), 1)).astype(F32).astype(BF)
    slot_of = mm(owner, slot.astype(BF), NT)
    weight_of = mm(owner, weight.astype(BF), NT)
    place = (lax.broadcasted_iota(jnp.int32, (rows, count), 0) % CAP).astype(F32)
    pick = jnp.where(slot_of == place, 1.0, 0.0)
    return pick, pick * weight_of


def prepare_body(experts, at, routes, gates, x, dy, send_x, send_dy):
    rows = send_x.shape[0]
    pick, weighted = select_rows(routes[...], gates[...], rows, experts)
    send_x[...] = mm(pick.astype(BF), x[...], NN).astype(BF)
    send_dy[...] = mm(weighted.astype(BF), dy[...], NN).astype(BF)


def prepare(at, routes, gates, tokens, grad_out, experts):
    count, width = tokens.shape
    block = width // (2 * CHIPS)
    rows = experts * CAP
    whole = lambda i, at: (0, 0)
    mine = lambda i, at: (0, 2 * at[0] + at[1])
    return call(
        functools.partial(prepare_body, experts),
        (shape((rows, block), BF), shape((rows, block), BF)),
        flops=4 * rows * count * block,
        moved=8 * rows * block,
        grid_spec=pltpu.PrefetchScalarGridSpec(
            num_scalar_prefetch=1,
            grid=(1,),
            in_specs=[
                pl.BlockSpec(routes.shape, whole),
                pl.BlockSpec(gates.shape, whole),
                pl.BlockSpec((count, block), mine),
                pl.BlockSpec((count, block), mine),
            ],
            out_specs=[pl.BlockSpec((rows, block), whole), pl.BlockSpec((rows, block), whole)],
        ),
    )(at, routes, gates, tokens, grad_out)


def copy_body(at, *refs):
    half = len(refs) // 2
    for source, target in zip(refs[:half], refs[half:]):
        target[0] = source[...]


def halves(at, w_gate, w_up, w_down):
    depth, units = w_gate.shape
    block = depth // (2 * CHIPS)
    other = lambda r, at: 2 * ((at[0] + r) % CHIPS) + 1 - at[1]
    down = pl.BlockSpec((block, units), lambda r, at: (other(r, at), 0))
    wide = pl.BlockSpec((units, block), lambda r, at: (0, other(r, at)))
    out = pl.BlockSpec((1, block, units), lambda r, at: (r, 0, 0))
    out_wide = pl.BlockSpec((1, units, block), lambda r, at: (r, 0, 0))
    return call(
        copy_body,
        (
            shape((CHIPS, block, units), BF),
            shape((CHIPS, block, units), BF),
            shape((CHIPS, units, block), BF),
        ),
        moved=12 * CHIPS * block * units,
        grid_spec=pltpu.PrefetchScalarGridSpec(
            num_scalar_prefetch=1,
            grid=(CHIPS,),
            in_specs=[down, down, wide],
            out_specs=[out, out, out_wide],
        ),
    )(at, w_gate, w_up, w_down)


def block_at(at, r):
    return 2 * lax.rem(at[0] + r, CHIPS) + at[1]


def tall(ref, at, r, block):
    return ref[pl.ds(pl.multiple_of(block_at(at, r) * block, 128), block), :]


def wide(ref, at, r, block):
    return ref[:, pl.ds(pl.multiple_of(block_at(at, r) * block, 128), block)]


def pre_weights(at, gate, up, gate_other, up_other, r, block):
    return jnp.concatenate(
        [tall(gate, at, r, block), gate_other[r], tall(up, at, r, block), up_other[r]], axis=1
    )


def blocks_of(own, right, left, opp_a, opp_b, lo, hi, half):
    far = opp_a[...] if lo < half else opp_b[...]
    return (own[lo:hi, :], right[lo:hi, :], far, left[lo:hi, :])


def pre_body(at, own, right, left, opp_a, opp_b, gate, up, gate_other, up_other, keep, send):
    rows, block = own.shape
    half = rows // 2
    units = gate.shape[1]
    for r in range(CHIPS):
        weights = pre_weights(at, gate, up, gate_other, up_other, r, block)
        for lo in (0, half):
            part = mm(blocks_of(own, right, left, opp_a, opp_b, lo, lo + half, half)[r], weights, NN)
            if r == 0:
                keep[lo : lo + half, :] = part
            else:
                keep[lo : lo + half, :] += part
    for i, j in ((0, 1), (1, 0), (2, 3), (3, 2)):
        send[:, i * units : (i + 1) * units] = keep[:, j * units : (j + 1) * units]


def back_body(at, own, right, left, opp_a, opp_b, down, down_other, keep, send):
    rows, block = own.shape
    half = rows // 2
    units = down.shape[0]
    for r in range(CHIPS):
        weights = jnp.concatenate([wide(down, at, r, block), down_other[r]], axis=0)
        for lo in (0, half):
            part = mm(blocks_of(own, right, left, opp_a, opp_b, lo, lo + half, half)[r], weights, NT)
            if r == 0:
                keep[lo : lo + half, :] = part
            else:
                keep[lo : lo + half, :] += part
    send[:, :units] = keep[:, units:]
    send[:, units:] = keep[:, :units]


def middle_body(
    at, pre, pre_recv, back, back_recv, gate, up, gate_other, up_other, d, weighted, sums, opp_a, opp_b
):
    rows = pre.shape[0]
    both = pre.shape[1] // 2
    half = rows // 2
    block = opp_a.shape[1]
    weights = pre_weights(at, gate, up, gate_other, up_other, 2, block)
    ones = jnp.ones((8, both), F32)
    for lo, out in ((0, opp_a), (half, opp_b)):
        span = slice(lo, lo + half)
        pre_all = pre[span, :] + pre_recv[span, :]
        back_all = back[span, :] + back_recv[span, :]
        pre_gate = pre_all[:, :both]
        pre_up = pre_all[:, both:]
        sig = jax.nn.sigmoid(pre_gate)
        silu = pre_gate * sig
        act = silu * pre_up
        sums[:, span] = lax.dot_general(
            ones, act * back_all, NT, preferred_element_type=F32, precision=lax.Precision.HIGHEST
        )
        weighted[span, :] = act.astype(BF)
        d_gate = (back_all * pre_up * (sig * (1.0 + pre_gate * (1.0 - sig)))).astype(BF)
        d_up = (back_all * silu).astype(BF)
        grads = jnp.concatenate([d_gate, d_up], axis=1)
        d[span, :] = grads
        out[...] = mm(grads, weights, NT).astype(BF)


def rows_body(at, d, gate, up, gate_other, up_other, to_right, to_left, right_later, left_later, own):
    rows = d.shape[0]
    half = rows // 2
    block = own.shape[1]
    weights = pre_weights(at, gate, up, gate_other, up_other, 1, block)
    to_right[...] = mm(d[half:, :], weights, NT).astype(BF)
    right_later[...] = mm(d[:half, :], weights, NT)
    weights = pre_weights(at, gate, up, gate_other, up_other, 3, block)
    to_left[...] = mm(d[:half, :], weights, NT).astype(BF)
    left_later[...] = mm(d[half:, :], weights, NT)
    weights = pre_weights(at, gate, up, gate_other, up_other, 0, block)
    own[:half, :] = mm(d[:half, :], weights, NT)
    own[half:, :] = mm(d[half:, :], weights, NT)


def grads_body(own, right, left, opp_a, opp_b, d, gate_own, gate_other, up_own, up_other):
    half = own.shape[0] // 2
    units = d.shape[1] // 4
    for r in range(CHIPS):
        total = None
        for lo in (0, half):
            rows = blocks_of(own, right, left, opp_a, opp_b, lo, lo + half, half)[r]
            part = mm(rows, d[lo : lo + half, :], TN)
            total = part if total is None else total + part
        for i, out in enumerate((gate_own, gate_other, up_own, up_other)):
            out[r] = total[:, i * units : (i + 1) * units].astype(BF)


def down_body(own, right, left, opp_a, opp_b, weighted, down_own, down_other):
    half = own.shape[0] // 2
    units = weighted.shape[1] // 2
    for r in range(CHIPS):
        total = None
        for lo in (0, half):
            rows = blocks_of(own, right, left, opp_a, opp_b, lo, lo + half, half)[r]
            part = mm(weighted[lo : lo + half, :], rows, TN)
            total = part if total is None else total + part
        down_own[r] = total[:units, :].astype(BF)
        down_other[r] = total[units:, :].astype(BF)


def place_body(at, *refs):
    pairs = len(refs) // 3
    mine = lax.rem(pl.program_id(0), 2) == at[1]
    for own, other, target in zip(refs[:pairs], refs[pairs : 2 * pairs], refs[2 * pairs :]):

        @pl.when(mine)
        def _():
            target[...] = own[0]

        @pl.when(jnp.logical_not(mine))
        def _():
            target[...] = other[0]


def place(at, gate_own, up_own, down_own, gate_other, up_other, down_other):
    _, block, units = gate_own.shape
    depth = 2 * CHIPS * block
    where = lambda b, at: ((b // 2 + CHIPS - at[0]) % CHIPS, 0, 0)
    source = pl.BlockSpec((1, block, units), where)
    source_wide = pl.BlockSpec((1, units, block), where)
    return call(
        place_body,
        (shape((depth, units), BF), shape((depth, units), BF), shape((units, depth), BF)),
        moved=18 * depth * units,
        grid_spec=pltpu.PrefetchScalarGridSpec(
            num_scalar_prefetch=1,
            grid=(2 * CHIPS,),
            in_specs=[source, source, source_wide] * 2,
            out_specs=[
                pl.BlockSpec((block, units), lambda b, at: (b, 0)),
                pl.BlockSpec((block, units), lambda b, at: (b, 0)),
                pl.BlockSpec((units, block), lambda b, at: (0, b)),
            ],
        ),
    )(at, gate_own, up_own, down_own, gate_other, up_other, down_other)


def finish_body(experts, routes, gates, back, grad):
    pick, _ = select_rows(routes[...], gates[...], back.shape[0], experts)
    grad[...] = mm(pick.astype(BF), back[...], TN).astype(BF)


def gating_body(experts, routes, gates, sums, grad):
    count, topk = routes.shape
    rows = experts * CAP
    pick, _ = select_rows(routes[...], gates[...], rows, experts)
    row = lax.broadcasted_iota(jnp.int32, (rows, experts), 0) // CAP
    owner = (row == lax.broadcasted_iota(jnp.int32, (rows, experts), 1)).astype(F32)
    cap_of = (
        lax.broadcasted_iota(jnp.int32, (rows, CAP), 0) % CAP == lax.broadcasted_iota(jnp.int32, (rows, CAP), 1)
    ).astype(F32)
    spread = lax.dot_general(owner, sums[...], NN, preferred_element_type=F32, precision=lax.Precision.HIGHEST)
    value = jnp.sum(spread * cap_of, axis=1, keepdims=True)
    table = lax.dot_general(
        pick * value, owner, TN, preferred_element_type=F32, precision=lax.Precision.HIGHEST
    )
    lane = lax.broadcasted_iota(jnp.int32, (count, experts), 1)
    for k in range(topk):
        hit = routes[:, k : k + 1] == lane
        picked = jnp.sum(jnp.where(hit, table, 0.0), axis=1, keepdims=True)
        grad[:, k : k + 1] = picked / gates[:, k : k + 1].astype(F32)


def to(value, shift):
    size = 2 * CHIPS
    return lax.ppermute(value, "hidden", [(i, (i + 2 * shift) % size) for i in range(size)])


def swap(value):
    return lax.ppermute(value, "hidden", [(i, i ^ 1) for i in range(2 * CHIPS)])


def ring_gather(own):
    half = own.shape[0] // 2
    left = to(own, 1)
    right = to(own, -1)
    opp_a = to(left[:half], 1)
    opp_b = to(right[half:], -1)
    return own, right, left, opp_a, opp_b


def local(tokens, grad_out, routes, gating, w_gate, w_up, w_down):
    experts = lax.axis_size("expert")
    hidden = lax.axis_index("hidden")
    at = jnp.stack([hidden // 2, hidden % 2]).astype(jnp.int32)
    rows = experts * CAP
    half = rows // 2
    count, width = tokens.shape
    topk = routes.shape[1]
    block = width // (2 * CHIPS)
    gate, up, down = w_gate[0], w_up[0], w_down[0]
    units = gate.shape[1]
    both = 2 * units

    def over_experts(value):
        split = value.reshape(experts, value.shape[0] // experts, value.shape[1])
        return lax.all_to_all(split, "expert", split_axis=0, concat_axis=0, tiled=True).reshape(value.shape)

    send_x, send_dy = prepare(at, routes, gating, tokens, grad_out, experts)
    x = ring_gather(over_experts(send_x))
    dy = ring_gather(over_experts(send_dy))
    gate_other, up_other, down_other = [swap(v) for v in halves(at, gate, up, down)]
    weights = (gate, up, gate_other, up_other)

    work = 4 * rows * block * CHIPS * both
    pre, pre_send = call(
        pre_body,
        (shape((rows, 2 * both), F32), shape((rows, 2 * both), F32)),
        flops=work,
        moved=8 * rows * block,
        in_specs=[SM] + [VM] * 9,
        out_specs=(VM, VM),
    )(at, *x, *weights)
    pre_recv = swap(pre_send)
    back, back_send = call(
        back_body,
        (shape((rows, both), F32), shape((rows, both), F32)),
        flops=work // 2,
        moved=8 * rows * block,
        in_specs=[SM] + [VM] * 7,
        out_specs=(VM, VM),
    )(at, *dy, down, down_other)
    back_recv = swap(back_send)

    d, weighted, sums, opp_a, opp_b = call(
        middle_body,
        (
            shape((rows, 2 * both), BF),
            shape((rows, both), BF),
            shape((8, rows), F32),
            shape((half, block), BF),
            shape((half, block), BF),
        ),
        flops=work // 4,
        moved=8 * rows * block,
        in_specs=[SM] + [VM] * 8,
        out_specs=(VM,) * 5,
    )(at, pre, pre_recv, back, back_recv, *weights)
    from_left = to(opp_a, 1)
    from_right = to(opp_b, -1)
    to_right, to_left, right_later, left_later, own = call(
        rows_body,
        (
            shape((half, block), BF),
            shape((half, block), BF),
            shape((half, block), F32),
            shape((half, block), F32),
            shape((rows, block), F32),
        ),
        flops=3 * work // 4,
        moved=12 * rows * block,
        in_specs=[SM] + [VM] * 5,
        out_specs=(VM,) * 5,
    )(at, d, *weights)
    left_b = to(to_right, 1)
    right_a = to(to_left, -1)
    left_a = to((right_later + from_left.astype(F32)).astype(BF), 1)
    right_b = to((left_later + from_right.astype(F32)).astype(BF), -1)
    total_a = own[:half] + left_a.astype(F32) + right_a.astype(F32)
    total_b = own[half:] + left_b.astype(F32) + right_b.astype(F32)
    returned = over_experts(jnp.concatenate([total_a, total_b]).astype(BF))

    grad_gate, gate_send, grad_up, up_send = call(
        grads_body,
        (shape((CHIPS, block, units), BF),) * 4,
        flops=work,
        moved=8 * rows * block,
        in_specs=[VM] * 6,
        out_specs=(VM,) * 4,
    )(*x, d)
    grad_down, down_send = call(
        down_body,
        (shape((CHIPS, units, block), BF),) * 2,
        flops=work // 2,
        moved=8 * rows * block,
        in_specs=[VM] * 6,
        out_specs=(VM,) * 2,
    )(*dy, weighted)
    grads = place(
        at, grad_gate, grad_up, grad_down, swap(gate_send), swap(up_send), swap(down_send)
    )

    slots = lax.all_to_all(
        sums[0].reshape(experts, 1, CAP), "expert", split_axis=0, concat_axis=0, tiled=True
    ).reshape(experts, CAP)
    slots = slots + to(slots, 1)
    slots = slots + to(slots, 2)
    grad_gating = call(
        functools.partial(gating_body, experts),
        shape((count, topk), F32),
        in_specs=[VM] * 3,
        out_specs=VM,
    )(routes, gating, slots)
    grad_tokens = call(
        functools.partial(finish_body, experts),
        shape((count, block), BF),
        in_specs=[VM] * 3,
        out_specs=VM,
    )(routes, gating, returned)
    return (grad_tokens, grad_gating, grads[0][None], grads[1][None], grads[2][None])


def solution(mesh):
    placed = (
        P("expert", None),
        P("expert", None),
        P("expert", None),
        P("expert", None),
        P("expert", None, "hidden"),
        P("expert", None, "hidden"),
        P("expert", "hidden", None),
    )
    return jax.shard_map(
        local,
        mesh=mesh,
        in_specs=placed,
        out_specs=(
            P("expert", "hidden"),
            P("expert", None),
            P("expert", None, "hidden"),
            P("expert", None, "hidden"),
            P("expert", "hidden", None),
        ),
        check_vma=False,
    )
```

time: 683 us -> 200 us (0.29)
  waiting for transfers between devices: 309 us -> 49.8 us
  local copies, waits for them, and re-layouts: 215 us -> 17.5 us
  matrix products: 53.7 us -> 0 us
  Pallas kernels: 0 us -> 30.5 us
  between operations: 14.5 us -> 1.01 us
  blocking collectives: 22.7 us -> 35.3 us
    all_to_all x5 -> x3, waiting for transfers between devices: 290 us -> 20.1 us  [the longest x2 20.1 us: over_experts(): lax.all_to_all(split, 'expert', split_axis=0, concat_axis=0, tiled=True)]
    unnamed x15 -> x61, local copies, waits for them, and re-layouts: 165 us -> 14.6 us
    dot_general x8 -> x0, matrix products: 53.7 us -> none  [the longest x1 10.4 us: local(): lax.dot_general(d_up, wup, (((1,), (1,)), ((), ())), preferred_element_ty...]
    ppermute x0 -> x24, starting transfers between devices: none -> 43.9 us  [the longest x8 25.5 us: swap(): return lax.ppermute(value, 'hidden', [(i, i ^ 1) for i in range(2 * CHIPS)])]
    scatter x3 -> x0, local copies, waits for them, and re-layouts: 42.1 us -> none  [the longest x1 20.1 us: build_sends(): jnp.zeros((slot_rows, x_src.shape[1]), jnp.bfloat16).at[target]]
    all_to_all x5 -> x3, starting transfers between devices: 56.5 us -> 15.5 us  [the longest x2 10.5 us: over_experts(): lax.all_to_all(split, 'expert', split_axis=0, concat_axis=0, tiled=True)]
    all_to_all x0 -> x1, blocking collectives: none -> 35.3 us  [over_experts(): lax.all_to_all(split, 'expert', split_axis=0, concat_axis=0, tiled=True)]
    pallas_call x0 -> x11, Pallas kernels: none -> 30.5 us  [the longest x1 8.03 us: place(): call(place_body, (shape((depth, units), BF), shape((depth, units), BF), s...]
  transfers between devices with their start and end apart: 6 -> 27, of which waited for: 4 -> 7; matrix products, arithmetic and copies ran while one was open for 14% -> 4% of each run, Pallas kernels for 0% -> 13%
where the time goes in v1:
time: 200 us; the launch traced here: 198 us
  starting transfers between devices  59.4 us (30%)
  waiting for transfers between devices  49.8 us (25%)
  blocking collectives  35.3 us (18%)
  Pallas kernels  30.5 us (15%)
  local copies, waits for them, and re-layouts  17.5 us (9%)
  other arithmetic  4.68 us (2%)
    all_to_all x1, blocking collectives, over_experts(): lax.all_to_all(split, 'expert', split_axis=0, concat_axis=0, tiled=True)  35.3 us
    ppermute x16, waiting for transfers between devices, to(): lax.ppermute(value, 'hidden', [(i, (i + 2 * shift) % size) for i in range...  28.2 us
    ppermute x8, starting transfers between devices, swap(): return lax.ppermute(value, 'hidden', [(i, i ^ 1) for i in range(2 * CHIPS)])  25.5 us
    all_to_all x2, waiting for transfers between devices, over_experts(): lax.all_to_all(split, 'expert', split_axis=0, concat_axis=0, tiled=True)  20.1 us
    ppermute x16, starting transfers between devices, to(): lax.ppermute(value, 'hidden', [(i, (i + 2 * shift) % size) for i in range...  18.3 us
    unnamed x61, local copies, waits for them, and re-layouts  14.6 us
    all_to_all x2, starting transfers between devices, over_experts(): lax.all_to_all(split, 'expert', split_axis=0, concat_axis=0, tiled=True)  10.5 us
    pallas_call x1, Pallas kernels, place(): call(place_body, (shape((depth, units), BF), shape((depth, units), BF), s...  8.03 us
  transfers between devices with their start and end apart: 27, of which 7 were waited for; matrix products, arithmetic and copies ran while one was open for 4% of the time, Pallas kernels for 13%

profile of v1, /device:TPU:17, one launch (start us, length us, event | category | flops | bytes accessed | tf_op | source)
XLA Modules:
  0.0 198.2 jit_solution(9942450460624818254)
XLA Ops:
  5.8 35.3 %all_to_all.20 = bf16[32,16,896]{2,1,0:T(8,128)(2,1)} all-to-all(bf16[32,16,896]{2,1,0:T(8,128)(2,1)S(1)} %bitcast.36), channel_id=1, replica_groups=mesh['expert'=32,'hidden'=8] {'expert'}, dimensions={0} | all-to-all | bytes 1835008 | tf_op jit(solution)/shard_map/all_to_all | solution.py:350
  41.1 5.5 %all-to-all-start.1 = ((bf16[32,16,896]{2,1,0:T(8,128)(2,1)}), bf16[32,16,896]{2,1,0:T(8,128)(2,1)S(1)}, u32[]{:S(2)}, u32[]{:S(2)}) async-start(bf16[32,16,896]{2,1,0:T(8,128)(2,1)} %bitcast.35), calls=%async_computation.1 | async-start | bytes 1835008 | tf_op jit(solution)/shard_map/all_to_all | solution.py:350
  49.4 20.1 %all-to-all-done.1 = bf16[32,16,896]{2,1,0:T(8,128)(2,1)S(1)} async-done(((bf16[32,16,896]{2,1,0:T(8,128)(2,1)}), bf16[32,16,896]{2,1,0:T(8,128)(2,1)S(1)}, u32[]{:S(2)}, u32[]{:S(2)}) %all-to-all-start.1) | async-done | bytes 917536 | tf_op jit(solution)/shard_map/all_to_all | solution.py:350
  76.1 4.3 %collective-permute-start.4 = (bf16[4,896,128]{2,1,0:T(8,128)(2,1)S(1)}, bf16[4,896,128]{2,1,0:T(8,128)(2,1)S(1)}, u32[]{:S(2)}, u32[]{:S(2)}) collective-permute-start(bf16[4,896,128]{2,1,0:T(8,128)(2,1)S(1)} %get-tuple-element.34), channel_id=1, source_target_pairs={{0,1},{1,0},{2,3},{3,2},{4,5},{5,4},{6,7},{7,6},{8,9},{9,8},{10,11... | collective-permute-start | bytes 2752520 | tf_op jit(solution)/shard_map/ppermute | solution.py:323
  82.9 6.0 %collective-permute-done.8.left = bf16[512,896]{1,0:T(8,128)(2,1)S(1)} collective-permute-done((bf16[512,896]{1,0:T(8,128)(2,1)S(1)}, bf16[512,896]{1,0:T(8,128)(2,1)S(1)}, u32[]{:S(2)}, u32[]{:S(2)}) %collective-permute-start.8) | collective-permute-done | bytes 917536 | tf_op jit(solution)/shard_map/ppermute | solution.py:319
  90.1 9.1 %collective-permute-start.11 = (bf16[4,128,896]{2,1,0:T(8,128)(2,1)S(1)}, bf16[4,128,896]{2,1,0:T(8,128)(2,1)S(1)}, u32[]{:S(2)}, u32[]{:S(2)}) collective-permute-start(bf16[4,128,896]{2,1,0:T(8,128)(2,1)S(1)} %get-tuple-element.39), channel_id=1, source_target_pairs={{0,1},{1,0},{2,3},{3,2},{4,5},{5,4},{6,7},{7,6},{8,9},{9,8},{10,11... | collective-permute-start | bytes 2752520 | tf_op jit(solution)/shard_map/ppermute | solution.py:323
  99.6 2.5 %collective-permute-start.10 = (bf16[256,896]{1,0:T(8,128)(2,1)S(1)}, bf16[256,896]{1,0:T(8,128)(2,1)S(1)}, u32[]{:S(2)}, u32[]{:S(2)}) collective-permute-start(bf16[256,896]{1,0:T(8,128)(2,1)S(1)} %slice.31), channel_id=1, source_target_pairs={{0,6},{1,7},{2,0},{3,1},{4,2},{5,3},{6,4},{7,5},{8,14},{9,15},{10,... | collective-permute-start | bytes 1376264 | tf_op jit(solution)/shard_map/ppermute | solution.py:319
  102.1 4.1 %shard_map.112 = (f32[512,512]{1,0:T(8,128)S(1)}, f32[512,512]{1,0:T(8,128)S(1)}) custom-call(s32[2]{0:T(128)S(1)} %pad_add_fusion.at, bf16[512,896]{1,0:T(8,128)(2,1)S(1)} %bitcast.32, bf16[512,896]{1,0:T(8,128)(2,1)} %collective-permute-done.right, bf16[512,896]{1,0:T(8,128)(2,1)} %collective-permute-done.1.left, ...), custom_call_target="tpu_custom_call" | custom-call | flops 1879048192 | bytes 3670016 | tf_op jit(solution)/shard_map/pallas_call | solution.py:359
  106.3 7.5 %collective-permute-start.6 = (f32[512,512]{1,0:T(8,128)S(1)}, f32[512,512]{1,0:T(8,128)S(1)}, u32[]{:S(2)}, u32[]{:S(2)}) collective-permute-start(f32[512,512]{1,0:T(8,128)S(1)} %get-tuple-element.37), channel_id=1, source_target_pairs={{0,1},{1,0},{2,3},{3,2},{4,5},{5,4},{6,7},{7,6},{8,9},{9,8},{10,11... | collective-permute-start | bytes 3145736 | tf_op jit(solution)/shard_map/ppermute | solution.py:323
  113.8 1.8 shard_map.113
  115.7 2.2 %collective-permute-start.12 = (f32[512,256]{1,0:T(8,128)S(1)}, f32[512,256]{1,0:T(8,128)S(1)}, u32[]{:S(2)}, u32[]{:S(2)}) collective-permute-start(f32[512,256]{1,0:T(8,128)S(1)} %get-tuple-element.41), channel_id=1, source_target_pairs={{0,1},{1,0},{2,3},{3,2},{4,5},{5,4},{6,7},{7,6},{8,9},{9,8},{10,11... | collective-permute-start | bytes 1572872 | tf_op jit(solution)/shard_map/ppermute | solution.py:323
  119.4 1.8 shard_map.114
  121.4 2.7 %collective-permute-start.17 = (bf16[256,896]{1,0:T(8,128)(2,1)S(1)}, bf16[256,896]{1,0:T(8,128)(2,1)S(1)}, u32[]{:S(2)}, u32[]{:S(2)}) collective-permute-start(bf16[256,896]{1,0:T(8,128)(2,1)S(1)} %get-tuple-element.49), channel_id=1, source_target_pairs={{0,6},{1,7},{2,0},{3,1},{4,2},{5,3},{6,4},{7,5},{8,14},{9,15},{10,... | collective-permute-start | bytes 1376264 | tf_op jit(solution)/shard_map/ppermute | solution.py:319
  124.0 2.6 %shard_map.115 = (bf16[256,896]{1,0:T(8,128)(2,1)}, bf16[256,896]{1,0:T(8,128)(2,1)}, f32[256,896]{1,0:T(8,128)S(1)}, f32[256,896]{1,0:T(8,128)S(1)}, f32[512,896]{1,0:T(8,128)S(1)}) custom-call(s32[2]{0:T(128)S(1)} %pad_add_fusion.at, bf16[512,512]{1,0:T(8,128)(2,1)S(1)} %get-tuple-element.42.d, bf16[7168,128]{1,0:T(8,128)(2,1)S(1)} %bitcast.19, ...), custom_call_target="tpu_custom_call" | custom-call | flops 1409286144 | bytes 5505024 | tf_op jit(solution)/shard_map/pallas_call | solution.py:394
  128.1 6.2 %collective-permute-done.13 = bf16[256,896]{1,0:T(8,128)(2,1)S(1)} collective-permute-done((bf16[256,896]{1,0:T(8,128)(2,1)S(1)}, bf16[256,896]{1,0:T(8,128)(2,1)S(1)}, u32[]{:S(2)}, u32[]{:S(2)}) %collective-permute-start.13) | collective-permute-done | bytes 458784 | tf_op jit(solution)/shard_map/ppermute | solution.py:319
  136.1 2.7 %collective-permute-start.18 = (bf16[256,896]{1,0:T(8,128)(2,1)}, bf16[256,896]{1,0:T(8,128)(2,1)S(1)}, u32[]{:S(2)}, u32[]{:S(2)}) collective-permute-start(bf16[256,896]{1,0:T(8,128)(2,1)} %add_convert_fusion.1), channel_id=1, source_target_pairs={{0,6},{1,7},{2,0},{3,1},{4,2},{5,3},{6,4},{7,5},{8,14},{9,15},{10,... | collective-permute-start | bytes 1376264 | tf_op jit(solution)/shard_map/ppermute | solution.py:319
  139.5 5.0 %all-to-all-start.3 = ((f32[32,1,16]{2,1,0:T(1,128)}), f32[32,1,16]{2,1,0:T(1,128)S(1)}, u32[]{:S(2)}, u32[]{:S(2)}) async-start(f32[32,1,16]{2,1,0:T(1,128)} %bitcast.11), calls=%async_computation.3 | async-start | bytes 32768 | tf_op jit(solution)/shard_map/all_to_all | solution.py:436
  144.5 9.5 %collective-permute-done.14 = bf16[256,896]{1,0:T(8,128)(2,1)S(1)} collective-permute-done((bf16[256,896]{1,0:T(8,128)(2,1)}, bf16[256,896]{1,0:T(8,128)(2,1)S(1)}, u32[]{:S(2)}, u32[]{:S(2)}) %collective-permute-start.14) | collective-permute-done | bytes 458784 | tf_op jit(solution)/shard_map/ppermute | solution.py:319
  156.8 5.0 %all-to-all-start.2 = ((bf16[32,16,896]{2,1,0:T(8,128)(2,1)}), bf16[32,16,896]{2,1,0:T(8,128)(2,1)S(1)}, u32[]{:S(2)}, u32[]{:S(2)}) async-start(bf16[32,16,896]{2,1,0:T(8,128)(2,1)} %bitcast.37), calls=%async_computation.2 | async-start | bytes 1835008 | tf_op jit(solution)/shard_map/all_to_all | solution.py:350
  165.0 4.9 %shard_map.118 = (bf16[4,896,128]{2,1,0:T(8,128)(2,1)S(1)}, bf16[4,896,128]{2,1,0:T(8,128)(2,1)}, bf16[4,896,128]{2,1,0:T(8,128)(2,1)S(1)}, bf16[4,896,128]{2,1,0:T(8,128)(2,1)}) custom-call(bf16[512,896]{1,0:T(8,128)(2,1)S(1)} %bitcast.33, bf16[512,896]{1,0:T(8,128)(2,1)} %collective-permute-done.right, bf16[512,896]{1,0:T(8,128)(2,1)} %collective-permute-done.1.left, ...), custom_call_target="tpu_custom_call" | custom-call | flops 1879048192 | bytes 3670016 | tf_op jit(solution)/shard_map/pallas_call | solution.py:416
  172.6 2.2 %shard_map.119 = (bf16[4,128,896]{2,1,0:T(8,128)(2,1)S(1)}, bf16[4,128,896]{2,1,0:T(8,128)(2,1)}) custom-call(bf16[512,896]{1,0:T(8,128)(2,1)S(1)} %bitcast.27, bf16[512,896]{1,0:T(8,128)(2,1)S(1)} %copy-done.8, bf16[512,896]{1,0:T(8,128)(2,1)S(1)} %copy-done.6, bf16[256,896]{1,0:T(8,128)(2,1)S(1)} %collective-permute-done.9.opp_a, ...), custom_call_target="tpu_custom_call" | custom-call | flops 939524096 | bytes 3670016 | tf_op jit(solution)/shard_map/pallas_call | solution.py:424
  176.9 3.4 %collective-permute-done.19 = f32[32,16]{1,0:T(8,128)S(1)} collective-permute-done((f32[32,16]{1,0:T(8,128)S(1)}, f32[32,16]{1,0:T(8,128)S(1)}, u32[]{:S(2)}, u32[]{:S(2)}) %collective-permute-start.19) | collective-permute-done | bytes 2080 | tf_op jit(solution)/shard_map/ppermute | solution.py:319
  181.6 3.1 %collective-permute-done.20 = f32[32,16]{1,0:T(8,128)S(1)} collective-permute-done((f32[32,16]{1,0:T(8,128)S(1)}, f32[32,16]{1,0:T(8,128)S(1)}, u32[]{:S(2)}, u32[]{:S(2)}) %collective-permute-start.20) | collective-permute-done | bytes 2080 | tf_op jit(solution)/shard_map/ppermute | solution.py:319
  188.9 8.0 %shard_map.120 = (bf16[7168,128]{1,0:T(8,128)(2,1)}, bf16[7168,128]{1,0:T(8,128)(2,1)}, bf16[128,7168]{1,0:T(8,128)(2,1)}) custom-call(s32[2]{0:T(128)S(1)} %pad_add_fusion.at, bf16[4,896,128]{2,1,0:T(8,128)(2,1)S(1)} %copy-done.16, bf16[4,896,128]{2,1,0:T(8,128)(2,1)S(1)} %copy-done.18, bf16[4,128,896]{2,1,0:T(8,128)(2,1)S(1)} %copy-done.20, ...), custom_call_target="tpu_custom_call" | custom-call | bytes 16515072 | tf_op jit(solution)/shard_map/pallas_call | solution.py:274
  (116 shorter events, 41.6 us)
Async XLA Ops:
  41.1 28.3 %all-to-all-start.1 = ((bf16[32,16,896]{2,1,0:T(8,128)(2,1)}), bf16[32,16,896]{2,1,0:T(8,128)(2,1)S(1)}, u32[]{:S(2)}, u32[]{:S(2)}) async-start(bf16[32,16,896]{2,1,0:T(8,128)(2,1)} %bitcast.35), calls=%async_computation.1 | async-start | bytes 1835008 | tf_op jit(solution)/shard_map/all_to_all | solution.py:350
  46.6 33.8 %collective-permute-start.1 = (bf16[512,896]{1,0:T(8,128)(2,1)}, bf16[512,896]{1,0:T(8,128)(2,1)}, u32[]{:S(2)}, u32[]{:S(2)}) collective-permute-start(bf16[512,896]{1,0:T(8,128)(2,1)} %bitcast.30), channel_id=1, source_target_pairs={{0,2},{1,3},{2,4},{3,5},{4,6},{5,7},{6,0},{7,1},{8,10},{9,11},{10,... | collective-permute-start | bytes 2752520 | tf_op jit(solution)/shard_map/ppermute | solution.py:319
  47.9 33.8 %collective-permute-start = (bf16[512,896]{1,0:T(8,128)(2,1)}, bf16[512,896]{1,0:T(8,128)(2,1)}, u32[]{:S(2)}, u32[]{:S(2)}) collective-permute-start(bf16[512,896]{1,0:T(8,128)(2,1)} %bitcast.31), channel_id=1, source_target_pairs={{0,6},{1,7},{2,0},{3,1},{4,2},{5,3},{6,4},{7,5},{8,14},{9,15},{10,... | collective-permute-start | bytes 2752520 | tf_op jit(solution)/shard_map/ppermute | solution.py:319
  69.4 19.4 %collective-permute-start.8 = (bf16[512,896]{1,0:T(8,128)(2,1)S(1)}, bf16[512,896]{1,0:T(8,128)(2,1)S(1)}, u32[]{:S(2)}, u32[]{:S(2)}) collective-permute-start(bf16[512,896]{1,0:T(8,128)(2,1)S(1)} %bitcast.24), channel_id=1, source_target_pairs={{0,2},{1,3},{2,4},{3,5},{4,6},{5,7},{6,0},{7,1},{8,10},{9,11},{10,... | collective-permute-start | bytes 2752520 | tf_op jit(solution)/shard_map/ppermute | solution.py:319
  70.7 19.4 %collective-permute-start.7 = (bf16[512,896]{1,0:T(8,128)(2,1)S(1)}, bf16[512,896]{1,0:T(8,128)(2,1)S(1)}, u32[]{:S(2)}, u32[]{:S(2)}) collective-permute-start(bf16[512,896]{1,0:T(8,128)(2,1)S(1)} %bitcast.25), channel_id=1, source_target_pairs={{0,6},{1,7},{2,0},{3,1},{4,2},{5,3},{6,4},{7,5},{8,14},{9,15},{10,... | collective-permute-start | bytes 2752520 | tf_op jit(solution)/shard_map/ppermute | solution.py:319
  76.1 23.1 %collective-permute-start.4 = (bf16[4,896,128]{2,1,0:T(8,128)(2,1)S(1)}, bf16[4,896,128]{2,1,0:T(8,128)(2,1)S(1)}, u32[]{:S(2)}, u32[]{:S(2)}) collective-permute-start(bf16[4,896,128]{2,1,0:T(8,128)(2,1)S(1)} %get-tuple-element.34), channel_id=1, source_target_pairs={{0,1},{1,0},{2,3},{3,2},{4,5},{5,4},{6,7},{7,6},{8,9},{9,8},{10,11... | collective-permute-start | bytes 2752520 | tf_op jit(solution)/shard_map/ppermute | solution.py:323
  80.5 19.1 %collective-permute-start.5 = (bf16[4,896,128]{2,1,0:T(8,128)(2,1)S(1)}, bf16[4,896,128]{2,1,0:T(8,128)(2,1)S(1)}, u32[]{:S(2)}, u32[]{:S(2)}) collective-permute-start(bf16[4,896,128]{2,1,0:T(8,128)(2,1)S(1)} %get-tuple-element.35), channel_id=1, source_target_pairs={{0,1},{1,0},{2,3},{3,2},{4,5},{5,4},{6,7},{7,6},{8,9},{9,8},{10,11... | collective-permute-start | bytes 2752520 | tf_op jit(solution)/shard_map/ppermute | solution.py:323
  81.7 20.3 %collective-permute-start.2 = (bf16[256,896]{1,0:T(8,128)(2,1)S(1)}, bf16[256,896]{1,0:T(8,128)(2,1)S(1)}, u32[]{:S(2)}, u32[]{:S(2)}) collective-permute-start(bf16[256,896]{1,0:T(8,128)(2,1)S(1)} %slice.28), channel_id=1, source_target_pairs={{0,2},{1,3},{2,4},{3,5},{4,6},{5,7},{6,0},{7,1},{8,10},{9,11},{10,... | collective-permute-start | bytes 1376264 | tf_op jit(solution)/shard_map/ppermute | solution.py:319
  88.8 13.2 %collective-permute-start.3 = (bf16[256,896]{1,0:T(8,128)(2,1)S(1)}, bf16[256,896]{1,0:T(8,128)(2,1)S(1)}, u32[]{:S(2)}, u32[]{:S(2)}) collective-permute-start(bf16[256,896]{1,0:T(8,128)(2,1)S(1)} %slice.29), channel_id=1, source_target_pairs={{0,6},{1,7},{2,0},{3,1},{4,2},{5,3},{6,4},{7,5},{8,14},{9,15},{10,... | collective-permute-start | bytes 1376264 | tf_op jit(solution)/shard_map/ppermute | solution.py:319
  90.1 23.7 %collective-permute-start.11 = (bf16[4,128,896]{2,1,0:T(8,128)(2,1)S(1)}, bf16[4,128,896]{2,1,0:T(8,128)(2,1)S(1)}, u32[]{:S(2)}, u32[]{:S(2)}) collective-permute-start(bf16[4,128,896]{2,1,0:T(8,128)(2,1)S(1)} %get-tuple-element.39), channel_id=1, source_target_pairs={{0,1},{1,0},{2,3},{3,2},{4,5},{5,4},{6,7},{7,6},{8,9},{9,8},{10,11... | collective-permute-start | bytes 2752520 | tf_op jit(solution)/shard_map/ppermute | solution.py:323
  99.3 14.5 %collective-permute-start.9 = (bf16[256,896]{1,0:T(8,128)(2,1)S(1)}, bf16[256,896]{1,0:T(8,128)(2,1)S(1)}, u32[]{:S(2)}, u32[]{:S(2)}) collective-permute-start(bf16[256,896]{1,0:T(8,128)(2,1)S(1)} %slice.30), channel_id=1, source_target_pairs={{0,2},{1,3},{2,4},{3,5},{4,6},{5,7},{6,0},{7,1},{8,10},{9,11},{10,... | collective-permute-start | bytes 1376264 | tf_op jit(solution)/shard_map/ppermute | solution.py:319
  99.6 14.2 %collective-permute-start.10 = (bf16[256,896]{1,0:T(8,128)(2,1)S(1)}, bf16[256,896]{1,0:T(8,128)(2,1)S(1)}, u32[]{:S(2)}, u32[]{:S(2)}) collective-permute-start(bf16[256,896]{1,0:T(8,128)(2,1)S(1)} %slice.31), channel_id=1, source_target_pairs={{0,6},{1,7},{2,0},{3,1},{4,2},{5,3},{6,4},{7,5},{8,14},{9,15},{10,... | collective-permute-start | bytes 1376264 | tf_op jit(solution)/shard_map/ppermute | solution.py:319
  106.3 13.2 %collective-permute-start.6 = (f32[512,512]{1,0:T(8,128)S(1)}, f32[512,512]{1,0:T(8,128)S(1)}, u32[]{:S(2)}, u32[]{:S(2)}) collective-permute-start(f32[512,512]{1,0:T(8,128)S(1)} %get-tuple-element.37), channel_id=1, source_target_pairs={{0,1},{1,0},{2,3},{3,2},{4,5},{5,4},{6,7},{7,6},{8,9},{9,8},{10,11... | collective-permute-start | bytes 3145736 | tf_op jit(solution)/shard_map/ppermute | solution.py:323
  121.3 13.0 %collective-permute-start.13 = (bf16[256,896]{1,0:T(8,128)(2,1)S(1)}, bf16[256,896]{1,0:T(8,128)(2,1)S(1)}, u32[]{:S(2)}, u32[]{:S(2)}) collective-permute-start(bf16[256,896]{1,0:T(8,128)(2,1)S(1)} %get-tuple-element.45), channel_id=1, source_target_pairs={{0,2},{1,3},{2,4},{3,5},{4,6},{5,7},{6,0},{7,1},{8,10},{9,11},{10,... | collective-permute-start | bytes 1376264 | tf_op jit(solution)/shard_map/ppermute | solution.py:319
  121.4 13.8 %collective-permute-start.17 = (bf16[256,896]{1,0:T(8,128)(2,1)S(1)}, bf16[256,896]{1,0:T(8,128)(2,1)S(1)}, u32[]{:S(2)}, u32[]{:S(2)}) collective-permute-start(bf16[256,896]{1,0:T(8,128)(2,1)S(1)} %get-tuple-element.49), channel_id=1, source_target_pairs={{0,6},{1,7},{2,0},{3,1},{4,2},{5,3},{6,4},{7,5},{8,14},{9,15},{10,... | collective-permute-start | bytes 1376264 | tf_op jit(solution)/shard_map/ppermute | solution.py:319
  126.7 17.8 %collective-permute-start.15 = (bf16[256,896]{1,0:T(8,128)(2,1)}, bf16[256,896]{1,0:T(8,128)(2,1)S(1)}, u32[]{:S(2)}, u32[]{:S(2)}) collective-permute-start(bf16[256,896]{1,0:T(8,128)(2,1)} %get-tuple-element.46), channel_id=1, source_target_pairs={{0,6},{1,7},{2,0},{3,1},{4,2},{5,3},{6,4},{7,5},{8,14},{9,15},{10,... | collective-permute-start | bytes 1376264 | tf_op jit(solution)/shard_map/ppermute | solution.py:319
  127.9 16.5 %collective-permute-start.16 = (bf16[256,896]{1,0:T(8,128)(2,1)}, bf16[256,896]{1,0:T(8,128)(2,1)S(1)}, u32[]{:S(2)}, u32[]{:S(2)}) collective-permute-start(bf16[256,896]{1,0:T(8,128)(2,1)} %get-tuple-element.47), channel_id=1, source_target_pairs={{0,2},{1,3},{2,4},{3,5},{4,6},{5,7},{6,0},{7,1},{8,10},{9,11},{10,... | collective-permute-start | bytes 1376264 | tf_op jit(solution)/shard_map/ppermute | solution.py:319
  135.2 18.8 %collective-permute-start.14 = (bf16[256,896]{1,0:T(8,128)(2,1)}, bf16[256,896]{1,0:T(8,128)(2,1)S(1)}, u32[]{:S(2)}, u32[]{:S(2)}) collective-permute-start(bf16[256,896]{1,0:T(8,128)(2,1)} %add_convert_fusion.3), channel_id=1, source_target_pairs={{0,2},{1,3},{2,4},{3,5},{4,6},{5,7},{6,0},{7,1},{8,10},{9,11},{10,... | collective-permute-start | bytes 1376264 | tf_op jit(solution)/shard_map/ppermute | solution.py:319
  136.1 17.9 %collective-permute-start.18 = (bf16[256,896]{1,0:T(8,128)(2,1)}, bf16[256,896]{1,0:T(8,128)(2,1)S(1)}, u32[]{:S(2)}, u32[]{:S(2)}) collective-permute-start(bf16[256,896]{1,0:T(8,128)(2,1)} %add_convert_fusion.1), channel_id=1, source_target_pairs={{0,6},{1,7},{2,0},{3,1},{4,2},{5,3},{6,4},{7,5},{8,14},{9,15},{10,... | collective-permute-start | bytes 1376264 | tf_op jit(solution)/shard_map/ppermute | solution.py:319
  139.5 17.4 %all-to-all-start.3 = ((f32[32,1,16]{2,1,0:T(1,128)}), f32[32,1,16]{2,1,0:T(1,128)S(1)}, u32[]{:S(2)}, u32[]{:S(2)}) async-start(f32[32,1,16]{2,1,0:T(1,128)} %bitcast.11), calls=%async_computation.3 | async-start | bytes 32768 | tf_op jit(solution)/shard_map/all_to_all | solution.py:436
  156.8 40.0 %all-to-all-start.2 = ((bf16[32,16,896]{2,1,0:T(8,128)(2,1)}), bf16[32,16,896]{2,1,0:T(8,128)(2,1)S(1)}, u32[]{:S(2)}, u32[]{:S(2)}) async-start(bf16[32,16,896]{2,1,0:T(8,128)(2,1)} %bitcast.37), calls=%async_computation.2 | async-start | bytes 1835008 | tf_op jit(solution)/shard_map/all_to_all | solution.py:350
  170.8 15.7 %collective-permute-start.21 = (bf16[4,896,128]{2,1,0:T(8,128)(2,1)}, bf16[4,896,128]{2,1,0:T(8,128)(2,1)}, u32[]{:S(2)}, u32[]{:S(2)}) collective-permute-start(bf16[4,896,128]{2,1,0:T(8,128)(2,1)} %get-tuple-element.55), channel_id=1, source_target_pairs={{0,1},{1,0},{2,3},{3,2},{4,5},{5,4},{6,7},{7,6},{8,9},{9,8},{10,11... | collective-permute-start | bytes 2752520 | tf_op jit(solution)/shard_map/ppermute | solution.py:323
  172.6 13.9 %collective-permute-start.22 = (bf16[4,896,128]{2,1,0:T(8,128)(2,1)}, bf16[4,896,128]{2,1,0:T(8,128)(2,1)}, u32[]{:S(2)}, u32[]{:S(2)}) collective-permute-start(bf16[4,896,128]{2,1,0:T(8,128)(2,1)} %get-tuple-element.56), channel_id=1, source_target_pairs={{0,1},{1,0},{2,3},{3,2},{4,5},{5,4},{6,7},{7,6},{8,9},{9,8},{10,11... | collective-permute-start | bytes 2752520 | tf_op jit(solution)/shard_map/ppermute | solution.py:323
  175.8 10.7 %collective-permute-start.23 = (bf16[4,128,896]{2,1,0:T(8,128)(2,1)}, bf16[4,128,896]{2,1,0:T(8,128)(2,1)}, u32[]{:S(2)}, u32[]{:S(2)}) collective-permute-start(bf16[4,128,896]{2,1,0:T(8,128)(2,1)} %get-tuple-element.57), channel_id=1, source_target_pairs={{0,1},{1,0},{2,3},{3,2},{4,5},{5,4},{6,7},{7,6},{8,9},{9,8},{10,11... | collective-permute-start | bytes 2752520 | tf_op jit(solution)/shard_map/ppermute | solution.py:323
  (32 other events, 296.1 us)

commit v2 on v0

v2 whole, which is shorter than its diff:
```python
import functools

import jax
import jax.numpy as jnp
from jax import lax
from jax.experimental import pallas as pl
from jax.experimental.pallas import tpu as pltpu
from jax.sharding import PartitionSpec as P

CAP = 16
CHIPS = 4
BF = jnp.bfloat16
F32 = jnp.float32
VMEM_LIMIT = 16 * 1024 * 1024


NN = (((1,), (0,)), ((), ()))
NT = (((1,), (1,)), ((), ()))
TN = (((0,), (0,)), ((), ()))


def mm(a, b, dims):
    return lax.dot_general(a, b, dims, preferred_element_type=F32)


def call(body, out_shape, operands, after=(), token=False, scratch=(), places=None, outs=None):
    count = len(operands)
    out_shape = tuple(out_shape)
    results = len(out_shape)
    ins = places or [SM] + [VM] * (count - 1)
    outs = outs or (VM,) * results

    moved = sum(v.size * v.dtype.itemsize for v in tuple(operands[1:]) + out_shape)

    def run(*refs):
        given, made = refs[:count], refs[count + len(after) :]
        if token:
            made[results][...] = jnp.zeros((8, 128), F32)
            made = made[:results] + made[results + 1 :]
        body(*given, *made)

    return pl.pallas_call(
        run,
        out_shape=out_shape + ((shape((8, 128), F32),) if token else ()),
        in_specs=list(ins) + [ANY] * len(after),
        out_specs=tuple(outs) + ((VM,) if token else ()),
        scratch_shapes=list(scratch),
        compiler_params=pltpu.CompilerParams(vmem_limit_bytes=VMEM_LIMIT),
        cost_estimate=pl.CostEstimate(flops=0, bytes_accessed=moved, transcendentals=0),
    )(*operands, *after)


def shape(dims, dtype):
    return jax.ShapeDtypeStruct(dims, dtype)


VM = pl.BlockSpec(memory_space=pltpu.VMEM)
SM = pl.BlockSpec(memory_space=pltpu.SMEM)
ANY = pl.BlockSpec(memory_space=pl.ANY)
HBM = pl.BlockSpec(memory_space=pltpu.HBM)


CUTS = (7, 14)


def plan(block):
    pieces = ([], [])
    start = 0
    for message, cut in enumerate(CUTS):
        end = 2 * block * cut // 14
        for kind in (0, 1):
            lo, hi = max(start, kind * block), min(end, (kind + 1) * block)
            if lo < hi:
                pieces[kind].append((message, lo - start, lo - kind * block, hi - lo))
        start = end
    return pieces


def widths(block):
    ends = [0] + [2 * block * cut // 14 for cut in CUTS]
    return [hi - lo for lo, hi in zip(ends, ends[1:])]


def owner_of(rows, experts):
    row = lax.broadcasted_iota(jnp.int32, (rows, experts), 0) // CAP
    return (row == lax.broadcasted_iota(jnp.int32, (rows, experts), 1)).astype(F32)


def slot_is(rows, count):
    row = lax.broadcasted_iota(jnp.int32, (rows, count), 0) % CAP
    return row == lax.broadcasted_iota(jnp.int32, (rows, count), 1)


def select_rows(routes, gates, rows, experts):
    topk, count = routes.shape
    expert = lax.broadcasted_iota(jnp.int32, (experts, count), 0)
    named = jnp.zeros((experts, count), F32)
    weight = jnp.zeros((experts, count), F32)
    for k in range(topk):
        hit = routes[k : k + 1, :] == expert
        named = jnp.where(hit, 1.0, named)
        weight = jnp.where(hit, gates[k : k + 1, :].astype(F32), weight)
    earlier = (
        lax.broadcasted_iota(jnp.int32, (count, count), 0) < lax.broadcasted_iota(jnp.int32, (count, count), 1)
    ).astype(F32)
    slot = mm(named.astype(BF), earlier.astype(BF), NN)
    slot = jnp.where(named > 0, slot, 2.0 * CAP)
    owner = owner_of(rows, experts).astype(BF)
    slot_of = mm(owner, slot.astype(BF), NN)
    weight_of = mm(owner, weight.astype(BF), NN)
    place = (lax.broadcasted_iota(jnp.int32, (rows, count), 0) % CAP).astype(F32)
    pick = jnp.where(slot_of == place, 1.0, 0.0)
    return pick, pick * weight_of


def first_body(experts, at, routes, gates, x, out, pick_out, weigh_out):
    pick, weighted = select_rows(routes[...], gates[...], pick_out.shape[0], experts)
    pick = pick.astype(BF)
    pick_out[...] = pick
    weigh_out[...] = weighted.astype(BF)
    out[...] = mm(pick, x[:, : out.shape[1]], NN).astype(BF)


def rest_body(at, pick, weighted, x, dy, *outs):
    for chosen, source, pieces in zip((pick, weighted), (x, dy), plan(x.shape[1])):
        for message, column, feature, many in pieces:
            if message > 0:
                value = mm(chosen[...], source[:, feature : feature + many], NN)
                outs[message - 1][:, column : column + many] = value.astype(BF)


def halves_body(at, gate, up, down, out):
    units, block = down.shape
    out[0, 0] = gate[...]
    out[0, 1] = up[...]
    for j in range(0, block, units):
        out[0, 2, j : j + units, :] = down[:, j : j + units]


def halves(at, w_gate, w_up, w_down):
    depth, units = w_gate.shape
    block = depth // (2 * CHIPS)
    other = lambda r, at: 2 * ((at[0] + r) % CHIPS) + 1 - at[1]
    tall = pl.BlockSpec((block, units), lambda r, at: (other(r, at), 0))
    wide = pl.BlockSpec((units, block), lambda r, at: (0, other(r, at)))
    return pl.pallas_call(
        halves_body,
        out_shape=shape((CHIPS, 3, block, units), BF),
        compiler_params=pltpu.CompilerParams(vmem_limit_bytes=VMEM_LIMIT),
        cost_estimate=pl.CostEstimate(flops=0, bytes_accessed=12 * depth * units, transcendentals=0),
        grid_spec=pltpu.PrefetchScalarGridSpec(
            num_scalar_prefetch=1,
            grid=(CHIPS,),
            in_specs=[tall, tall, wide],
            out_specs=pl.BlockSpec((1, 3, block, units), lambda r, at: (r, 0, 0, 0)),
        ),
    )(at, w_gate, w_up, w_down)


def block_at(at, r):
    return 2 * lax.rem(at[0] + r, CHIPS) + at[1]


def pre_weights(at, gate, up, others, r, lo, hi):
    block = others.shape[2]
    mine = pl.ds(pl.multiple_of(block_at(at, r) * block + lo, 128), hi - lo)
    return jnp.concatenate([gate[mine, :], others[r, 0, lo:hi, :], up[mine, :], others[r, 1, lo:hi, :]], axis=1)


def down_weights(at, down, others, r, lo, hi):
    units = down.shape[0]
    block = others.shape[2]
    mine = pl.ds(pl.multiple_of(block_at(at, r) * block + lo, 128), hi - lo)
    other = [others[r, 2, j : j + units, :] for j in range(lo, hi, units)]
    return jnp.concatenate([down[:, mine], jnp.concatenate(other, axis=1)], axis=0)


def halves_of(parts, r, half, columns):
    if r == 2:
        return ((0, parts[3][:, columns]), (half, parts[4][:, columns]))
    ref = parts[{0: 0, 1: 1, 3: 2}[r]]
    return ((0, ref[:half, columns]), (half, ref[half:, columns]))


def send_swapped(keep, send, units):
    for i in range(keep.shape[1] // units):
        j = i ^ 1
        send[:, i * units : (i + 1) * units] = keep[:, j * units : (j + 1) * units]


def add_body(piece, which, first, last, pre, at, *refs):
    _, column, feature, many = piece
    columns = slice(column, column + many)
    weights, refs = (refs[:3], refs[3:]) if pre else (refs[:2], refs[2:])
    given = 3 * (which[0] == 0) + 2 * (2 in which)
    parts, refs = refs[:given], refs[given:]
    parts = [None] * (5 - given) + list(parts) if which[0] == 2 else parts
    before, refs = (None, refs) if first else (refs[0], refs[1:])
    keep = refs[0]
    half = keep.shape[0] // 2
    for r in which:
        cut = (feature, feature + many)
        block = pre_weights(at, *weights, r, *cut) if pre else down_weights(at, *weights, r, *cut)
        for lo, part in halves_of(parts, r, half, columns):
            value = mm(part, block, NN if pre else NT)
            if r == which[0]:
                keep[lo : lo + half, :] = value if first else before[lo : lo + half, :] + value
            else:
                keep[lo : lo + half, :] += value
    if last:
        send_swapped(keep, refs[1], weights[0].shape[1 if pre else 0])


def middle_body(at, pre, pre_recv, back, back_recv, gate, up, others, d, act_rows, sums, opp_a, opp_b):
    rows = pre.shape[0]
    both = pre.shape[1] // 2
    half = rows // 2
    experts = rows // CAP
    owner = owner_of(rows, experts)
    slot = slot_is(rows, CAP)
    weights = pre_weights(at, gate, up, others, 2, 0, opp_a.shape[1])
    total = None
    for lo, out in ((0, opp_a), (half, opp_b)):
        span = slice(lo, lo + half)
        pre_all = pre[span, :] + pre_recv[span, :]
        back_all = back[span, :] + back_recv[span, :]
        pre_gate = pre_all[:, :both]
        pre_up = pre_all[:, both:]
        sig = jax.nn.sigmoid(pre_gate)
        silu = pre_gate * sig
        act = silu * pre_up
        act_rows[span, :] = act.astype(BF)
        d_gate = (back_all * pre_up * (sig * (1.0 + pre_gate * (1.0 - sig)))).astype(BF)
        d_up = (back_all * silu).astype(BF)
        grads = jnp.concatenate([d_gate, d_up], axis=1)
        d[span, :] = grads
        out[...] = mm(grads, weights, NT).astype(BF)
        value = jnp.sum(act * back_all, axis=1, keepdims=True)
        part = lax.dot_general(
            owner[span, :],
            jnp.where(slot[span, :], value, 0.0),
            TN,
            preferred_element_type=F32,
            precision=lax.Precision.HIGHEST,
        )
        total = part if total is None else total + part
    sums[...] = total


def rows_body(at, d, gate, up, others, to_right, to_left, right_later, left_later, own):
    half = d.shape[0] // 2
    block = own.shape[1]
    weights = pre_weights(at, gate, up, others, 1, 0, block)
    to_right[...] = mm(d[half:, :], weights, NT).astype(BF)
    right_later[...] = mm(d[:half, :], weights, NT)
    weights = pre_weights(at, gate, up, others, 3, 0, block)
    to_left[...] = mm(d[:half, :], weights, NT).astype(BF)
    left_later[...] = mm(d[half:, :], weights, NT)
    weights = pre_weights(at, gate, up, others, 0, 0, block)
    own[:half, :] = mm(d[:half, :], weights, NT)
    own[half:, :] = mm(d[half:, :], weights, NT)


def later_body(at, right_later, left_later, from_left, from_right, to_right, to_left):
    to_right[...] = (right_later[...] + from_left[...].astype(F32)).astype(BF)
    to_left[...] = (left_later[...] + from_right[...].astype(F32)).astype(BF)


def total_body(at, own, left_a, left_b, right_a, right_b, out):
    half = own.shape[0] // 2
    for span, left, right in ((slice(0, half), left_a, right_a), (slice(half, 2 * half), left_b, right_b)):
        out[span, :] = (own[span, :] + left[...].astype(F32) + right[...].astype(F32)).astype(BF)


def grads_body(at, d, act_rows, *refs):
    keep, send = refs[-2:]
    messages = [refs[i : i + 5] for i in range(0, len(refs) - 2, 5)]
    block = keep.shape[2]
    units = keep.shape[3]
    half = d.shape[0] // 2
    tokens, cotangents = plan(block)
    for r in range(CHIPS):
        for message, column, feature, many in tokens:
            total = None
            for lo, part in halves_of(messages[message], r, half, slice(column, column + many)):
                value = mm(part, d[lo : lo + half, :], TN)
                total = value if total is None else total + value
            for i, (out, kind) in enumerate(((keep, 0), (send, 0), (keep, 1), (send, 1))):
                out[r, kind, feature : feature + many, :] = total[:, i * units : (i + 1) * units].astype(BF)
        for message, column, feature, many in cotangents:
            total = None
            for lo, part in halves_of(messages[message], r, half, slice(column, column + many)):
                value = mm(act_rows[lo : lo + half, :], part, TN)
                total = value if total is None else total + value
            total = total.astype(BF)
            for j in range(0, many, units):
                keep[r, 2, feature + j : feature + j + units, :] = total[:units, j : j + units]
                send[r, 2, feature + j : feature + j + units, :] = total[units:, j : j + units]


def place_body(at, keep, recv, gate, up, down, sems):
    block, units = keep.shape[2:]
    copies = []

    def add(source, target):
        copies.append(pltpu.make_async_copy(source, target, sems.at[len(copies)]))
        copies[-1].start()

    for r in range(CHIPS):
        for held, core in ((keep, at[1]), (recv, 1 - at[1])):
            start = pl.multiple_of((2 * lax.rem(at[0] + r, CHIPS) + core) * block, 128)
            add(held.at[r, 0], gate.at[pl.ds(start, block), :])
            add(held.at[r, 1], up.at[pl.ds(start, block), :])
            for j in range(0, block, units):
                add(held.at[r, 2, pl.ds(j, units)], down.at[:, pl.ds(pl.multiple_of(start + j, 128), units)])
    for copy in copies:
        copy.wait()


def finish_body(at, pick, back, grad):
    grad[...] = mm(pick[...], back[...], TN).astype(BF)


def gating_body(at, pick, routes, gates, sums, others, grad):
    topk, count = routes.shape
    rows = pick.shape[0]
    experts = rows // CAP
    owner = owner_of(rows, experts)
    spread = lax.dot_general(
        owner, sums[...] + others[...], NN, preferred_element_type=F32, precision=lax.Precision.HIGHEST
    )
    value = jnp.sum(jnp.where(slot_is(rows, CAP), spread, 0.0), axis=1, keepdims=True)
    table = lax.dot_general(
        owner, pick[...].astype(F32) * value, TN, preferred_element_type=F32, precision=lax.Precision.HIGHEST
    )
    expert = lax.broadcasted_iota(jnp.int32, (experts, count), 0)
    for k in range(topk):
        hit = routes[k : k + 1, :] == expert
        picked = jnp.sum(jnp.where(hit, table, 0.0), axis=0, keepdims=True)
        grad[k : k + 1, :] = picked / gates[k : k + 1, :].astype(F32)


def to(value, shift):
    size = 2 * CHIPS
    return lax.ppermute(value, "hidden", [(i, (i + 2 * shift) % size) for i in range(size)])


def swap(value):
    return lax.ppermute(value, "hidden", [(i, i ^ 1) for i in range(2 * CHIPS)])


def split_body(at, left, right, out_a, out_b):
    half = left.shape[0] // 2
    out_a[...] = left[:half, :]
    out_b[...] = right[half:, :]


def ring_gather(at, own, after):
    half = own.shape[0] // 2
    left = to(own, 1)
    right = to(own, -1)
    pass_a, pass_b, token = call(
        split_body,
        (shape((half, own.shape[1]), BF),) * 2,
        (at, left, right),
        after=after,
        token=True,
    )
    return (own, right, left, to(pass_a, 1), to(pass_b, -1)), (token,)


def behind(value, token):
    return pl.pallas_call(
        lambda *refs: None,
        out_shape=shape(value.shape, value.dtype),
        in_specs=[ANY, ANY],
        out_specs=ANY,
        input_output_aliases={0: 0},
        compiler_params=pltpu.CompilerParams(vmem_limit_bytes=VMEM_LIMIT // 4),
    )(value, token)


def local(tokens, grad_out, routes, gating, w_gate, w_up, w_down):
    experts = lax.axis_size("expert")
    hidden = lax.axis_index("hidden")
    at = jnp.stack([lax.shift_right_logical(hidden, 1), lax.bitwise_and(hidden, 1)]).astype(jnp.int32)
    rows = experts * CAP
    half = rows // 2
    count, width = tokens.shape
    topk = routes.shape[1]
    block = width // (2 * CHIPS)
    gate, up, down = w_gate[0], w_up[0], w_down[0]
    units = gate.shape[1]
    both = 2 * units
    routes, gates = routes.T, gating.T
    of_tokens, of_cotangents = plan(block)

    def over_experts(value):
        split = value.reshape(experts, value.shape[0] // experts, value.shape[1])
        return lax.all_to_all(split, "expert", split_axis=0, concat_axis=0, tiled=True).reshape(value.shape)

    def my_block(value):
        return lax.dynamic_slice(value, (0, hidden * block), (count, block))

    my_tokens = my_block(tokens)
    message, pick, weighted = call(
        functools.partial(first_body, experts),
        (shape((rows, widths(block)[0]), BF),) + (shape((rows, count), BF),) * 2,
        (at, routes, gates, my_tokens),
    )
    arrived = [over_experts(message)]
    messages = call(
        rest_body,
        tuple(shape((rows, many), BF) for many in widths(block)[1:]),
        (at, pick, weighted, my_tokens, my_block(grad_out)),
    )
    arrived += [over_experts(message) for message in messages]
    gathered = []
    token = ()
    for value in arrived:
        parts, token = ring_gather(at, value, token)
        gathered.append(parts)
    others = swap(halves(at, gate, up, down))
    weights = (gate, up, others)

    pre = ()
    for i, piece in enumerate(of_tokens):
        pre = call(
            functools.partial(add_body, piece, (0, 1, 3, 2), i == 0, i == len(of_tokens) - 1, True),
            (shape((rows, 2 * both), F32),) * (1 + (i == len(of_tokens) - 1)),
            (at, *weights, *gathered[piece[0]], *pre),
        )
    pre, pre_send = pre
    pre_recv = swap(pre_send)
    narrow = (shape((rows, both), F32),)
    back = ()
    turns = [(piece, (0, 1, 3, 2)) for piece in of_cotangents[:-1]]
    for piece, which in turns + [(of_cotangents[-1], (0, 1, 3)), (of_cotangents[-1], (2,))]:
        last = which == (2,)
        parts = gathered[piece[0]]
        parts = parts[3:] if last else parts[: 5 if 2 in which else 3]
        back = call(
            functools.partial(add_body, piece, which, not back, last, False),
            narrow * (1 + last),
            (at, down, others, *parts, *back),
        )
    back, back_send = back
    back_recv = swap(back_send)

    part = (shape((half, block), BF),)
    later = (shape((half, block), F32),)
    d, act_rows, sums, opp_a, opp_b = call(
        middle_body,
        (shape((rows, 2 * both), BF), shape((rows, both), BF), shape((experts, CAP), F32)) + part * 2,
        (at, pre, pre_recv, back, back_recv, *weights),
    )
    from_left, from_right = to(opp_a, 1), to(opp_b, -1)
    to_right, to_left, right_later, left_later, own, *token = call(
        rows_body,
        part * 2 + later * 2 + (shape((rows, block), F32),),
        (at, d, *weights),
        token=True,
    )
    left_b, right_a = to(to_right, 1), to(to_left, -1)
    keep, send, *token = call(
        grads_body,
        (shape((CHIPS, 3, block, units), BF),) * 2,
        (at, d, act_rows, *[part for parts in gathered for part in parts]),
        after=token,
        token=True,
    )
    to_right, to_left = call(later_body, part * 2, (at, right_later, left_later, from_left, from_right), after=token)
    left_a, right_b = to(to_right, 1), to(to_left, -1)
    slots = over_experts(sums)
    total, *token = call(
        total_body,
        (shape((rows, block), BF),),
        (at, own, left_a, left_b, right_a, right_b),
        after=(slots,),
        token=True,
    )
    returned = over_experts(total)
    *grads, placed = call(
        place_body,
        (shape((2 * CHIPS * block, units), BF),) * 2 + (shape((units, 2 * CHIPS * block), BF),),
        (at, keep, swap(behind(send, token[0]))),
        token=True,
        scratch=[pltpu.SemaphoreType.DMA((2 * CHIPS * (2 + block // units),))],
        places=[SM] + [ANY] * 2,
        outs=(HBM,) * 3,
    )

    slots = slots + to(slots, 1)
    grad_gating, gated = call(
        gating_body,
        (shape((topk, count), F32),),
        (at, pick, routes, gates, slots, to(slots, 2)),
        token=True,
    )
    (grad_tokens,) = call(
        finish_body,
        (shape((count, block), BF),),
        (at, pick, returned),
        after=(placed, gated),
    )
    return (grad_tokens, grad_gating.T, grads[0][None], grads[1][None], grads[2][None])


def solution(mesh):
    placed = (
        P("expert", None),
        P("expert", None),
        P("expert", None),
        P("expert", None),
        P("expert", None, "hidden"),
        P("expert", None, "hidden"),
        P("expert", "hidden", None),
    )
    return jax.shard_map(
        local,
        mesh=mesh,
        in_specs=placed,
        out_specs=(
            P("expert", "hidden"),
            P("expert", None),
            P("expert", None, "hidden"),
            P("expert", None, "hidden"),
            P("expert", "hidden", None),
        ),
        check_vma=False,
    )
```

time: 683 us -> 276 us (0.40)
  waiting for transfers between devices: 309 us -> 76 us
  local copies, waits for them, and re-layouts: 215 us -> 11.1 us
  Pallas kernels: 0 us -> 118 us
  matrix products: 53.7 us -> 0 us
  between operations: 14.5 us -> 0.88 us
  blocking collectives: 22.7 us -> 15.1 us
    all_to_all x5 -> x3, waiting for transfers between devices: 290 us -> 35.6 us  [over_experts(): lax.all_to_all(split, 'expert', split_axis=0, concat_axis=0, tiled=True)]
    unnamed x15 -> x28, local copies, waits for them, and re-layouts: 165 us -> 10.1 us
    pallas_call x0 -> x17, Pallas kernels: none -> 118 us  [the longest x15 115 us: call(): pl.pallas_call(run, out_shape=out_shape + ((shape((8, 128), F32),) if tok...]
    dot_general x8 -> x0, matrix products: 53.7 us -> none  [the longest x1 10.4 us: local(): lax.dot_general(d_up, wup, (((1,), (1,)), ((), ())), preferred_element_ty...]
    scatter x3 -> x0, local copies, waits for them, and re-layouts: 42.1 us -> none  [the longest x1 20.1 us: build_sends(): jnp.zeros((slot_rows, x_src.shape[1]), jnp.bfloat16).at[target]]
    ppermute x0 -> x20, waiting for transfers between devices: none -> 40.4 us  [the longest x16 38.9 us: to(): lax.ppermute(value, 'hidden', [(i, (i + 2 * shift) % size) for i in range...]
    all_to_all x5 -> x3, starting transfers between devices: 56.5 us -> 22.2 us  [over_experts(): lax.all_to_all(split, 'expert', split_axis=0, concat_axis=0, tiled=True)]
    ppermute x0 -> x20, starting transfers between devices: none -> 29.7 us  [the longest x16 19.3 us: to(): lax.ppermute(value, 'hidden', [(i, (i + 2 * shift) % size) for i in range...]
  transfers between devices with their start and end apart: 6 -> 23, of which waited for: 4 -> 7; matrix products, arithmetic and copies ran while one was open for 14% -> 0% of each run, Pallas kernels for 0% -> 41%
where the time goes in v2:
time: 276 us; the launch traced here: 273 us
  Pallas kernels  118 us (43%)
  waiting for transfers between devices  76 us (28%)
  starting transfers between devices  51.9 us (19%)
  blocking collectives  15.1 us (5%)
  local copies, waits for them, and re-layouts  11.1 us (4%)
    pallas_call x15, Pallas kernels, call(): pl.pallas_call(run, out_shape=out_shape + ((shape((8, 128), F32),) if tok...  115 us
    ppermute x16, waiting for transfers between devices, to(): lax.ppermute(value, 'hidden', [(i, (i + 2 * shift) % size) for i in range...  38.9 us
    all_to_all x3, waiting for transfers between devices, over_experts(): lax.all_to_all(split, 'expert', split_axis=0, concat_axis=0, tiled=True)  35.6 us
    all_to_all x3, starting transfers between devices, over_experts(): lax.all_to_all(split, 'expert', split_axis=0, concat_axis=0, tiled=True)  22.2 us
    ppermute x16, starting transfers between devices, to(): lax.ppermute(value, 'hidden', [(i, (i + 2 * shift) % size) for i in range...  19.3 us
    all_to_all x1, blocking collectives, over_experts(): lax.all_to_all(split, 'expert', split_axis=0, concat_axis=0, tiled=True)  15.1 us
    ppermute x4, starting transfers between devices, swap(): return lax.ppermute(value, 'hidden', [(i, i ^ 1) for i in range(2 * CHIPS)])  10.4 us
    unnamed x28, local copies, waits for them, and re-layouts  10.1 us
  transfers between devices with their start and end apart: 23, of which 7 were waited for; matrix products, arithmetic and copies ran while one was open for 0% of the time, Pallas kernels for 41%

profile of v2, /device:TPU:17, one launch (start us, length us, event | category | flops | bytes accessed | tf_op | source)
XLA Modules:
  0.0 273.2 jit_solution(2688706246301008593)
XLA Ops:
  3.1 2.1 shard_map.110
  5.2 11.1 %all-to-all-start = ((bf16[32,16,896]{2,1,0:T(8,128)(2,1)}), bf16[32,16,896]{2,1,0:T(8,128)(2,1)}, u32[]{:S(2)}, u32[]{:S(2)}) async-start(bf16[32,16,896]{2,1,0:T(8,128)(2,1)} %bitcast.7), calls=%async_computation | async-start | bytes 1835008 | tf_op jit(solution)/shard_map/all_to_all | solution.py:400
  19.3 2.8 %shard_map.111 = bf16[4,3,896,128]{3,2,1,0:T(8,128)(2,1)} custom-call(s32[2]{0:T(128)S(1)} %pad_add_fusion.refs_0_.at, bf16[7168,128]{1,0:T(8,128)(2,1)S(1)} %bitcast.21, bf16[7168,128]{1,0:T(8,128)(2,1)S(1)} %bitcast.25, bf16[128,7168]{1,0:T(8,128)(2,1)S(1)} %bitcast.29), custom_call_target="tpu_custom_call" | custom-call | bytes 11010048 | tf_op jit(solution)/shard_map/pallas_call | solution.py:146
  25.2 15.3 %all-to-all-done = bf16[32,16,896]{2,1,0:T(8,128)(2,1)} async-done(((bf16[32,16,896]{2,1,0:T(8,128)(2,1)}), bf16[32,16,896]{2,1,0:T(8,128)(2,1)}, u32[]{:S(2)}, u32[]{:S(2)}) %all-to-all-start) | async-done | bytes 917536 | tf_op jit(solution)/shard_map/all_to_all | solution.py:400
  40.4 5.6 %all-to-all-start.1 = ((bf16[32,16,896]{2,1,0:T(8,128)(2,1)}), bf16[32,16,896]{2,1,0:T(8,128)(2,1)}, u32[]{:S(2)}, u32[]{:S(2)}) async-start(bf16[32,16,896]{2,1,0:T(8,128)(2,1)} %bitcast.32), calls=%async_computation.1 | async-start | bytes 1835008 | tf_op jit(solution)/shard_map/all_to_all | solution.py:400
  46.0 2.6 collective-permute-start.1
  48.6 20.3 %all-to-all-done.1 = bf16[32,16,896]{2,1,0:T(8,128)(2,1)} async-done(((bf16[32,16,896]{2,1,0:T(8,128)(2,1)}), bf16[32,16,896]{2,1,0:T(8,128)(2,1)}, u32[]{:S(2)}, u32[]{:S(2)}) %all-to-all-start.1) | async-done | bytes 917536 | tf_op jit(solution)/shard_map/all_to_all | solution.py:400
  73.2 2.7 collective-permute-start.4
  75.9 22.4 %collective-permute-done.3.refs_7_.refs_6_ = bf16[256,896]{1,0:T(8,128)(2,1)S(1)} collective-permute-done((bf16[256,896]{1,0:T(8,128)(2,1)S(1)}, bf16[256,896]{1,0:T(8,128)(2,1)S(1)}, u32[]{:S(2)}, u32[]{:S(2)}) %collective-permute-start.3) | collective-permute-done | bytes 458784 | tf_op jit(solution)/shard_map/ppermute | solution.py:345
  99.8 4.1 %shard_map.113 = (f32[512,512]{1,0:T(8,128)S(1)}, f32[512,512]{1,0:T(8,128)S(1)}) custom-call(s32[2]{0:T(128)S(1)} %pad_add_fusion.refs_0_.at, bf16[7168,128]{1,0:T(8,128)(2,1)S(1)} %bitcast.22, bf16[7168,128]{1,0:T(8,128)(2,1)S(1)} %bitcast.26, bf16[4,3,896,128]{3,2,1,0:T(8,128)(2,1)S(1)} %collective-permute-done.refs_3_.refs_2_.refs_7_.refs_4_, ...), custom_call_target="tpu_custom_call" | custom-call | bytes 12189696 | tf_op jit(solution)/shard_map/pallas_call | solution.py:42
  103.9 4.7 %collective-permute-start.5 = (f32[512,512]{1,0:T(8,128)S(1)}, f32[512,512]{1,0:T(8,128)S(1)}, u32[]{:S(2)}, u32[]{:S(2)}) collective-permute-start(f32[512,512]{1,0:T(8,128)S(1)} %get-tuple-element.46), channel_id=1, source_target_pairs={{0,1},{1,0},{2,3},{3,2},{4,5},{5,4},{6,7},{7,6},{8,9},{9,8},{10,11... | collective-permute-start | bytes 3145736 | tf_op jit(solution)/shard_map/ppermute | solution.py:349
  112.4 2.2 shard_map.116.refs_5_
  114.6 8.4 %collective-permute-done.8.refs_3_.refs_11_ = bf16[256,896]{1,0:T(8,128)(2,1)S(1)} collective-permute-done((bf16[256,896]{1,0:T(8,128)(2,1)S(1)}, bf16[256,896]{1,0:T(8,128)(2,1)S(1)}, u32[]{:S(2)}, u32[]{:S(2)}) %collective-permute-start.8) | collective-permute-done | bytes 458784 | tf_op jit(solution)/shard_map/ppermute | solution.py:345
  131.1 2.4 shard_map.119
  133.6 2.7 collective-permute-start.15
  136.3 6.8 %shard_map.120 = (bf16[4,3,896,128]{3,2,1,0:T(8,128)(2,1)S(1)}, bf16[4,3,896,128]{3,2,1,0:T(8,128)(2,1)}, f32[8,128]{1,0:T(8,128)S(1)}) custom-call(s32[2]{0:T(128)S(1)} %pad_add_fusion.refs_0_.at, bf16[512,512]{1,0:T(8,128)(2,1)S(1)} %get-tuple-element.53.refs_1_, bf16[512,256]{1,0:T(8,128)(2,1)S(1)} %get-tuple-element.59.refs_2_, ...), custom_call_target="tpu_custom_call" | custom-call | bytes 13631488 | tf_op jit(solution)/shard_map/pallas_call | solution.py:42
  145.4 2.7 collective-permute-start.16
  148.1 15.1 %all_to_all.20 = f32[32,1,16]{2,1,0:T(1,128)S(1)} all-to-all(f32[32,1,16]{2,1,0:T(1,128)S(1)} %bitcast.39), channel_id=1, replica_groups=mesh['expert'=32,'hidden'=8] {'expert'}, dimensions={0} | all-to-all | bytes 4096 | tf_op jit(solution)/shard_map/all_to_all | solution.py:400
  165.0 3.4 %collective-permute-start.17 = (bf16[4,3,896,128]{3,2,1,0:T(8,128)(2,1)}, bf16[4,3,896,128]{3,2,1,0:T(8,128)(2,1)}, u32[]{:S(2)}, u32[]{:S(2)}) collective-permute-start(bf16[4,3,896,128]{3,2,1,0:T(8,128)(2,1)} %shard_map.123), channel_id=1, source_target_pairs={{0,1},{1,0},{2,3},{3,2},{4,5},{5,4},{6,7},{7,6},{8,9},{9,8},{10,11... | collective-permute-start | bytes 8257544 | tf_op jit(solution)/shard_map/ppermute | solution.py:349
  168.4 5.6 %all-to-all-start.3 = ((bf16[32,16,896]{2,1,0:T(8,128)(2,1)}), bf16[32,16,896]{2,1,0:T(8,128)(2,1)S(1)}, u32[]{:S(2)}, u32[]{:S(2)}) async-start(bf16[32,16,896]{2,1,0:T(8,128)(2,1)} %bitcast.14), calls=%async_computation.3 | async-start | bytes 1835008 | tf_op jit(solution)/shard_map/all_to_all | solution.py:400
  174.1 3.8 %collective-permute-done.18 = f32[32,16]{1,0:T(8,128)S(1)} collective-permute-done((f32[32,16]{1,0:T(8,128)S(1)}, f32[32,16]{1,0:T(8,128)S(1)}, u32[]{:S(2)}, u32[]{:S(2)}) %collective-permute-start.18) | collective-permute-done | bytes 2080 | tf_op jit(solution)/shard_map/ppermute | solution.py:345
  178.1 4.2 %collective-permute-done.19.refs_5_ = f32[32,16]{1,0:T(8,128)S(1)} collective-permute-done((f32[32,16]{1,0:T(8,128)S(1)}, f32[32,16]{1,0:T(8,128)S(1)}, u32[]{:S(2)}, u32[]{:S(2)}) %collective-permute-start.19) | collective-permute-done | bytes 2080 | tf_op jit(solution)/shard_map/ppermute | solution.py:345
  182.3 2.0 shard_map.125
  186.1 85.7 %shard_map.124 = (bf16[7168,128]{1,0:T(8,128)(2,1)}, bf16[7168,128]{1,0:T(8,128)(2,1)}, bf16[128,7168]{1,0:T(8,128)(2,1)}, f32[8,128]{1,0:T(8,128)S(1)}) custom-call(s32[2]{0:T(128)S(1)} %pad_add_fusion.refs_0_.at, bf16[4,3,896,128]{3,2,1,0:T(8,128)(2,1)S(1)} %copy-done.9, bf16[4,3,896,128]{3,2,1,0:T(8,128)(2,1)} %collective-permute-done.17.refs_2_), custom_call_target="tpu_custom_call" | custom-call | bytes 11010048 | tf_op jit(solution)/shard_map/pallas_call | solution.py:42
  (71 shorter events, 33.9 us)
Async XLA Ops:
  5.2 35.2 %all-to-all-start = ((bf16[32,16,896]{2,1,0:T(8,128)(2,1)}), bf16[32,16,896]{2,1,0:T(8,128)(2,1)}, u32[]{:S(2)}, u32[]{:S(2)}) async-start(bf16[32,16,896]{2,1,0:T(8,128)(2,1)} %bitcast.7), calls=%async_computation | async-start | bytes 1835008 | tf_op jit(solution)/shard_map/all_to_all | solution.py:400
  22.1 53.8 %collective-permute-start = (bf16[4,3,896,128]{3,2,1,0:T(8,128)(2,1)}, bf16[4,3,896,128]{3,2,1,0:T(8,128)(2,1)S(1)}, u32[]{:S(2)}, u32[]{:S(2)}) collective-permute-start(bf16[4,3,896,128]{3,2,1,0:T(8,128)(2,1)} %shard_map.111), channel_id=1, source_target_pairs={{0,1},{1,0},{2,3},{3,2},{4,5},{5,4},{6,7},{7,6},{8,9},{9,8},{10,11... | collective-permute-start | bytes 8257544 | tf_op jit(solution)/shard_map/ppermute | solution.py:349
  40.4 28.4 %all-to-all-start.1 = ((bf16[32,16,896]{2,1,0:T(8,128)(2,1)}), bf16[32,16,896]{2,1,0:T(8,128)(2,1)}, u32[]{:S(2)}, u32[]{:S(2)}) async-start(bf16[32,16,896]{2,1,0:T(8,128)(2,1)} %bitcast.32), calls=%async_computation.1 | async-start | bytes 1835008 | tf_op jit(solution)/shard_map/all_to_all | solution.py:400
  46.0 25.6 %collective-permute-start.1 = (bf16[512,896]{1,0:T(8,128)(2,1)}, bf16[512,896]{1,0:T(8,128)(2,1)}, u32[]{:S(2)}, u32[]{:S(2)}) collective-permute-start(bf16[512,896]{1,0:T(8,128)(2,1)} %bitcast.8.refs_4_.refs_3_), channel_id=1, source_target_pairs={{0,6},{1,7},{2,0},{3,1},{4,2},{5,3},{6,4},{7,5},{8,14},{9,15},{10,... | collective-permute-start | bytes 2752520 | tf_op jit(solution)/shard_map/ppermute | solution.py:345
  48.6 23.0 %collective-permute-start.2 = (bf16[512,896]{1,0:T(8,128)(2,1)}, bf16[512,896]{1,0:T(8,128)(2,1)}, u32[]{:S(2)}, u32[]{:S(2)}) collective-permute-start(bf16[512,896]{1,0:T(8,128)(2,1)} %bitcast.8.refs_4_.refs_3_), channel_id=1, source_target_pairs={{0,2},{1,3},{2,4},{3,5},{4,6},{5,7},{6,0},{7,1},{8,10},{9,11},{10,... | collective-permute-start | bytes 2752520 | tf_op jit(solution)/shard_map/ppermute | solution.py:345
  68.9 29.4 %copy-start.1 = (bf16[1,7168,128]{2,1,0:T(8,128)(2,1)S(1)}, bf16[1,7168,128]{2,1,0:T(8,128)(2,1)}, u32[]{:S(2)}) copy-start(bf16[1,7168,128]{2,1,0:T(8,128)(2,1)} %param.11) | copy-start | bytes 5505028
  68.9 39.7 %collective-permute-start.6 = (bf16[512,896]{1,0:T(8,128)(2,1)}, bf16[512,896]{1,0:T(8,128)(2,1)S(1)}, u32[]{:S(2)}, u32[]{:S(2)}) collective-permute-start(bf16[512,896]{1,0:T(8,128)(2,1)} %bitcast.10.refs_3_.refs_8_), channel_id=1, source_target_pairs={{0,2},{1,3},{2,4},{3,5},{4,6},{5,7},{6,0},{7,1},{8,10},{9,11},{10,... | collective-permute-start | bytes 2752520 | tf_op jit(solution)/shard_map/ppermute | solution.py:345
  70.1 38.5 %collective-permute-start.7 = (bf16[512,896]{1,0:T(8,128)(2,1)}, bf16[512,896]{1,0:T(8,128)(2,1)S(1)}, u32[]{:S(2)}, u32[]{:S(2)}) collective-permute-start(bf16[512,896]{1,0:T(8,128)(2,1)} %bitcast.10.refs_3_.refs_8_), channel_id=1, source_target_pairs={{0,6},{1,7},{2,0},{3,1},{4,2},{5,3},{6,4},{7,5},{8,14},{9,15},{10,... | collective-permute-start | bytes 2752520 | tf_op jit(solution)/shard_map/ppermute | solution.py:345
  73.1 25.2 %collective-permute-start.3 = (bf16[256,896]{1,0:T(8,128)(2,1)S(1)}, bf16[256,896]{1,0:T(8,128)(2,1)S(1)}, u32[]{:S(2)}, u32[]{:S(2)}) collective-permute-start(bf16[256,896]{1,0:T(8,128)(2,1)S(1)} %get-tuple-element.43), channel_id=1, source_target_pairs={{0,2},{1,3},{2,4},{3,5},{4,6},{5,7},{6,0},{7,1},{8,10},{9,11},{10,... | collective-permute-start | bytes 1376264 | tf_op jit(solution)/shard_map/ppermute | solution.py:345
  73.2 25.1 %collective-permute-start.4 = (bf16[256,896]{1,0:T(8,128)(2,1)S(1)}, bf16[256,896]{1,0:T(8,128)(2,1)S(1)}, u32[]{:S(2)}, u32[]{:S(2)}) collective-permute-start(bf16[256,896]{1,0:T(8,128)(2,1)S(1)} %get-tuple-element.44), channel_id=1, source_target_pairs={{0,6},{1,7},{2,0},{3,1},{4,2},{5,3},{6,4},{7,5},{8,14},{9,15},{10,... | collective-permute-start | bytes 1376264 | tf_op jit(solution)/shard_map/ppermute | solution.py:345
  103.9 22.8 %collective-permute-start.5 = (f32[512,512]{1,0:T(8,128)S(1)}, f32[512,512]{1,0:T(8,128)S(1)}, u32[]{:S(2)}, u32[]{:S(2)}) collective-permute-start(f32[512,512]{1,0:T(8,128)S(1)} %get-tuple-element.46), channel_id=1, source_target_pairs={{0,1},{1,0},{2,3},{3,2},{4,5},{5,4},{6,7},{7,6},{8,9},{9,8},{10,11... | collective-permute-start | bytes 3145736 | tf_op jit(solution)/shard_map/ppermute | solution.py:349
  109.7 13.3 %collective-permute-start.8 = (bf16[256,896]{1,0:T(8,128)(2,1)S(1)}, bf16[256,896]{1,0:T(8,128)(2,1)S(1)}, u32[]{:S(2)}, u32[]{:S(2)}) collective-permute-start(bf16[256,896]{1,0:T(8,128)(2,1)S(1)} %get-tuple-element.49), channel_id=1, source_target_pairs={{0,2},{1,3},{2,4},{3,5},{4,6},{5,7},{6,0},{7,1},{8,10},{9,11},{10,... | collective-permute-start | bytes 1376264 | tf_op jit(solution)/shard_map/ppermute | solution.py:345
  110.9 12.1 %collective-permute-start.9 = (bf16[256,896]{1,0:T(8,128)(2,1)S(1)}, bf16[256,896]{1,0:T(8,128)(2,1)S(1)}, u32[]{:S(2)}, u32[]{:S(2)}) collective-permute-start(bf16[256,896]{1,0:T(8,128)(2,1)S(1)} %get-tuple-element.50), channel_id=1, source_target_pairs={{0,6},{1,7},{2,0},{3,1},{4,2},{5,3},{6,4},{7,5},{8,14},{9,15},{10,... | collective-permute-start | bytes 1376264 | tf_op jit(solution)/shard_map/ppermute | solution.py:345
  124.1 2.6 collective-permute-start.10
  128.3 16.3 %collective-permute-start.11 = (bf16[256,896]{1,0:T(8,128)(2,1)S(1)}, bf16[256,896]{1,0:T(8,128)(2,1)S(1)}, u32[]{:S(2)}, u32[]{:S(2)}) collective-permute-start(bf16[256,896]{1,0:T(8,128)(2,1)S(1)} %get-tuple-element.57), channel_id=1, source_target_pairs={{0,2},{1,3},{2,4},{3,5},{4,6},{5,7},{6,0},{7,1},{8,10},{9,11},{10,... | collective-permute-start | bytes 1376264 | tf_op jit(solution)/shard_map/ppermute | solution.py:345
  129.3 15.3 %collective-permute-start.12 = (bf16[256,896]{1,0:T(8,128)(2,1)S(1)}, bf16[256,896]{1,0:T(8,128)(2,1)S(1)}, u32[]{:S(2)}, u32[]{:S(2)}) collective-permute-start(bf16[256,896]{1,0:T(8,128)(2,1)S(1)} %get-tuple-element.58), channel_id=1, source_target_pairs={{0,6},{1,7},{2,0},{3,1},{4,2},{5,3},{6,4},{7,5},{8,14},{9,15},{10,... | collective-permute-start | bytes 1376264 | tf_op jit(solution)/shard_map/ppermute | solution.py:345
  133.6 29.6 %collective-permute-start.14 = (bf16[256,896]{1,0:T(8,128)(2,1)S(1)}, bf16[256,896]{1,0:T(8,128)(2,1)S(1)}, u32[]{:S(2)}, u32[]{:S(2)}) collective-permute-start(bf16[256,896]{1,0:T(8,128)(2,1)S(1)} %get-tuple-element.63), channel_id=1, source_target_pairs={{0,2},{1,3},{2,4},{3,5},{4,6},{5,7},{6,0},{7,1},{8,10},{9,11},{10,... | collective-permute-start | bytes 1376264 | tf_op jit(solution)/shard_map/ppermute | solution.py:345
  133.6 29.6 %collective-permute-start.15 = (bf16[256,896]{1,0:T(8,128)(2,1)S(1)}, bf16[256,896]{1,0:T(8,128)(2,1)S(1)}, u32[]{:S(2)}, u32[]{:S(2)}) collective-permute-start(bf16[256,896]{1,0:T(8,128)(2,1)S(1)} %get-tuple-element.64), channel_id=1, source_target_pairs={{0,6},{1,7},{2,0},{3,1},{4,2},{5,3},{6,4},{7,5},{8,14},{9,15},{10,... | collective-permute-start | bytes 1376264 | tf_op jit(solution)/shard_map/ppermute | solution.py:345
  145.3 17.9 %collective-permute-start.13 = (bf16[256,896]{1,0:T(8,128)(2,1)S(1)}, bf16[256,896]{1,0:T(8,128)(2,1)S(1)}, u32[]{:S(2)}, u32[]{:S(2)}) collective-permute-start(bf16[256,896]{1,0:T(8,128)(2,1)S(1)} %get-tuple-element.62), channel_id=1, source_target_pairs={{0,2},{1,3},{2,4},{3,5},{4,6},{5,7},{6,0},{7,1},{8,10},{9,11},{10,... | collective-permute-start | bytes 1376264 | tf_op jit(solution)/shard_map/ppermute | solution.py:345
  145.4 17.8 %collective-permute-start.16 = (bf16[256,896]{1,0:T(8,128)(2,1)S(1)}, bf16[256,896]{1,0:T(8,128)(2,1)S(1)}, u32[]{:S(2)}, u32[]{:S(2)}) collective-permute-start(bf16[256,896]{1,0:T(8,128)(2,1)S(1)} %get-tuple-element.65), channel_id=1, source_target_pairs={{0,6},{1,7},{2,0},{3,1},{4,2},{5,3},{6,4},{7,5},{8,14},{9,15},{10,... | collective-permute-start | bytes 1376264 | tf_op jit(solution)/shard_map/ppermute | solution.py:345
  165.0 19.3 %collective-permute-start.17 = (bf16[4,3,896,128]{3,2,1,0:T(8,128)(2,1)}, bf16[4,3,896,128]{3,2,1,0:T(8,128)(2,1)}, u32[]{:S(2)}, u32[]{:S(2)}) collective-permute-start(bf16[4,3,896,128]{3,2,1,0:T(8,128)(2,1)} %shard_map.123), channel_id=1, source_target_pairs={{0,1},{1,0},{2,3},{3,2},{4,5},{5,4},{6,7},{7,6},{8,9},{9,8},{10,11... | collective-permute-start | bytes 8257544 | tf_op jit(solution)/shard_map/ppermute | solution.py:349
  168.4 103.3 %all-to-all-start.3 = ((bf16[32,16,896]{2,1,0:T(8,128)(2,1)}), bf16[32,16,896]{2,1,0:T(8,128)(2,1)S(1)}, u32[]{:S(2)}, u32[]{:S(2)}) async-start(bf16[32,16,896]{2,1,0:T(8,128)(2,1)} %bitcast.14), calls=%async_computation.3 | async-start | bytes 1835008 | tf_op jit(solution)/shard_map/all_to_all | solution.py:400
  174.0 3.9 %collective-permute-start.18 = (f32[32,16]{1,0:T(8,128)S(1)}, f32[32,16]{1,0:T(8,128)S(1)}, u32[]{:S(2)}, u32[]{:S(2)}) collective-permute-start(f32[32,16]{1,0:T(8,128)S(1)} %bitcast.35), channel_id=1, source_target_pairs={{0,2},{1,3},{2,4},{3,5},{4,6},{5,7},{6,0},{7,1},{8,10},{9,11},{10,... | collective-permute-start | bytes 6152 | tf_op jit(solution)/shard_map/ppermute | solution.py:345
  177.9 4.4 %collective-permute-start.19 = (f32[32,16]{1,0:T(8,128)S(1)}, f32[32,16]{1,0:T(8,128)S(1)}, u32[]{:S(2)}, u32[]{:S(2)}) collective-permute-start(f32[32,16]{1,0:T(8,128)S(1)} %add.8.refs_4_), channel_id=1, source_target_pairs={{0,4},{1,5},{2,6},{3,7},{4,0},{5,1},{6,2},{7,3},{8,12},{9,13},{10,... | collective-permute-start | bytes 6152 | tf_op jit(solution)/shard_map/ppermute | solution.py:345
  (13 other events, 81.0 us)

commit v3 on v2

--- a/solution.py
+++ b/solution.py
@@ -57,7 +57,6 @@
 VM = pl.BlockSpec(memory_space=pltpu.VMEM)
 SM = pl.BlockSpec(memory_space=pltpu.SMEM)
 ANY = pl.BlockSpec(memory_space=pl.ANY)
-HBM = pl.BlockSpec(memory_space=pltpu.HBM)
 
 
 CUTS = (7, 14)
@@ -129,7 +128,8 @@
                 outs[message - 1][:, column : column + many] = value.astype(BF)
 
 
-def halves_body(at, gate, up, down, out):
+def halves_body(at, gate, up, down, out, token):
+    token[...] = jnp.zeros((8, 128), F32)
     units, block = down.shape
     out[0, 0] = gate[...]
     out[0, 1] = up[...]
@@ -145,14 +145,17 @@
     wide = pl.BlockSpec((units, block), lambda r, at: (0, other(r, at)))
     return pl.pallas_call(
         halves_body,
-        out_shape=shape((CHIPS, 3, block, units), BF),
+        out_shape=(shape((CHIPS, 3, block, units), BF), shape((8, 128), F32)),
         compiler_params=pltpu.CompilerParams(vmem_limit_bytes=VMEM_LIMIT),
         cost_estimate=pl.CostEstimate(flops=0, bytes_accessed=12 * depth * units, transcendentals=0),
         grid_spec=pltpu.PrefetchScalarGridSpec(
             num_scalar_prefetch=1,
             grid=(CHIPS,),
             in_specs=[tall, tall, wide],
-            out_specs=pl.BlockSpec((1, 3, block, units), lambda r, at: (r, 0, 0, 0)),
+            out_specs=[
+                pl.BlockSpec((1, 3, block, units), lambda r, at: (r, 0, 0, 0)),
+                pl.BlockSpec((8, 128), lambda r, at: (0, 0)),
+            ],
         ),
     )(at, w_gate, w_up, w_down)
 
@@ -182,13 +185,12 @@
     return ((0, ref[:half, columns]), (half, ref[half:, columns]))
 
 
-def send_swapped(keep, send, units):
-    for i in range(keep.shape[1] // units):
-        j = i ^ 1
-        send[:, i * units : (i + 1) * units] = keep[:, j * units : (j + 1) * units]
-
-
-def add_body(piece, which, first, last, pre, at, *refs):
+def swapped(value, units):
+    pieces = [value[:, i : i + units] for i in range(0, value.shape[1], units)]
+    return jnp.concatenate([pieces[i ^ 1] for i in range(len(pieces))], axis=1).astype(BF)
+
+
+def add_body(piece, which, first, pre, at, *refs):
     _, column, feature, many = piece
     columns = slice(column, column + many)
     weights, refs = (refs[:3], refs[3:]) if pre else (refs[:2], refs[2:])
@@ -207,11 +209,22 @@
                 keep[lo : lo + half, :] = value if first else before[lo : lo + half, :] + value
             else:
                 keep[lo : lo + half, :] += value
-    if last:
-        send_swapped(keep, refs[1], weights[0].shape[1 if pre else 0])
-
-
-def middle_body(at, pre, pre_recv, back, back_recv, gate, up, others, d, act_rows, sums, opp_a, opp_b):
+
+
+def early_body(x_piece, dy_piece, at, gate, up, others, down, *refs):
+    x, dy, (pre, back) = refs[:5], refs[5:8], refs[8:]
+    add_body(x_piece, (0, 1, 3, 2), True, True, at, gate, up, others, *x, pre)
+    add_body(dy_piece, (0, 1, 3), True, False, at, down, others, *dy, back)
+
+
+def late_body(dy_piece, at, down, others, opp_a, opp_b, before, pre, back, send):
+    add_body(dy_piece, (2,), False, False, at, down, others, opp_a, opp_b, before, back)
+    units = down.shape[0]
+    send[:, : 4 * units] = swapped(pre[...], units)
+    send[:, 4 * units :] = swapped(back[...], units)
+
+
+def middle_body(at, pre, back, recv, gate, up, others, d, act_rows, sums, opp_a, opp_b):
     rows = pre.shape[0]
     both = pre.shape[1] // 2
     half = rows // 2
@@ -222,8 +235,8 @@
     total = None
     for lo, out in ((0, opp_a), (half, opp_b)):
         span = slice(lo, lo + half)
-        pre_all = pre[span, :] + pre_recv[span, :]
-        back_all = back[span, :] + back_recv[span, :]
+        pre_all = pre[span, :] + recv[span, : 2 * both].astype(F32)
+        back_all = back[span, :] + recv[span, 2 * both :].astype(F32)
         pre_gate = pre_all[:, :both]
         pre_up = pre_all[:, both:]
         sig = jax.nn.sigmoid(pre_gate)
@@ -298,36 +311,65 @@
                 send[r, 2, feature + j : feature + j + units, :] = total[units:, j : j + units]
 
 
-def place_body(at, keep, recv, gate, up, down, sems):
-    block, units = keep.shape[2:]
-    copies = []
-
-    def add(source, target):
-        copies.append(pltpu.make_async_copy(source, target, sems.at[len(copies)]))
-        copies[-1].start()
-
-    for r in range(CHIPS):
-        for held, core in ((keep, at[1]), (recv, 1 - at[1])):
-            start = pl.multiple_of((2 * lax.rem(at[0] + r, CHIPS) + core) * block, 128)
-            add(held.at[r, 0], gate.at[pl.ds(start, block), :])
-            add(held.at[r, 1], up.at[pl.ds(start, block), :])
-            for j in range(0, block, units):
-                add(held.at[r, 2, pl.ds(j, units)], down.at[:, pl.ds(pl.multiple_of(start + j, 128), units)])
-    for copy in copies:
-        copy.wait()
+def place_body(at, keep, recv, gate, up, down, token):
+    token[...] = jnp.zeros((8, 128), F32)
+    units = gate.shape[1]
+    mine = lax.rem(pl.program_id(0), 2) == at[1]
+
+    def put(held):
+        gate[...] = held[0, 0]
+        up[...] = held[0, 1]
+        for j in range(0, gate.shape[0], units):
+            down[:, j : j + units] = held[0, 2, j : j + units, :]
+
+    @pl.when(mine)
+    def _():
+        put(keep)
+
+    @pl.when(jnp.logical_not(mine))
+    def _():
+        put(recv)
+
+
+def place(at, keep, recv):
+    _, _, block, units = keep.shape
+    depth = 2 * CHIPS * block
+    source = pl.BlockSpec((1, 3, block, units), lambda b, at: ((b // 2 + CHIPS - at[0]) % CHIPS, 0, 0, 0))
+    return pl.pallas_call(
+        place_body,
+        out_shape=(
+            shape((depth, units), BF),
+            shape((depth, units), BF),
+            shape((units, depth), BF),
+            shape((8, 128), F32),
+        ),
+        compiler_params=pltpu.CompilerParams(vmem_limit_bytes=VMEM_LIMIT),
+        cost_estimate=pl.CostEstimate(flops=0, bytes_accessed=12 * depth * units, transcendentals=0),
+        grid_spec=pltpu.PrefetchScalarGridSpec(
+            num_scalar_prefetch=1,
+            grid=(2 * CHIPS,),
+            in_specs=[source, source],
+            out_specs=[
+                pl.BlockSpec((block, units), lambda b, at: (b, 0)),
+                pl.BlockSpec((block, units), lambda b, at: (b, 0)),
+                pl.BlockSpec((units, block), lambda b, at: (0, b)),
+                pl.BlockSpec((8, 128), lambda b, at: (0, 0)),
+            ],
+        ),
+    )(at, keep, recv)
 
 
 def finish_body(at, pick, back, grad):
     grad[...] = mm(pick[...], back[...], TN).astype(BF)
 
 
-def gating_body(at, pick, routes, gates, sums, others, grad):
+def gating_body(at, pick, routes, gates, sums, left, far, right, grad):
     topk, count = routes.shape
     rows = pick.shape[0]
     experts = rows // CAP
     owner = owner_of(rows, experts)
     spread = lax.dot_general(
-        owner, sums[...] + others[...], NN, preferred_element_type=F32, precision=lax.Precision.HIGHEST
+        owner, sums[...] + left[...] + far[...] + right[...], NN, preferred_element_type=F32, precision=lax.Precision.HIGHEST
     )
     value = jnp.sum(jnp.where(slot_is(rows, CAP), spread, 0.0), axis=1, keepdims=True)
     table = lax.dot_general(
@@ -409,10 +451,12 @@
         (at, routes, gates, my_tokens),
     )
     arrived = [over_experts(message)]
+    halved, token = halves(at, gate, up, down)
     messages = call(
         rest_body,
         tuple(shape((rows, many), BF) for many in widths(block)[1:]),
         (at, pick, weighted, my_tokens, my_block(grad_out)),
+        after=(token,),
     )
     arrived += [over_experts(message) for message in messages]
     gathered = []
@@ -420,39 +464,31 @@
     for value in arrived:
         parts, token = ring_gather(at, value, token)
         gathered.append(parts)
-    others = swap(halves(at, gate, up, down))
+    others = swap(halved)
     weights = (gate, up, others)
 
-    pre = ()
-    for i, piece in enumerate(of_tokens):
-        pre = call(
-            functools.partial(add_body, piece, (0, 1, 3, 2), i == 0, i == len(of_tokens) - 1, True),
-            (shape((rows, 2 * both), F32),) * (1 + (i == len(of_tokens) - 1)),
-            (at, *weights, *gathered[piece[0]], *pre),
-        )
-    pre, pre_send = pre
-    pre_recv = swap(pre_send)
-    narrow = (shape((rows, both), F32),)
-    back = ()
-    turns = [(piece, (0, 1, 3, 2)) for piece in of_cotangents[:-1]]
-    for piece, which in turns + [(of_cotangents[-1], (0, 1, 3)), (of_cotangents[-1], (2,))]:
-        last = which == (2,)
-        parts = gathered[piece[0]]
-        parts = parts[3:] if last else parts[: 5 if 2 in which else 3]
-        back = call(
-            functools.partial(add_body, piece, which, not back, last, False),
-            narrow * (1 + last),
-            (at, down, others, *parts, *back),
-        )
-    back, back_send = back
-    back_recv = swap(back_send)
+    (x_piece,), (dy_piece,) = of_tokens, of_cotangents
+    x, dy = gathered
+    narrow = shape((rows, both), F32)
+    pre, back = call(
+        functools.partial(early_body, x_piece, dy_piece),
+        (shape((rows, 2 * both), F32), narrow),
+        (at, gate, up, others, down, *x, *dy[:3]),
+        after=token,
+    )
+    back, send = call(
+        functools.partial(late_body, dy_piece),
+        (narrow, shape((rows, 3 * both), BF)),
+        (at, down, others, *dy[3:], back, pre),
+    )
+    recv = swap(send)
 
     part = (shape((half, block), BF),)
     later = (shape((half, block), F32),)
     d, act_rows, sums, opp_a, opp_b = call(
         middle_body,
         (shape((rows, 2 * both), BF), shape((rows, both), BF), shape((experts, CAP), F32)) + part * 2,
-        (at, pre, pre_recv, back, back_recv, *weights),
+        (at, pre, back, recv, *weights),
     )
     from_left, from_right = to(opp_a, 1), to(opp_b, -1)
     to_right, to_left, right_later, left_later, own, *token = call(
@@ -480,28 +516,18 @@
         token=True,
     )
     returned = over_experts(total)
-    *grads, placed = call(
-        place_body,
-        (shape((2 * CHIPS * block, units), BF),) * 2 + (shape((units, 2 * CHIPS * block), BF),),
-        (at, keep, swap(behind(send, token[0]))),
-        token=True,
-        scratch=[pltpu.SemaphoreType.DMA((2 * CHIPS * (2 + block // units),))],
-        places=[SM] + [ANY] * 2,
-        outs=(HBM,) * 3,
-    )
-
-    slots = slots + to(slots, 1)
+    *grads, placed = place(at, keep, swap(behind(send, token[0])))
     grad_gating, gated = call(
         gating_body,
         (shape((topk, count), F32),),
-        (at, pick, routes, gates, slots, to(slots, 2)),
+        (at, pick, routes, gates, slots, *[to(slots, shift) for shift in (1, 2, 3)]),
         token=True,
     )
     (grad_tokens,) = call(
         finish_body,
         (shape((count, block), BF),),
         (at, pick, returned),
-        after=(placed, gated),
+        after=(gated, placed),
     )
     return (grad_tokens, grad_gating.T, grads[0][None], grads[1][None], grads[2][None])
 

time: 276 us -> 194 us (0.70)
  Pallas kernels: 118 us -> 36.3 us
  starting transfers between devices: 51.9 us -> 56.7 us
  waiting for transfers between devices: 76 us -> 72.2 us
    pallas_call x15 -> x13, Pallas kernels: 115 us -> 27.4 us  [call(): pl.pallas_call(run, out_shape=out_shape + ((shape((8, 128), F32),) if tok...]
    ppermute x16 -> x17, waiting for transfers between devices: 38.9 us -> 27 us  [to(): lax.ppermute(value, 'hidden', [(i, (i + 2 * shift) % size) for i in range...]
    all_to_all x3, waiting for transfers between devices: 35.6 us -> 43.3 us  [over_experts(): lax.all_to_all(split, 'expert', split_axis=0, concat_axis=0, tiled=True)]
    pallas_call x1 -> x2, Pallas kernels: 2.78 us -> 8.94 us  [the longest x1 7.85 us: place(): pl.pallas_call(place_body, out_shape=(shape((depth, units), BF), shape((d...]
    unnamed x28 -> x34, local copies, waits for them, and re-layouts: 10.1 us -> 12.8 us
    ppermute x4 -> x3, starting transfers between devices: 10.4 us -> 13 us  [swap(): return lax.ppermute(value, 'hidden', [(i, i ^ 1) for i in range(2 * CHIPS)])]
    ppermute x16 -> x17, starting transfers between devices: 19.3 us -> 21.5 us  [to(): lax.ppermute(value, 'hidden', [(i, (i + 2 * shift) % size) for i in range...]
  transfers between devices with their start and end apart: 23 -> 23, of which waited for: 7 -> 13; matrix products, arithmetic and copies ran while one was open for 0% -> 0% of each run, Pallas kernels for 41% -> 15%
where the time goes in v3:
time: 194 us; the launch traced here: 193 us
  waiting for transfers between devices  72.2 us (37%)
  starting transfers between devices  56.7 us (29%)
  Pallas kernels  36.3 us (19%)
  local copies, waits for them, and re-layouts  13.8 us (7%)
  blocking collectives  12.9 us (7%)
    all_to_all x3, waiting for transfers between devices, over_experts(): lax.all_to_all(split, 'expert', split_axis=0, concat_axis=0, tiled=True)  43.3 us
    pallas_call x13, Pallas kernels, call(): pl.pallas_call(run, out_shape=out_shape + ((shape((8, 128), F32),) if tok...  27.4 us
    ppermute x17, waiting for transfers between devices, to(): lax.ppermute(value, 'hidden', [(i, (i + 2 * shift) % size) for i in range...  27 us
    all_to_all x3, starting transfers between devices, over_experts(): lax.all_to_all(split, 'expert', split_axis=0, concat_axis=0, tiled=True)  22.2 us
    ppermute x17, starting transfers between devices, to(): lax.ppermute(value, 'hidden', [(i, (i + 2 * shift) % size) for i in range...  21.5 us
    ppermute x3, starting transfers between devices, swap(): return lax.ppermute(value, 'hidden', [(i, i ^ 1) for i in range(2 * CHIPS)])  13 us
    all_to_all x1, blocking collectives, over_experts(): lax.all_to_all(split, 'expert', split_axis=0, concat_axis=0, tiled=True)  12.9 us
    unnamed x34, local copies, waits for them, and re-layouts  12.8 us
  transfers between devices with their start and end apart: 23, of which 13 were waited for; matrix products, arithmetic and copies ran while one was open for 0% of the time, Pallas kernels for 15%

profile of v3, /device:TPU:17, one launch (start us, length us, event | category | flops | bytes accessed | tf_op | source)
XLA Modules:
  0.0 192.8 jit_solution(14243218354164186968)
XLA Ops:
  5.2 11.0 %all-to-all-start = ((bf16[32,16,896]{2,1,0:T(8,128)(2,1)}), bf16[32,16,896]{2,1,0:T(8,128)(2,1)S(1)}, u32[]{:S(2)}, u32[]{:S(2)}) async-start(bf16[32,16,896]{2,1,0:T(8,128)(2,1)} %bitcast.37), calls=%async_computation | async-start | bytes 1835008 | tf_op jit(solution)/shard_map/all_to_all | solution.py:442
  23.7 16.6 %all-to-all-done = bf16[32,16,896]{2,1,0:T(8,128)(2,1)S(1)} async-done(((bf16[32,16,896]{2,1,0:T(8,128)(2,1)}), bf16[32,16,896]{2,1,0:T(8,128)(2,1)S(1)}, u32[]{:S(2)}, u32[]{:S(2)}) %all-to-all-start) | async-done | bytes 917536 | tf_op jit(solution)/shard_map/all_to_all | solution.py:442
  40.3 5.5 %all-to-all-start.1 = ((bf16[32,16,896]{2,1,0:T(8,128)(2,1)}), bf16[32,16,896]{2,1,0:T(8,128)(2,1)}, u32[]{:S(2)}, u32[]{:S(2)}) async-start(bf16[32,16,896]{2,1,0:T(8,128)(2,1)} %bitcast.9), calls=%async_computation.1 | async-start | bytes 1835008 | tf_op jit(solution)/shard_map/all_to_all | solution.py:442
  45.9 2.5 %collective-permute-start = (bf16[4,3,896,128]{3,2,1,0:T(8,128)(2,1)}, bf16[4,3,896,128]{3,2,1,0:T(8,128)(2,1)S(1)}, u32[]{:S(2)}, u32[]{:S(2)}) collective-permute-start(bf16[4,3,896,128]{3,2,1,0:T(8,128)(2,1)} %copy-done.16), channel_id=1, source_target_pairs={{0,1},{1,0},{2,3},{3,2},{4,5},{5,4},{6,7},{7,6},{8,9},{9,8},{10,11... | collective-permute-start | bytes 8257544 | tf_op jit(solution)/shard_map/ppermute | solution.py:391
  48.5 2.5 %collective-permute-start.1 = (bf16[512,896]{1,0:T(8,128)(2,1)}, bf16[512,896]{1,0:T(8,128)(2,1)}, u32[]{:S(2)}, u32[]{:S(2)}) collective-permute-start(bf16[512,896]{1,0:T(8,128)(2,1)} %bitcast.32), channel_id=1, source_target_pairs={{0,6},{1,7},{2,0},{3,1},{4,2},{5,3},{6,4},{7,5},{8,14},{9,15},{10,... | collective-permute-start | bytes 2752520 | tf_op jit(solution)/shard_map/ppermute | solution.py:387
  51.0 17.8 %all-to-all-done.1 = bf16[32,16,896]{2,1,0:T(8,128)(2,1)} async-done(((bf16[32,16,896]{2,1,0:T(8,128)(2,1)}), bf16[32,16,896]{2,1,0:T(8,128)(2,1)}, u32[]{:S(2)}, u32[]{:S(2)}) %all-to-all-start.1) | async-done | bytes 917536 | tf_op jit(solution)/shard_map/all_to_all | solution.py:442
  71.3 2.8 %collective-permute-done.2.refs_1_.refs_7_.refs_5_ = bf16[512,896]{1,0:T(8,128)(2,1)} collective-permute-done((bf16[512,896]{1,0:T(8,128)(2,1)}, bf16[512,896]{1,0:T(8,128)(2,1)}, u32[]{:S(2)}, u32[]{:S(2)}) %collective-permute-start.2) | collective-permute-done | bytes 917536 | tf_op jit(solution)/shard_map/ppermute | solution.py:387
  75.7 2.7 %collective-permute-start.4 = (bf16[256,896]{1,0:T(8,128)(2,1)S(1)}, bf16[256,896]{1,0:T(8,128)(2,1)S(1)}, u32[]{:S(2)}, u32[]{:S(2)}) collective-permute-start(bf16[256,896]{1,0:T(8,128)(2,1)S(1)} %get-tuple-element.48), channel_id=1, source_target_pairs={{0,6},{1,7},{2,0},{3,1},{4,2},{5,3},{6,4},{7,5},{8,14},{9,15},{10,... | collective-permute-start | bytes 1376264 | tf_op jit(solution)/shard_map/ppermute | solution.py:387
  78.4 9.2 %collective-permute-done.5.refs_2_.refs_11_.refs_9_ = bf16[512,896]{1,0:T(8,128)(2,1)S(1)} collective-permute-done((bf16[512,896]{1,0:T(8,128)(2,1)}, bf16[512,896]{1,0:T(8,128)(2,1)S(1)}, u32[]{:S(2)}, u32[]{:S(2)}) %collective-permute-start.5) | collective-permute-done | bytes 917536 | tf_op jit(solution)/shard_map/ppermute | solution.py:387
  87.5 3.0 %collective-permute-done.6.refs_1_.refs_12_.refs_10_ = bf16[512,896]{1,0:T(8,128)(2,1)S(1)} collective-permute-done((bf16[512,896]{1,0:T(8,128)(2,1)}, bf16[512,896]{1,0:T(8,128)(2,1)S(1)}, u32[]{:S(2)}, u32[]{:S(2)}) %collective-permute-start.6) | collective-permute-done | bytes 917536 | tf_op jit(solution)/shard_map/ppermute | solution.py:387
  91.3 2.7 %collective-permute-start.8 = (bf16[256,896]{1,0:T(8,128)(2,1)S(1)}, bf16[256,896]{1,0:T(8,128)(2,1)S(1)}, u32[]{:S(2)}, u32[]{:S(2)}) collective-permute-start(bf16[256,896]{1,0:T(8,128)(2,1)S(1)} %get-tuple-element.55), channel_id=1, source_target_pairs={{0,6},{1,7},{2,0},{3,1},{4,2},{5,3},{6,4},{7,5},{8,14},{9,15},{10,... | collective-permute-start | bytes 1376264 | tf_op jit(solution)/shard_map/ppermute | solution.py:387
  93.9 6.5 %collective-permute-done.3.refs_8_.refs_6_ = bf16[256,896]{1,0:T(8,128)(2,1)S(1)} collective-permute-done((bf16[256,896]{1,0:T(8,128)(2,1)S(1)}, bf16[256,896]{1,0:T(8,128)(2,1)S(1)}, u32[]{:S(2)}, u32[]{:S(2)}) %collective-permute-start.3) | collective-permute-done | bytes 458784 | tf_op jit(solution)/shard_map/ppermute | solution.py:387
  103.1 4.9 %shard_map.115 = (f32[512,512]{1,0:T(8,128)S(1)}, f32[512,256]{1,0:T(8,128)S(1)}) custom-call(s32[2]{0:T(128)S(1)} %pad_add_fusion.refs_0_.at, bf16[7168,128]{1,0:T(8,128)(2,1)S(1)} %bitcast.22, bf16[7168,128]{1,0:T(8,128)(2,1)S(1)} %bitcast.26, bf16[4,3,896,128]{3,2,1,0:T(8,128)(2,1)S(1)} %collective-permute-done.refs_3_.refs_2_.refs_6_.refs_4_, ...), custom_call_target="tpu_custom_call" | custom-call | bytes 16252928 | tf_op jit(solution)/shard_map/pallas_call | solution.py:42
  111.3 7.4 %collective-permute-start.9 = (bf16[512,768]{1,0:T(8,128)(2,1)S(1)}, bf16[512,768]{1,0:T(8,128)(2,1)S(1)}, u32[]{:S(2)}, u32[]{:S(2)}) collective-permute-start(bf16[512,768]{1,0:T(8,128)(2,1)S(1)} %get-tuple-element.58), channel_id=1, source_target_pairs={{0,1},{1,0},{2,3},{3,2},{4,5},{5,4},{6,7},{7,6},{8,9},{9,8},{10,11... | collective-permute-start | bytes 2359304 | tf_op jit(solution)/shard_map/ppermute | solution.py:391
  122.2 2.7 %collective-permute-start.11 = (bf16[256,896]{1,0:T(8,128)(2,1)S(1)}, bf16[256,896]{1,0:T(8,128)(2,1)S(1)}, u32[]{:S(2)}, u32[]{:S(2)}) collective-permute-start(bf16[256,896]{1,0:T(8,128)(2,1)S(1)} %get-tuple-element.64), channel_id=1, source_target_pairs={{0,6},{1,7},{2,0},{3,1},{4,2},{5,3},{6,4},{7,5},{8,14},{9,15},{10,... | collective-permute-start | bytes 1376264 | tf_op jit(solution)/shard_map/ppermute | solution.py:387
  127.3 2.7 %collective-permute-start.14 = (bf16[256,896]{1,0:T(8,128)(2,1)S(1)}, bf16[256,896]{1,0:T(8,128)(2,1)S(1)}, u32[]{:S(2)}, u32[]{:S(2)}) collective-permute-start(bf16[256,896]{1,0:T(8,128)(2,1)S(1)} %get-tuple-element.70), channel_id=1, source_target_pairs={{0,6},{1,7},{2,0},{3,1},{4,2},{5,3},{6,4},{7,5},{8,14},{9,15},{10,... | collective-permute-start | bytes 1376264 | tf_op jit(solution)/shard_map/ppermute | solution.py:387
  130.0 6.5 %shard_map.119 = (bf16[4,3,896,128]{3,2,1,0:T(8,128)(2,1)S(1)}, bf16[4,3,896,128]{3,2,1,0:T(8,128)(2,1)}, f32[8,128]{1,0:T(8,128)S(1)}) custom-call(s32[2]{0:T(128)S(1)} %pad_add_fusion.refs_0_.at, bf16[512,512]{1,0:T(8,128)(2,1)S(1)} %get-tuple-element.59.refs_1_, bf16[512,256]{1,0:T(8,128)(2,1)S(1)} %get-tuple-element.65.refs_2_, ...), custom_call_target="tpu_custom_call" | custom-call | bytes 13631488 | tf_op jit(solution)/shard_map/pallas_call | solution.py:42
  138.8 2.7 %collective-permute-start.15 = (bf16[256,896]{1,0:T(8,128)(2,1)S(1)}, bf16[256,896]{1,0:T(8,128)(2,1)S(1)}, u32[]{:S(2)}, u32[]{:S(2)}) collective-permute-start(bf16[256,896]{1,0:T(8,128)(2,1)S(1)} %get-tuple-element.71), channel_id=1, source_target_pairs={{0,6},{1,7},{2,0},{3,1},{4,2},{5,3},{6,4},{7,5},{8,14},{9,15},{10,... | collective-permute-start | bytes 1376264 | tf_op jit(solution)/shard_map/ppermute | solution.py:387
  141.5 12.9 %all_to_all.20 = f32[32,1,16]{2,1,0:T(1,128)S(1)} all-to-all(f32[32,1,16]{2,1,0:T(1,128)S(1)} %bitcast.45), channel_id=1, replica_groups=mesh['expert'=32,'hidden'=8] {'expert'}, dimensions={0} | all-to-all | bytes 4096 | tf_op jit(solution)/shard_map/all_to_all | solution.py:442
  156.5 3.1 %collective-permute-start.19 = (bf16[4,3,896,128]{3,2,1,0:T(8,128)(2,1)}, bf16[4,3,896,128]{3,2,1,0:T(8,128)(2,1)}, u32[]{:S(2)}, u32[]{:S(2)}) collective-permute-start(bf16[4,3,896,128]{3,2,1,0:T(8,128)(2,1)} %shard_map.123), channel_id=1, source_target_pairs={{0,1},{1,0},{2,3},{3,2},{4,5},{5,4},{6,7},{7,6},{8,9},{9,8},{10,11... | collective-permute-start | bytes 8257544 | tf_op jit(solution)/shard_map/ppermute | solution.py:391
  159.6 5.6 %all-to-all-start.3 = ((bf16[32,16,896]{2,1,0:T(8,128)(2,1)}), bf16[32,16,896]{2,1,0:T(8,128)(2,1)S(1)}, u32[]{:S(2)}, u32[]{:S(2)}) async-start(bf16[32,16,896]{2,1,0:T(8,128)(2,1)} %bitcast.14), calls=%async_computation.3 | async-start | bytes 1835008 | tf_op jit(solution)/shard_map/all_to_all | solution.py:442
  165.3 2.7 %collective-permute-start.17 = (f32[32,16]{1,0:T(8,128)S(1)}, f32[32,16]{1,0:T(8,128)S(1)}, u32[]{:S(2)}, u32[]{:S(2)}) collective-permute-start(f32[32,16]{1,0:T(8,128)S(1)} %bitcast.40), channel_id=1, source_target_pairs={{0,4},{1,5},{2,6},{3,7},{4,0},{5,1},{6,2},{7,3},{8,12},{9,13},{10,... | collective-permute-start | bytes 6152 | tf_op jit(solution)/shard_map/ppermute | solution.py:387
  174.6 7.9 %shard_map.124 = (bf16[7168,128]{1,0:T(8,128)(2,1)}, bf16[7168,128]{1,0:T(8,128)(2,1)}, bf16[128,7168]{1,0:T(8,128)(2,1)}, f32[8,128]{1,0:T(8,128)S(1)}) custom-call(s32[2]{0:T(128)S(1)} %pad_add_fusion.refs_0_.at, bf16[4,3,896,128]{3,2,1,0:T(8,128)(2,1)S(1)} %copy-done.10, bf16[4,3,896,128]{3,2,1,0:T(8,128)(2,1)} %collective-permute-done.19.recv), custom_call_target="tpu_custom_call" | custom-call | bytes 11010048 | tf_op jit(solution)/shard_map/pallas_call | solution.py:338
  182.5 8.9 %all-to-all-done.3 = bf16[32,16,896]{2,1,0:T(8,128)(2,1)S(1)} async-done(((bf16[32,16,896]{2,1,0:T(8,128)(2,1)}), bf16[32,16,896]{2,1,0:T(8,128)(2,1)S(1)}, u32[]{:S(2)}, u32[]{:S(2)}) %all-to-all-start.3) | async-done | bytes 917536 | tf_op jit(solution)/shard_map/all_to_all | solution.py:442
  (75 shorter events, 41.4 us)
Async XLA Ops:
  5.2 35.1 %all-to-all-start = ((bf16[32,16,896]{2,1,0:T(8,128)(2,1)}), bf16[32,16,896]{2,1,0:T(8,128)(2,1)S(1)}, u32[]{:S(2)}, u32[]{:S(2)}) async-start(bf16[32,16,896]{2,1,0:T(8,128)(2,1)} %bitcast.37), calls=%async_computation | async-start | bytes 1835008 | tf_op jit(solution)/shard_map/all_to_all | solution.py:442
  40.3 28.4 %all-to-all-start.1 = ((bf16[32,16,896]{2,1,0:T(8,128)(2,1)}), bf16[32,16,896]{2,1,0:T(8,128)(2,1)}, u32[]{:S(2)}, u32[]{:S(2)}) async-start(bf16[32,16,896]{2,1,0:T(8,128)(2,1)} %bitcast.9), calls=%async_computation.1 | async-start | bytes 1835008 | tf_op jit(solution)/shard_map/all_to_all | solution.py:442
  45.9 48.0 %collective-permute-start = (bf16[4,3,896,128]{3,2,1,0:T(8,128)(2,1)}, bf16[4,3,896,128]{3,2,1,0:T(8,128)(2,1)S(1)}, u32[]{:S(2)}, u32[]{:S(2)}) collective-permute-start(bf16[4,3,896,128]{3,2,1,0:T(8,128)(2,1)} %copy-done.16), channel_id=1, source_target_pairs={{0,1},{1,0},{2,3},{3,2},{4,5},{5,4},{6,7},{7,6},{8,9},{9,8},{10,11... | collective-permute-start | bytes 8257544 | tf_op jit(solution)/shard_map/ppermute | solution.py:391
  48.5 22.8 %collective-permute-start.1 = (bf16[512,896]{1,0:T(8,128)(2,1)}, bf16[512,896]{1,0:T(8,128)(2,1)}, u32[]{:S(2)}, u32[]{:S(2)}) collective-permute-start(bf16[512,896]{1,0:T(8,128)(2,1)} %bitcast.32), channel_id=1, source_target_pairs={{0,6},{1,7},{2,0},{3,1},{4,2},{5,3},{6,4},{7,5},{8,14},{9,15},{10,... | collective-permute-start | bytes 2752520 | tf_op jit(solution)/shard_map/ppermute | solution.py:387
  51.0 23.1 %collective-permute-start.2 = (bf16[512,896]{1,0:T(8,128)(2,1)}, bf16[512,896]{1,0:T(8,128)(2,1)}, u32[]{:S(2)}, u32[]{:S(2)}) collective-permute-start(bf16[512,896]{1,0:T(8,128)(2,1)} %bitcast.33), channel_id=1, source_target_pairs={{0,2},{1,3},{2,4},{3,5},{4,6},{5,7},{6,0},{7,1},{8,10},{9,11},{10,... | collective-permute-start | bytes 2752520 | tf_op jit(solution)/shard_map/ppermute | solution.py:387
  68.8 31.6 %copy-start.3 = (bf16[1,7168,128]{2,1,0:T(8,128)(2,1)S(1)}, bf16[1,7168,128]{2,1,0:T(8,128)(2,1)}, u32[]{:S(2)}) copy-start(bf16[1,7168,128]{2,1,0:T(8,128)(2,1)} %param.12) | copy-start | bytes 5505028
  68.8 18.8 %collective-permute-start.5 = (bf16[512,896]{1,0:T(8,128)(2,1)}, bf16[512,896]{1,0:T(8,128)(2,1)S(1)}, u32[]{:S(2)}, u32[]{:S(2)}) collective-permute-start(bf16[512,896]{1,0:T(8,128)(2,1)} %bitcast.10.refs_10_.refs_8_), channel_id=1, source_target_pairs={{0,6},{1,7},{2,0},{3,1},{4,2},{5,3},{6,4},{7,5},{8,14},{9,15},{10,... | collective-permute-start | bytes 2752520 | tf_op jit(solution)/shard_map/ppermute | solution.py:387
  71.3 19.3 %collective-permute-start.6 = (bf16[512,896]{1,0:T(8,128)(2,1)}, bf16[512,896]{1,0:T(8,128)(2,1)S(1)}, u32[]{:S(2)}, u32[]{:S(2)}) collective-permute-start(bf16[512,896]{1,0:T(8,128)(2,1)} %bitcast.10.refs_10_.refs_8_), channel_id=1, source_target_pairs={{0,2},{1,3},{2,4},{3,5},{4,6},{5,7},{6,0},{7,1},{8,10},{9,11},{10,... | collective-permute-start | bytes 2752520 | tf_op jit(solution)/shard_map/ppermute | solution.py:387
  75.6 24.8 %collective-permute-start.3 = (bf16[256,896]{1,0:T(8,128)(2,1)S(1)}, bf16[256,896]{1,0:T(8,128)(2,1)S(1)}, u32[]{:S(2)}, u32[]{:S(2)}) collective-permute-start(bf16[256,896]{1,0:T(8,128)(2,1)S(1)} %get-tuple-element.47), channel_id=1, source_target_pairs={{0,2},{1,3},{2,4},{3,5},{4,6},{5,7},{6,0},{7,1},{8,10},{9,11},{10,... | collective-permute-start | bytes 1376264 | tf_op jit(solution)/shard_map/ppermute | solution.py:387
  75.7 24.7 %collective-permute-start.4 = (bf16[256,896]{1,0:T(8,128)(2,1)S(1)}, bf16[256,896]{1,0:T(8,128)(2,1)S(1)}, u32[]{:S(2)}, u32[]{:S(2)}) collective-permute-start(bf16[256,896]{1,0:T(8,128)(2,1)S(1)} %get-tuple-element.48), channel_id=1, source_target_pairs={{0,6},{1,7},{2,0},{3,1},{4,2},{5,3},{6,4},{7,5},{8,14},{9,15},{10,... | collective-permute-start | bytes 1376264 | tf_op jit(solution)/shard_map/ppermute | solution.py:387
  91.2 19.0 %collective-permute-start.7 = (bf16[256,896]{1,0:T(8,128)(2,1)S(1)}, bf16[256,896]{1,0:T(8,128)(2,1)S(1)}, u32[]{:S(2)}, u32[]{:S(2)}) collective-permute-start(bf16[256,896]{1,0:T(8,128)(2,1)S(1)} %get-tuple-element.54), channel_id=1, source_target_pairs={{0,2},{1,3},{2,4},{3,5},{4,6},{5,7},{6,0},{7,1},{8,10},{9,11},{10,... | collective-permute-start | bytes 1376264 | tf_op jit(solution)/shard_map/ppermute | solution.py:387
  91.3 19.0 %collective-permute-start.8 = (bf16[256,896]{1,0:T(8,128)(2,1)S(1)}, bf16[256,896]{1,0:T(8,128)(2,1)S(1)}, u32[]{:S(2)}, u32[]{:S(2)}) collective-permute-start(bf16[256,896]{1,0:T(8,128)(2,1)S(1)} %get-tuple-element.55), channel_id=1, source_target_pairs={{0,6},{1,7},{2,0},{3,1},{4,2},{5,3},{6,4},{7,5},{8,14},{9,15},{10,... | collective-permute-start | bytes 1376264 | tf_op jit(solution)/shard_map/ppermute | solution.py:387
  111.3 9.3 %collective-permute-start.9 = (bf16[512,768]{1,0:T(8,128)(2,1)S(1)}, bf16[512,768]{1,0:T(8,128)(2,1)S(1)}, u32[]{:S(2)}, u32[]{:S(2)}) collective-permute-start(bf16[512,768]{1,0:T(8,128)(2,1)S(1)} %get-tuple-element.58), channel_id=1, source_target_pairs={{0,1},{1,0},{2,3},{3,2},{4,5},{5,4},{6,7},{7,6},{8,9},{9,8},{10,11... | collective-permute-start | bytes 2359304 | tf_op jit(solution)/shard_map/ppermute | solution.py:391
  122.1 15.9 %collective-permute-start.10 = (bf16[256,896]{1,0:T(8,128)(2,1)S(1)}, bf16[256,896]{1,0:T(8,128)(2,1)S(1)}, u32[]{:S(2)}, u32[]{:S(2)}) collective-permute-start(bf16[256,896]{1,0:T(8,128)(2,1)S(1)} %get-tuple-element.63), channel_id=1, source_target_pairs={{0,2},{1,3},{2,4},{3,5},{4,6},{5,7},{6,0},{7,1},{8,10},{9,11},{10,... | collective-permute-start | bytes 1376264 | tf_op jit(solution)/shard_map/ppermute | solution.py:387
  122.2 15.8 %collective-permute-start.11 = (bf16[256,896]{1,0:T(8,128)(2,1)S(1)}, bf16[256,896]{1,0:T(8,128)(2,1)S(1)}, u32[]{:S(2)}, u32[]{:S(2)}) collective-permute-start(bf16[256,896]{1,0:T(8,128)(2,1)S(1)} %get-tuple-element.64), channel_id=1, source_target_pairs={{0,6},{1,7},{2,0},{3,1},{4,2},{5,3},{6,4},{7,5},{8,14},{9,15},{10,... | collective-permute-start | bytes 1376264 | tf_op jit(solution)/shard_map/ppermute | solution.py:387
  127.3 27.1 %collective-permute-start.13 = (bf16[256,896]{1,0:T(8,128)(2,1)S(1)}, bf16[256,896]{1,0:T(8,128)(2,1)S(1)}, u32[]{:S(2)}, u32[]{:S(2)}) collective-permute-start(bf16[256,896]{1,0:T(8,128)(2,1)S(1)} %get-tuple-element.69), channel_id=1, source_target_pairs={{0,2},{1,3},{2,4},{3,5},{4,6},{5,7},{6,0},{7,1},{8,10},{9,11},{10,... | collective-permute-start | bytes 1376264 | tf_op jit(solution)/shard_map/ppermute | solution.py:387
  127.3 27.0 %collective-permute-start.14 = (bf16[256,896]{1,0:T(8,128)(2,1)S(1)}, bf16[256,896]{1,0:T(8,128)(2,1)S(1)}, u32[]{:S(2)}, u32[]{:S(2)}) collective-permute-start(bf16[256,896]{1,0:T(8,128)(2,1)S(1)} %get-tuple-element.70), channel_id=1, source_target_pairs={{0,6},{1,7},{2,0},{3,1},{4,2},{5,3},{6,4},{7,5},{8,14},{9,15},{10,... | collective-permute-start | bytes 1376264 | tf_op jit(solution)/shard_map/ppermute | solution.py:387
  138.8 16.0 %collective-permute-start.12 = (bf16[256,896]{1,0:T(8,128)(2,1)S(1)}, bf16[256,896]{1,0:T(8,128)(2,1)S(1)}, u32[]{:S(2)}, u32[]{:S(2)}) collective-permute-start(bf16[256,896]{1,0:T(8,128)(2,1)S(1)} %get-tuple-element.68), channel_id=1, source_target_pairs={{0,2},{1,3},{2,4},{3,5},{4,6},{5,7},{6,0},{7,1},{8,10},{9,11},{10,... | collective-permute-start | bytes 1376264 | tf_op jit(solution)/shard_map/ppermute | solution.py:387
  138.8 16.0 %collective-permute-start.15 = (bf16[256,896]{1,0:T(8,128)(2,1)S(1)}, bf16[256,896]{1,0:T(8,128)(2,1)S(1)}, u32[]{:S(2)}, u32[]{:S(2)}) collective-permute-start(bf16[256,896]{1,0:T(8,128)(2,1)S(1)} %get-tuple-element.71), channel_id=1, source_target_pairs={{0,6},{1,7},{2,0},{3,1},{4,2},{5,3},{6,4},{7,5},{8,14},{9,15},{10,... | collective-permute-start | bytes 1376264 | tf_op jit(solution)/shard_map/ppermute | solution.py:387
  156.5 16.3 %collective-permute-start.19 = (bf16[4,3,896,128]{3,2,1,0:T(8,128)(2,1)}, bf16[4,3,896,128]{3,2,1,0:T(8,128)(2,1)}, u32[]{:S(2)}, u32[]{:S(2)}) collective-permute-start(bf16[4,3,896,128]{3,2,1,0:T(8,128)(2,1)} %shard_map.123), channel_id=1, source_target_pairs={{0,1},{1,0},{2,3},{3,2},{4,5},{5,4},{6,7},{7,6},{8,9},{9,8},{10,11... | collective-permute-start | bytes 8257544 | tf_op jit(solution)/shard_map/ppermute | solution.py:391
  159.6 31.7 %all-to-all-start.3 = ((bf16[32,16,896]{2,1,0:T(8,128)(2,1)}), bf16[32,16,896]{2,1,0:T(8,128)(2,1)S(1)}, u32[]{:S(2)}, u32[]{:S(2)}) async-start(bf16[32,16,896]{2,1,0:T(8,128)(2,1)} %bitcast.14), calls=%async_computation.3 | async-start | bytes 1835008 | tf_op jit(solution)/shard_map/all_to_all | solution.py:442
  165.3 3.9 %collective-permute-start.16 = (f32[32,16]{1,0:T(8,128)S(1)}, f32[32,16]{1,0:T(8,128)S(1)}, u32[]{:S(2)}, u32[]{:S(2)}) collective-permute-start(f32[32,16]{1,0:T(8,128)S(1)} %bitcast.39), channel_id=1, source_target_pairs={{0,2},{1,3},{2,4},{3,5},{4,6},{5,7},{6,0},{7,1},{8,10},{9,11},{10,... | collective-permute-start | bytes 6152 | tf_op jit(solution)/shard_map/ppermute | solution.py:387
  165.3 4.2 %collective-permute-start.17 = (f32[32,16]{1,0:T(8,128)S(1)}, f32[32,16]{1,0:T(8,128)S(1)}, u32[]{:S(2)}, u32[]{:S(2)}) collective-permute-start(f32[32,16]{1,0:T(8,128)S(1)} %bitcast.40), channel_id=1, source_target_pairs={{0,4},{1,5},{2,6},{3,7},{4,0},{5,1},{6,2},{7,3},{8,12},{9,13},{10,... | collective-permute-start | bytes 6152 | tf_op jit(solution)/shard_map/ppermute | solution.py:387
  168.0 2.9 %collective-permute-start.18 = (f32[32,16]{1,0:T(8,128)S(1)}, f32[32,16]{1,0:T(8,128)S(1)}, u32[]{:S(2)}, u32[]{:S(2)}) collective-permute-start(f32[32,16]{1,0:T(8,128)S(1)} %bitcast.41), channel_id=1, source_target_pairs={{0,6},{1,7},{2,0},{3,1},{4,2},{5,3},{6,4},{7,5},{8,14},{9,15},{10,... | collective-permute-start | bytes 6152 | tf_op jit(solution)/shard_map/ppermute | solution.py:387
  (16 other events, 99.4 us)

commit v4 on v3

--- a/solution.py
+++ b/solution.py
@@ -211,9 +211,20 @@
                 keep[lo : lo + half, :] += value
 
 
+def split_body(at, left, right, out_a, out_b):
+    half = left.shape[0] // 2
+    out_a[...] = left[:half, :]
+    out_b[...] = right[half:, :]
+
+
+def turn_body(piece, at, own, right, left, gate, up, others, out_a, out_b, pre):
+    split_body(at, left, right, out_a, out_b)
+    add_body(piece, (0, 1, 3), True, True, at, gate, up, others, own, right, left, pre)
+
+
 def early_body(x_piece, dy_piece, at, gate, up, others, down, *refs):
-    x, dy, (pre, back) = refs[:5], refs[5:8], refs[8:]
-    add_body(x_piece, (0, 1, 3, 2), True, True, at, gate, up, others, *x, pre)
+    far, before, dy, (pre, back) = refs[:2], refs[2], refs[3:6], refs[6:]
+    add_body(x_piece, (2,), False, True, at, gate, up, others, *far, before, pre)
     add_body(dy_piece, (0, 1, 3), True, False, at, down, others, *dy, back)
 
 
@@ -391,26 +402,6 @@
     return lax.ppermute(value, "hidden", [(i, i ^ 1) for i in range(2 * CHIPS)])
 
 
-def split_body(at, left, right, out_a, out_b):
-    half = left.shape[0] // 2
-    out_a[...] = left[:half, :]
-    out_b[...] = right[half:, :]
-
-
-def ring_gather(at, own, after):
-    half = own.shape[0] // 2
-    left = to(own, 1)
-    right = to(own, -1)
-    pass_a, pass_b, token = call(
-        split_body,
-        (shape((half, own.shape[1]), BF),) * 2,
-        (at, left, right),
-        after=after,
-        token=True,
-    )
-    return (own, right, left, to(pass_a, 1), to(pass_b, -1)), (token,)
-
-
 def behind(value, token):
     return pl.pallas_call(
         lambda *refs: None,
@@ -459,21 +450,28 @@
         after=(token,),
     )
     arrived += [over_experts(message) for message in messages]
-    gathered = []
-    token = ()
-    for value in arrived:
-        parts, token = ring_gather(at, value, token)
-        gathered.append(parts)
     others = swap(halved)
     weights = (gate, up, others)
-
     (x_piece,), (dy_piece,) = of_tokens, of_cotangents
-    x, dy = gathered
+    part = (shape((half, block), BF),)
+
+    left, right = to(arrived[0], 1), to(arrived[0], -1)
+    pass_a, pass_b, pre, *token = call(
+        functools.partial(turn_body, x_piece),
+        part * 2 + (shape((rows, 2 * both), F32),),
+        (at, arrived[0], right, left, *weights),
+        token=True,
+    )
+    x = (arrived[0], right, left, to(pass_a, 1), to(pass_b, -1))
+    left, right = to(arrived[1], 1), to(arrived[1], -1)
+    pass_a, pass_b, *token = call(split_body, part * 2, (at, left, right), after=token, token=True)
+    dy = (arrived[1], right, left, to(pass_a, 1), to(pass_b, -1))
+
     narrow = shape((rows, both), F32)
     pre, back = call(
         functools.partial(early_body, x_piece, dy_piece),
         (shape((rows, 2 * both), F32), narrow),
-        (at, gate, up, others, down, *x, *dy[:3]),
+        (at, *weights, down, *x[3:], pre, *dy[:3]),
         after=token,
     )
     back, send = call(
@@ -483,7 +481,6 @@
     )
     recv = swap(send)
 
-    part = (shape((half, block), BF),)
     later = (shape((half, block), F32),)
     d, act_rows, sums, opp_a, opp_b = call(
         middle_body,
@@ -501,7 +498,7 @@
     keep, send, *token = call(
         grads_body,
         (shape((CHIPS, 3, block, units), BF),) * 2,
-        (at, d, act_rows, *[part for parts in gathered for part in parts]),
+        (at, d, act_rows, *x, *dy),
         after=token,
         token=True,
     )

time: 194 us -> 192 us (0.990)
  starting transfers between devices: 56.7 us -> 53.7 us
  Pallas kernels: 36.3 us -> 38.4 us
    ppermute x3, starting transfers between devices: 13 us -> 9.87 us  [swap(): return lax.ppermute(value, 'hidden', [(i, i ^ 1) for i in range(2 * CHIPS)])]
    unnamed x34 -> x30, local copies, waits for them, and re-layouts: 12.8 us -> 11.6 us
  transfers between devices with their start and end apart: 23 -> 23, of which waited for: 13 -> 11; matrix products, arithmetic and copies ran while one was open for 0% -> 0% of each run, Pallas kernels for 15% -> 16%
where the time goes in v4:
time: 192 us; the launch traced here: 191 us
  waiting for transfers between devices  72.5 us (38%)
  starting transfers between devices  53.7 us (28%)
  Pallas kernels  38.4 us (20%)
  blocking collectives  13.1 us (7%)
  local copies, waits for them, and re-layouts  12.6 us (7%)
    all_to_all x3, waiting for transfers between devices, over_experts(): lax.all_to_all(split, 'expert', split_axis=0, concat_axis=0, tiled=True)  44.8 us
    pallas_call x13, Pallas kernels, call(): pl.pallas_call(run, out_shape=out_shape + ((shape((8, 128), F32),) if tok...  27.8 us
    ppermute x17, waiting for transfers between devices, to(): lax.ppermute(value, 'hidden', [(i, (i + 2 * shift) % size) for i in range...  25.7 us
    all_to_all x3, starting transfers between devices, over_experts(): lax.all_to_all(split, 'expert', split_axis=0, concat_axis=0, tiled=True)  22.2 us
    ppermute x17, starting transfers between devices, to(): lax.ppermute(value, 'hidden', [(i, (i + 2 * shift) % size) for i in range...  21.6 us
    all_to_all x1, blocking collectives, over_experts(): lax.all_to_all(split, 'expert', split_axis=0, concat_axis=0, tiled=True)  13.1 us
    unnamed x30, local copies, waits for them, and re-layouts  11.6 us
    ppermute x3, starting transfers between devices, swap(): return lax.ppermute(value, 'hidden', [(i, i ^ 1) for i in range(2 * CHIPS)])  9.87 us
  transfers between devices with their start and end apart: 23, of which 11 were waited for; matrix products, arithmetic and copies ran while one was open for 0% of the time, Pallas kernels for 16%

profile of v4, /device:TPU:17, one launch (start us, length us, event | category | flops | bytes accessed | tf_op | source)
XLA Modules:
  0.0 191.3 jit_solution(9210945688871087158)
XLA Ops:
  5.2 11.1 %all-to-all-start = ((bf16[32,16,896]{2,1,0:T(8,128)(2,1)}), bf16[32,16,896]{2,1,0:T(8,128)(2,1)}, u32[]{:S(2)}, u32[]{:S(2)}) async-start(bf16[32,16,896]{2,1,0:T(8,128)(2,1)} %bitcast.7), calls=%async_computation | async-start | bytes 1835008 | tf_op jit(solution)/shard_map/all_to_all | solution.py:433
  19.3 2.8 %shard_map.111 = (bf16[4,3,896,128]{3,2,1,0:T(8,128)(2,1)}, f32[8,128]{1,0:T(8,128)S(1)}) custom-call(s32[2]{0:T(128)S(1)} %pad_add_fusion.refs_0_.at, bf16[7168,128]{1,0:T(8,128)(2,1)S(1)} %bitcast.21, bf16[7168,128]{1,0:T(8,128)(2,1)S(1)} %bitcast.26, bf16[128,7168]{1,0:T(8,128)(2,1)S(1)} %bitcast.31), custom_call_target="tpu_custom_call" | custom-call | bytes 11010048 | tf_op jit(solution)/shard_map/pallas_call | solution.py:146
  25.2 15.3 %all-to-all-done = bf16[32,16,896]{2,1,0:T(8,128)(2,1)} async-done(((bf16[32,16,896]{2,1,0:T(8,128)(2,1)}), bf16[32,16,896]{2,1,0:T(8,128)(2,1)}, u32[]{:S(2)}, u32[]{:S(2)}) %all-to-all-start) | async-done | bytes 917536 | tf_op jit(solution)/shard_map/all_to_all | solution.py:433
  40.4 5.5 %all-to-all-start.1 = ((bf16[32,16,896]{2,1,0:T(8,128)(2,1)}), bf16[32,16,896]{2,1,0:T(8,128)(2,1)}, u32[]{:S(2)}, u32[]{:S(2)}) async-start(bf16[32,16,896]{2,1,0:T(8,128)(2,1)} %bitcast.34), calls=%async_computation.1 | async-start | bytes 1835008 | tf_op jit(solution)/shard_map/all_to_all | solution.py:433
  46.0 2.6 %collective-permute-start.1 = (bf16[512,896]{1,0:T(8,128)(2,1)}, bf16[512,896]{1,0:T(8,128)(2,1)}, u32[]{:S(2)}, u32[]{:S(2)}) collective-permute-start(bf16[512,896]{1,0:T(8,128)(2,1)} %bitcast.8.refs_1_.refs_3_), channel_id=1, source_target_pairs={{0,6},{1,7},{2,0},{3,1},{4,2},{5,3},{6,4},{7,5},{8,14},{9,15},{10,... | collective-permute-start | bytes 2752520 | tf_op jit(solution)/shard_map/ppermute | solution.py:398
  48.6 20.3 %all-to-all-done.1 = bf16[32,16,896]{2,1,0:T(8,128)(2,1)} async-done(((bf16[32,16,896]{2,1,0:T(8,128)(2,1)}), bf16[32,16,896]{2,1,0:T(8,128)(2,1)}, u32[]{:S(2)}, u32[]{:S(2)}) %all-to-all-start.1) | async-done | bytes 917536 | tf_op jit(solution)/shard_map/all_to_all | solution.py:433
  74.4 3.7 %shard_map.112 = (bf16[256,896]{1,0:T(8,128)(2,1)S(1)}, bf16[256,896]{1,0:T(8,128)(2,1)S(1)}, f32[512,512]{1,0:T(8,128)S(1)}, f32[8,128]{1,0:T(8,128)S(1)}) custom-call(s32[2]{0:T(128)S(1)} %pad_add_fusion.refs_0_.at, bf16[512,896]{1,0:T(8,128)(2,1)} %bitcast.8.refs_1_.refs_3_, bf16[512,896]{1,0:T(8,128)(2,1)} %collective-permute-done.1.refs_2_.refs_4_, ...), custom_call_target="tpu_custom_call" | custom-call | bytes 11141120 | tf_op jit(solution)/shard_map/pallas_call | solution.py:42
  78.4 2.6 %collective-permute-start.4 = (bf16[256,896]{1,0:T(8,128)(2,1)S(1)}, bf16[256,896]{1,0:T(8,128)(2,1)S(1)}, u32[]{:S(2)}, u32[]{:S(2)}) collective-permute-start(bf16[256,896]{1,0:T(8,128)(2,1)S(1)} %get-tuple-element.49), channel_id=1, source_target_pairs={{0,6},{1,7},{2,0},{3,1},{4,2},{5,3},{6,4},{7,5},{8,14},{9,15},{10,... | collective-permute-start | bytes 1376264 | tf_op jit(solution)/shard_map/ppermute | solution.py:398
  81.0 6.7 %collective-permute-done.5.refs_2_.refs_9_ = bf16[512,896]{1,0:T(8,128)(2,1)S(1)} collective-permute-done((bf16[512,896]{1,0:T(8,128)(2,1)}, bf16[512,896]{1,0:T(8,128)(2,1)S(1)}, u32[]{:S(2)}, u32[]{:S(2)}) %collective-permute-start.5) | collective-permute-done | bytes 917536 | tf_op jit(solution)/shard_map/ppermute | solution.py:398
  87.6 3.0 %collective-permute-done.6.refs_1_.refs_10_ = bf16[512,896]{1,0:T(8,128)(2,1)S(1)} collective-permute-done((bf16[512,896]{1,0:T(8,128)(2,1)}, bf16[512,896]{1,0:T(8,128)(2,1)S(1)}, u32[]{:S(2)}, u32[]{:S(2)}) %collective-permute-start.6) | collective-permute-done | bytes 917536 | tf_op jit(solution)/shard_map/ppermute | solution.py:398
  91.4 2.7 %collective-permute-start.8 = (bf16[256,896]{1,0:T(8,128)(2,1)S(1)}, bf16[256,896]{1,0:T(8,128)(2,1)S(1)}, u32[]{:S(2)}, u32[]{:S(2)}) collective-permute-start(bf16[256,896]{1,0:T(8,128)(2,1)S(1)} %get-tuple-element.57), channel_id=1, source_target_pairs={{0,6},{1,7},{2,0},{3,1},{4,2},{5,3},{6,4},{7,5},{8,14},{9,15},{10,... | collective-permute-start | bytes 1376264 | tf_op jit(solution)/shard_map/ppermute | solution.py:398
  94.0 6.5 %collective-permute-done.3.refs_5_.refs_6_ = bf16[256,896]{1,0:T(8,128)(2,1)S(1)} collective-permute-done((bf16[256,896]{1,0:T(8,128)(2,1)S(1)}, bf16[256,896]{1,0:T(8,128)(2,1)S(1)}, u32[]{:S(2)}, u32[]{:S(2)}) %collective-permute-start.3) | collective-permute-done | bytes 458784 | tf_op jit(solution)/shard_map/ppermute | solution.py:398
  100.5 2.7 %shard_map.115 = (f32[512,512]{1,0:T(8,128)S(1)}, f32[512,256]{1,0:T(8,128)S(1)}) custom-call(s32[2]{0:T(128)S(1)} %pad_add_fusion.refs_0_.at, bf16[7168,128]{1,0:T(8,128)(2,1)S(1)} %bitcast.23, bf16[7168,128]{1,0:T(8,128)(2,1)S(1)} %bitcast.28, bf16[4,3,896,128]{3,2,1,0:T(8,128)(2,1)S(1)} %collective-permute-done.refs_6_.refs_3_.refs_2_.refs_4_, ...), custom_call_target="tpu_custom_call" | custom-call | bytes 14548992 | tf_op jit(solution)/shard_map/pallas_call | solution.py:42
  103.3 7.1 %collective-permute-done.7.refs_3_.refs_11_ = bf16[256,896]{1,0:T(8,128)(2,1)S(1)} collective-permute-done((bf16[256,896]{1,0:T(8,128)(2,1)S(1)}, bf16[256,896]{1,0:T(8,128)(2,1)S(1)}, u32[]{:S(2)}, u32[]{:S(2)}) %collective-permute-start.7) | collective-permute-done | bytes 458784 | tf_op jit(solution)/shard_map/ppermute | solution.py:398
  111.4 5.1 %collective-permute-start.9 = (bf16[512,768]{1,0:T(8,128)(2,1)S(1)}, bf16[512,768]{1,0:T(8,128)(2,1)S(1)}, u32[]{:S(2)}, u32[]{:S(2)}) collective-permute-start(bf16[512,768]{1,0:T(8,128)(2,1)S(1)} %get-tuple-element.60), channel_id=1, source_target_pairs={{0,1},{1,0},{2,3},{3,2},{4,5},{5,4},{6,7},{7,6},{8,9},{9,8},{10,11... | collective-permute-start | bytes 2359304 | tf_op jit(solution)/shard_map/ppermute | solution.py:402
  120.0 2.7 %collective-permute-start.11 = (bf16[256,896]{1,0:T(8,128)(2,1)S(1)}, bf16[256,896]{1,0:T(8,128)(2,1)S(1)}, u32[]{:S(2)}, u32[]{:S(2)}) collective-permute-start(bf16[256,896]{1,0:T(8,128)(2,1)S(1)} %get-tuple-element.66), channel_id=1, source_target_pairs={{0,6},{1,7},{2,0},{3,1},{4,2},{5,3},{6,4},{7,5},{8,14},{9,15},{10,... | collective-permute-start | bytes 1376264 | tf_op jit(solution)/shard_map/ppermute | solution.py:398
  125.2 2.7 %collective-permute-start.14 = (bf16[256,896]{1,0:T(8,128)(2,1)S(1)}, bf16[256,896]{1,0:T(8,128)(2,1)S(1)}, u32[]{:S(2)}, u32[]{:S(2)}) collective-permute-start(bf16[256,896]{1,0:T(8,128)(2,1)S(1)} %get-tuple-element.72), channel_id=1, source_target_pairs={{0,6},{1,7},{2,0},{3,1},{4,2},{5,3},{6,4},{7,5},{8,14},{9,15},{10,... | collective-permute-start | bytes 1376264 | tf_op jit(solution)/shard_map/ppermute | solution.py:398
  127.9 6.8 %shard_map.119 = (bf16[4,3,896,128]{3,2,1,0:T(8,128)(2,1)S(1)}, bf16[4,3,896,128]{3,2,1,0:T(8,128)(2,1)}, f32[8,128]{1,0:T(8,128)S(1)}) custom-call(s32[2]{0:T(128)S(1)} %pad_add_fusion.refs_0_.at, bf16[512,512]{1,0:T(8,128)(2,1)S(1)} %get-tuple-element.61.refs_1_, bf16[512,256]{1,0:T(8,128)(2,1)S(1)} %get-tuple-element.67.refs_2_, ...), custom_call_target="tpu_custom_call" | custom-call | bytes 13631488 | tf_op jit(solution)/shard_map/pallas_call | solution.py:42
  137.0 2.7 %collective-permute-start.15 = (bf16[256,896]{1,0:T(8,128)(2,1)S(1)}, bf16[256,896]{1,0:T(8,128)(2,1)S(1)}, u32[]{:S(2)}, u32[]{:S(2)}) collective-permute-start(bf16[256,896]{1,0:T(8,128)(2,1)S(1)} %get-tuple-element.73), channel_id=1, source_target_pairs={{0,6},{1,7},{2,0},{3,1},{4,2},{5,3},{6,4},{7,5},{8,14},{9,15},{10,... | collective-permute-start | bytes 1376264 | tf_op jit(solution)/shard_map/ppermute | solution.py:398
  139.7 13.1 %all_to_all.20 = f32[32,1,16]{2,1,0:T(1,128)S(1)} all-to-all(f32[32,1,16]{2,1,0:T(1,128)S(1)} %bitcast.43), channel_id=1, replica_groups=mesh['expert'=32,'hidden'=8] {'expert'}, dimensions={0} | all-to-all | bytes 4096 | tf_op jit(solution)/shard_map/all_to_all | solution.py:433
  154.6 3.5 %collective-permute-start.19 = (bf16[4,3,896,128]{3,2,1,0:T(8,128)(2,1)}, bf16[4,3,896,128]{3,2,1,0:T(8,128)(2,1)}, u32[]{:S(2)}, u32[]{:S(2)}) collective-permute-start(bf16[4,3,896,128]{3,2,1,0:T(8,128)(2,1)} %shard_map.123), channel_id=1, source_target_pairs={{0,1},{1,0},{2,3},{3,2},{4,5},{5,4},{6,7},{7,6},{8,9},{9,8},{10,11... | collective-permute-start | bytes 8257544 | tf_op jit(solution)/shard_map/ppermute | solution.py:402
  158.1 5.6 %all-to-all-start.3 = ((bf16[32,16,896]{2,1,0:T(8,128)(2,1)}), bf16[32,16,896]{2,1,0:T(8,128)(2,1)S(1)}, u32[]{:S(2)}, u32[]{:S(2)}) async-start(bf16[32,16,896]{2,1,0:T(8,128)(2,1)} %bitcast.14), calls=%async_computation.3 | async-start | bytes 1835008 | tf_op jit(solution)/shard_map/all_to_all | solution.py:433
  172.7 7.9 %shard_map.124 = (bf16[7168,128]{1,0:T(8,128)(2,1)}, bf16[7168,128]{1,0:T(8,128)(2,1)}, bf16[128,7168]{1,0:T(8,128)(2,1)}, f32[8,128]{1,0:T(8,128)S(1)}) custom-call(s32[2]{0:T(128)S(1)} %pad_add_fusion.refs_0_.at, bf16[4,3,896,128]{3,2,1,0:T(8,128)(2,1)S(1)} %copy-done.10, bf16[4,3,896,128]{3,2,1,0:T(8,128)(2,1)} %collective-permute-done.19.recv), custom_call_target="tpu_custom_call" | custom-call | bytes 11010048 | tf_op jit(solution)/shard_map/pallas_call | solution.py:349
  180.6 9.2 %all-to-all-done.3 = bf16[32,16,896]{2,1,0:T(8,128)(2,1)S(1)} async-done(((bf16[32,16,896]{2,1,0:T(8,128)(2,1)}), bf16[32,16,896]{2,1,0:T(8,128)(2,1)S(1)}, u32[]{:S(2)}, u32[]{:S(2)}) %all-to-all-start.3) | async-done | bytes 917536 | tf_op jit(solution)/shard_map/all_to_all | solution.py:433
  (71 shorter events, 38.7 us)
Async XLA Ops:
  5.2 35.2 %all-to-all-start = ((bf16[32,16,896]{2,1,0:T(8,128)(2,1)}), bf16[32,16,896]{2,1,0:T(8,128)(2,1)}, u32[]{:S(2)}, u32[]{:S(2)}) async-start(bf16[32,16,896]{2,1,0:T(8,128)(2,1)} %bitcast.7), calls=%async_computation | async-start | bytes 1835008 | tf_op jit(solution)/shard_map/all_to_all | solution.py:433
  22.1 49.3 %collective-permute-start = (bf16[4,3,896,128]{3,2,1,0:T(8,128)(2,1)}, bf16[4,3,896,128]{3,2,1,0:T(8,128)(2,1)S(1)}, u32[]{:S(2)}, u32[]{:S(2)}) collective-permute-start(bf16[4,3,896,128]{3,2,1,0:T(8,128)(2,1)} %get-tuple-element.46), channel_id=1, source_target_pairs={{0,1},{1,0},{2,3},{3,2},{4,5},{5,4},{6,7},{7,6},{8,9},{9,8},{10,11... | collective-permute-start | bytes 8257544 | tf_op jit(solution)/shard_map/ppermute | solution.py:402
  40.4 28.4 %all-to-all-start.1 = ((bf16[32,16,896]{2,1,0:T(8,128)(2,1)}), bf16[32,16,896]{2,1,0:T(8,128)(2,1)}, u32[]{:S(2)}, u32[]{:S(2)}) async-start(bf16[32,16,896]{2,1,0:T(8,128)(2,1)} %bitcast.34), calls=%async_computation.1 | async-start | bytes 1835008 | tf_op jit(solution)/shard_map/all_to_all | solution.py:433
  46.0 25.4 %collective-permute-start.1 = (bf16[512,896]{1,0:T(8,128)(2,1)}, bf16[512,896]{1,0:T(8,128)(2,1)}, u32[]{:S(2)}, u32[]{:S(2)}) collective-permute-start(bf16[512,896]{1,0:T(8,128)(2,1)} %bitcast.8.refs_1_.refs_3_), channel_id=1, source_target_pairs={{0,6},{1,7},{2,0},{3,1},{4,2},{5,3},{6,4},{7,5},{8,14},{9,15},{10,... | collective-permute-start | bytes 2752520 | tf_op jit(solution)/shard_map/ppermute | solution.py:398
  48.6 22.8 %collective-permute-start.2 = (bf16[512,896]{1,0:T(8,128)(2,1)}, bf16[512,896]{1,0:T(8,128)(2,1)}, u32[]{:S(2)}, u32[]{:S(2)}) collective-permute-start(bf16[512,896]{1,0:T(8,128)(2,1)} %bitcast.8.refs_1_.refs_3_), channel_id=1, source_target_pairs={{0,2},{1,3},{2,4},{3,5},{4,6},{5,7},{6,0},{7,1},{8,10},{9,11},{10,... | collective-permute-start | bytes 2752520 | tf_op jit(solution)/shard_map/ppermute | solution.py:398
  68.9 18.8 %collective-permute-start.5 = (bf16[512,896]{1,0:T(8,128)(2,1)}, bf16[512,896]{1,0:T(8,128)(2,1)S(1)}, u32[]{:S(2)}, u32[]{:S(2)}) collective-permute-start(bf16[512,896]{1,0:T(8,128)(2,1)} %bitcast.10.refs_8_), channel_id=1, source_target_pairs={{0,6},{1,7},{2,0},{3,1},{4,2},{5,3},{6,4},{7,5},{8,14},{9,15},{10,... | collective-permute-start | bytes 2752520 | tf_op jit(solution)/shard_map/ppermute | solution.py:398
  71.3 19.3 %collective-permute-start.6 = (bf16[512,896]{1,0:T(8,128)(2,1)}, bf16[512,896]{1,0:T(8,128)(2,1)S(1)}, u32[]{:S(2)}, u32[]{:S(2)}) collective-permute-start(bf16[512,896]{1,0:T(8,128)(2,1)} %bitcast.10.refs_8_), channel_id=1, source_target_pairs={{0,2},{1,3},{2,4},{3,5},{4,6},{5,7},{6,0},{7,1},{8,10},{9,11},{10,... | collective-permute-start | bytes 2752520 | tf_op jit(solution)/shard_map/ppermute | solution.py:398
  74.4 26.1 %copy-start.7 = (bf16[1,128,7168]{2,1,0:T(8,128)(2,1)S(1)}, bf16[1,128,7168]{2,1,0:T(8,128)(2,1)}, u32[]{:S(2)}) copy-start(bf16[1,128,7168]{2,1,0:T(8,128)(2,1)} %param.13) | copy-start | bytes 5505028
  78.1 22.3 %collective-permute-start.3 = (bf16[256,896]{1,0:T(8,128)(2,1)S(1)}, bf16[256,896]{1,0:T(8,128)(2,1)S(1)}, u32[]{:S(2)}, u32[]{:S(2)}) collective-permute-start(bf16[256,896]{1,0:T(8,128)(2,1)S(1)} %get-tuple-element.48), channel_id=1, source_target_pairs={{0,2},{1,3},{2,4},{3,5},{4,6},{5,7},{6,0},{7,1},{8,10},{9,11},{10,... | collective-permute-start | bytes 1376264 | tf_op jit(solution)/shard_map/ppermute | solution.py:398
  78.4 22.1 %collective-permute-start.4 = (bf16[256,896]{1,0:T(8,128)(2,1)S(1)}, bf16[256,896]{1,0:T(8,128)(2,1)S(1)}, u32[]{:S(2)}, u32[]{:S(2)}) collective-permute-start(bf16[256,896]{1,0:T(8,128)(2,1)S(1)} %get-tuple-element.49), channel_id=1, source_target_pairs={{0,6},{1,7},{2,0},{3,1},{4,2},{5,3},{6,4},{7,5},{8,14},{9,15},{10,... | collective-permute-start | bytes 1376264 | tf_op jit(solution)/shard_map/ppermute | solution.py:398
  91.3 19.0 %collective-permute-start.7 = (bf16[256,896]{1,0:T(8,128)(2,1)S(1)}, bf16[256,896]{1,0:T(8,128)(2,1)S(1)}, u32[]{:S(2)}, u32[]{:S(2)}) collective-permute-start(bf16[256,896]{1,0:T(8,128)(2,1)S(1)} %get-tuple-element.56), channel_id=1, source_target_pairs={{0,2},{1,3},{2,4},{3,5},{4,6},{5,7},{6,0},{7,1},{8,10},{9,11},{10,... | collective-permute-start | bytes 1376264 | tf_op jit(solution)/shard_map/ppermute | solution.py:398
  91.4 19.0 %collective-permute-start.8 = (bf16[256,896]{1,0:T(8,128)(2,1)S(1)}, bf16[256,896]{1,0:T(8,128)(2,1)S(1)}, u32[]{:S(2)}, u32[]{:S(2)}) collective-permute-start(bf16[256,896]{1,0:T(8,128)(2,1)S(1)} %get-tuple-element.57), channel_id=1, source_target_pairs={{0,6},{1,7},{2,0},{3,1},{4,2},{5,3},{6,4},{7,5},{8,14},{9,15},{10,... | collective-permute-start | bytes 1376264 | tf_op jit(solution)/shard_map/ppermute | solution.py:398
  111.4 7.1 %collective-permute-start.9 = (bf16[512,768]{1,0:T(8,128)(2,1)S(1)}, bf16[512,768]{1,0:T(8,128)(2,1)S(1)}, u32[]{:S(2)}, u32[]{:S(2)}) collective-permute-start(bf16[512,768]{1,0:T(8,128)(2,1)S(1)} %get-tuple-element.60), channel_id=1, source_target_pairs={{0,1},{1,0},{2,3},{3,2},{4,5},{5,4},{6,7},{7,6},{8,9},{9,8},{10,11... | collective-permute-start | bytes 2359304 | tf_op jit(solution)/shard_map/ppermute | solution.py:402
  119.9 16.3 %collective-permute-start.10 = (bf16[256,896]{1,0:T(8,128)(2,1)S(1)}, bf16[256,896]{1,0:T(8,128)(2,1)S(1)}, u32[]{:S(2)}, u32[]{:S(2)}) collective-permute-start(bf16[256,896]{1,0:T(8,128)(2,1)S(1)} %get-tuple-element.65), channel_id=1, source_target_pairs={{0,2},{1,3},{2,4},{3,5},{4,6},{5,7},{6,0},{7,1},{8,10},{9,11},{10,... | collective-permute-start | bytes 1376264 | tf_op jit(solution)/shard_map/ppermute | solution.py:398
  120.0 16.2 %collective-permute-start.11 = (bf16[256,896]{1,0:T(8,128)(2,1)S(1)}, bf16[256,896]{1,0:T(8,128)(2,1)S(1)}, u32[]{:S(2)}, u32[]{:S(2)}) collective-permute-start(bf16[256,896]{1,0:T(8,128)(2,1)S(1)} %get-tuple-element.66), channel_id=1, source_target_pairs={{0,6},{1,7},{2,0},{3,1},{4,2},{5,3},{6,4},{7,5},{8,14},{9,15},{10,... | collective-permute-start | bytes 1376264 | tf_op jit(solution)/shard_map/ppermute | solution.py:398
  125.1 27.6 %collective-permute-start.13 = (bf16[256,896]{1,0:T(8,128)(2,1)S(1)}, bf16[256,896]{1,0:T(8,128)(2,1)S(1)}, u32[]{:S(2)}, u32[]{:S(2)}) collective-permute-start(bf16[256,896]{1,0:T(8,128)(2,1)S(1)} %get-tuple-element.71), channel_id=1, source_target_pairs={{0,2},{1,3},{2,4},{3,5},{4,6},{5,7},{6,0},{7,1},{8,10},{9,11},{10,... | collective-permute-start | bytes 1376264 | tf_op jit(solution)/shard_map/ppermute | solution.py:398
  125.2 27.6 %collective-permute-start.14 = (bf16[256,896]{1,0:T(8,128)(2,1)S(1)}, bf16[256,896]{1,0:T(8,128)(2,1)S(1)}, u32[]{:S(2)}, u32[]{:S(2)}) collective-permute-start(bf16[256,896]{1,0:T(8,128)(2,1)S(1)} %get-tuple-element.72), channel_id=1, source_target_pairs={{0,6},{1,7},{2,0},{3,1},{4,2},{5,3},{6,4},{7,5},{8,14},{9,15},{10,... | collective-permute-start | bytes 1376264 | tf_op jit(solution)/shard_map/ppermute | solution.py:398
  136.9 15.9 %collective-permute-start.12 = (bf16[256,896]{1,0:T(8,128)(2,1)S(1)}, bf16[256,896]{1,0:T(8,128)(2,1)S(1)}, u32[]{:S(2)}, u32[]{:S(2)}) collective-permute-start(bf16[256,896]{1,0:T(8,128)(2,1)S(1)} %get-tuple-element.70), channel_id=1, source_target_pairs={{0,2},{1,3},{2,4},{3,5},{4,6},{5,7},{6,0},{7,1},{8,10},{9,11},{10,... | collective-permute-start | bytes 1376264 | tf_op jit(solution)/shard_map/ppermute | solution.py:398
  137.0 15.8 %collective-permute-start.15 = (bf16[256,896]{1,0:T(8,128)(2,1)S(1)}, bf16[256,896]{1,0:T(8,128)(2,1)S(1)}, u32[]{:S(2)}, u32[]{:S(2)}) collective-permute-start(bf16[256,896]{1,0:T(8,128)(2,1)S(1)} %get-tuple-element.73), channel_id=1, source_target_pairs={{0,6},{1,7},{2,0},{3,1},{4,2},{5,3},{6,4},{7,5},{8,14},{9,15},{10,... | collective-permute-start | bytes 1376264 | tf_op jit(solution)/shard_map/ppermute | solution.py:398
  154.6 16.4 %collective-permute-start.19 = (bf16[4,3,896,128]{3,2,1,0:T(8,128)(2,1)}, bf16[4,3,896,128]{3,2,1,0:T(8,128)(2,1)}, u32[]{:S(2)}, u32[]{:S(2)}) collective-permute-start(bf16[4,3,896,128]{3,2,1,0:T(8,128)(2,1)} %shard_map.123), channel_id=1, source_target_pairs={{0,1},{1,0},{2,3},{3,2},{4,5},{5,4},{6,7},{7,6},{8,9},{9,8},{10,11... | collective-permute-start | bytes 8257544 | tf_op jit(solution)/shard_map/ppermute | solution.py:402
  158.1 31.7 %all-to-all-start.3 = ((bf16[32,16,896]{2,1,0:T(8,128)(2,1)}), bf16[32,16,896]{2,1,0:T(8,128)(2,1)S(1)}, u32[]{:S(2)}, u32[]{:S(2)}) async-start(bf16[32,16,896]{2,1,0:T(8,128)(2,1)} %bitcast.14), calls=%async_computation.3 | async-start | bytes 1835008 | tf_op jit(solution)/shard_map/all_to_all | solution.py:433
  163.7 3.9 %collective-permute-start.16 = (f32[32,16]{1,0:T(8,128)S(1)}, f32[32,16]{1,0:T(8,128)S(1)}, u32[]{:S(2)}, u32[]{:S(2)}) collective-permute-start(f32[32,16]{1,0:T(8,128)S(1)} %bitcast.37), channel_id=1, source_target_pairs={{0,2},{1,3},{2,4},{3,5},{4,6},{5,7},{6,0},{7,1},{8,10},{9,11},{10,... | collective-permute-start | bytes 6152 | tf_op jit(solution)/shard_map/ppermute | solution.py:398
  163.8 4.2 %collective-permute-start.17 = (f32[32,16]{1,0:T(8,128)S(1)}, f32[32,16]{1,0:T(8,128)S(1)}, u32[]{:S(2)}, u32[]{:S(2)}) collective-permute-start(f32[32,16]{1,0:T(8,128)S(1)} %bitcast.38), channel_id=1, source_target_pairs={{0,4},{1,5},{2,6},{3,7},{4,0},{5,1},{6,2},{7,3},{8,12},{9,13},{10,... | collective-permute-start | bytes 6152 | tf_op jit(solution)/shard_map/ppermute | solution.py:398
  166.1 2.9 %collective-permute-start.18 = (f32[32,16]{1,0:T(8,128)S(1)}, f32[32,16]{1,0:T(8,128)S(1)}, u32[]{:S(2)}, u32[]{:S(2)}) collective-permute-start(f32[32,16]{1,0:T(8,128)S(1)} %bitcast.39), channel_id=1, source_target_pairs={{0,6},{1,7},{2,0},{3,1},{4,2},{5,3},{6,4},{7,5},{8,14},{9,15},{10,... | collective-permute-start | bytes 6152 | tf_op jit(solution)/shard_map/ppermute | solution.py:398
  (14 other events, 104.5 us)

commit v5 on v4

--- a/solution.py
+++ b/solution.py
@@ -59,27 +59,6 @@
 ANY = pl.BlockSpec(memory_space=pl.ANY)
 
 
-CUTS = (7, 14)
-
-
-def plan(block):
-    pieces = ([], [])
-    start = 0
-    for message, cut in enumerate(CUTS):
-        end = 2 * block * cut // 14
-        for kind in (0, 1):
-            lo, hi = max(start, kind * block), min(end, (kind + 1) * block)
-            if lo < hi:
-                pieces[kind].append((message, lo - start, lo - kind * block, hi - lo))
-        start = end
-    return pieces
-
-
-def widths(block):
-    ends = [0] + [2 * block * cut // 14 for cut in CUTS]
-    return [hi - lo for lo, hi in zip(ends, ends[1:])]
-
-
 def owner_of(rows, experts):
     row = lax.broadcasted_iota(jnp.int32, (rows, experts), 0) // CAP
     return (row == lax.broadcasted_iota(jnp.int32, (rows, experts), 1)).astype(F32)
@@ -90,15 +69,12 @@
     return row == lax.broadcasted_iota(jnp.int32, (rows, count), 1)
 
 
-def select_rows(routes, gates, rows, experts):
+def select_rows(routes, rows, experts):
     topk, count = routes.shape
     expert = lax.broadcasted_iota(jnp.int32, (experts, count), 0)
     named = jnp.zeros((experts, count), F32)
-    weight = jnp.zeros((experts, count), F32)
     for k in range(topk):
-        hit = routes[k : k + 1, :] == expert
-        named = jnp.where(hit, 1.0, named)
-        weight = jnp.where(hit, gates[k : k + 1, :].astype(F32), weight)
+        named = jnp.where(routes[k : k + 1, :] == expert, 1.0, named)
     earlier = (
         lax.broadcasted_iota(jnp.int32, (count, count), 0) < lax.broadcasted_iota(jnp.int32, (count, count), 1)
     ).astype(F32)
@@ -106,26 +82,30 @@
     slot = jnp.where(named > 0, slot, 2.0 * CAP)
     owner = owner_of(rows, experts).astype(BF)
     slot_of = mm(owner, slot.astype(BF), NN)
-    weight_of = mm(owner, weight.astype(BF), NN)
     place = (lax.broadcasted_iota(jnp.int32, (rows, count), 0) % CAP).astype(F32)
-    pick = jnp.where(slot_of == place, 1.0, 0.0)
-    return pick, pick * weight_of
-
-
-def first_body(experts, at, routes, gates, x, out, pick_out, weigh_out):
-    pick, weighted = select_rows(routes[...], gates[...], pick_out.shape[0], experts)
-    pick = pick.astype(BF)
+    return jnp.where(slot_of == place, 1.0, 0.0)
+
+
+def weigh_rows(pick, routes, gates):
+    topk, count = routes.shape
+    rows = pick.shape[0]
+    experts = rows // CAP
+    expert = lax.broadcasted_iota(jnp.int32, (experts, count), 0)
+    weight = jnp.zeros((experts, count), F32)
+    for k in range(topk):
+        weight = jnp.where(routes[k : k + 1, :] == expert, gates[k : k + 1, :].astype(F32), weight)
+    return pick.astype(F32) * mm(owner_of(rows, experts).astype(BF), weight.astype(BF), NN)
+
+
+def first_body(experts, at, routes, x, out, pick_out):
+    pick = select_rows(routes[...], pick_out.shape[0], experts).astype(BF)
     pick_out[...] = pick
-    weigh_out[...] = weighted.astype(BF)
-    out[...] = mm(pick, x[:, : out.shape[1]], NN).astype(BF)
-
-
-def rest_body(at, pick, weighted, x, dy, *outs):
-    for chosen, source, pieces in zip((pick, weighted), (x, dy), plan(x.shape[1])):
-        for message, column, feature, many in pieces:
-            if message > 0:
-                value = mm(chosen[...], source[:, feature : feature + many], NN)
-                outs[message - 1][:, column : column + many] = value.astype(BF)
+    out[...] = mm(pick, x[...], NN).astype(BF)
+
+
+def rest_body(at, pick, routes, gates, dy, out):
+    weighted = weigh_rows(pick[...], routes[...], gates[...]).astype(BF)
+    out[...] = mm(weighted, dy[...], NN).astype(BF)
 
 
 def halves_body(at, gate, up, down, out, token):
@@ -178,11 +158,11 @@
     return jnp.concatenate([down[:, mine], jnp.concatenate(other, axis=1)], axis=0)
 
 
-def halves_of(parts, r, half, columns):
+def halves_of(parts, r, half):
     if r == 2:
-        return ((0, parts[3][:, columns]), (half, parts[4][:, columns]))
+        return ((0, parts[3][...]), (half, parts[4][...]))
     ref = parts[{0: 0, 1: 1, 3: 2}[r]]
-    return ((0, ref[:half, columns]), (half, ref[half:, columns]))
+    return ((0, ref[:half, :]), (half, ref[half:, :]))
 
 
 def swapped(value, units):
@@ -190,9 +170,7 @@
     return jnp.concatenate([pieces[i ^ 1] for i in range(len(pieces))], axis=1).astype(BF)
 
 
-def add_body(piece, which, first, pre, at, *refs):
-    _, column, feature, many = piece
-    columns = slice(column, column + many)
+def add_body(which, first, pre, at, *refs):
     weights, refs = (refs[:3], refs[3:]) if pre else (refs[:2], refs[2:])
     given = 3 * (which[0] == 0) + 2 * (2 in which)
     parts, refs = refs[:given], refs[given:]
@@ -201,9 +179,9 @@
     keep = refs[0]
     half = keep.shape[0] // 2
     for r in which:
-        cut = (feature, feature + many)
-        block = pre_weights(at, *weights, r, *cut) if pre else down_weights(at, *weights, r, *cut)
-        for lo, part in halves_of(parts, r, half, columns):
+        width = weights[-1].shape[2]
+        block = pre_weights(at, *weights, r, 0, width) if pre else down_weights(at, *weights, r, 0, width)
+        for lo, part in halves_of(parts, r, half):
             value = mm(part, block, NN if pre else NT)
             if r == which[0]:
                 keep[lo : lo + half, :] = value if first else before[lo : lo + half, :] + value
@@ -217,33 +195,30 @@
     out_b[...] = right[half:, :]
 
 
-def turn_body(piece, at, own, right, left, gate, up, others, out_a, out_b, pre):
+def turn_body(at, own, right, left, gate, up, others, out_a, out_b, pre):
     split_body(at, left, right, out_a, out_b)
-    add_body(piece, (0, 1, 3), True, True, at, gate, up, others, own, right, left, pre)
-
-
-def early_body(x_piece, dy_piece, at, gate, up, others, down, *refs):
-    far, before, dy, (pre, back) = refs[:2], refs[2], refs[3:6], refs[6:]
-    add_body(x_piece, (2,), False, True, at, gate, up, others, *far, before, pre)
-    add_body(dy_piece, (0, 1, 3), True, False, at, down, others, *dy, back)
-
-
-def late_body(dy_piece, at, down, others, opp_a, opp_b, before, pre, back, send):
-    add_body(dy_piece, (2,), False, False, at, down, others, opp_a, opp_b, before, back)
+    add_body((0, 1, 3), True, True, at, gate, up, others, own, right, left, pre)
+
+
+def early_body(at, gate, up, others, down, *refs):
+    far, before, dy, (pre, back, pre_send) = refs[:2], refs[2], refs[3:6], refs[6:]
+    add_body((2,), False, True, at, gate, up, others, *far, before, pre)
+    pre_send[...] = swapped(pre[...], down.shape[0])
+    add_body((0, 1, 3), True, False, at, down, others, *dy, back)
+
+
+def late_body(at, down, others, opp_a, opp_b, before, pre_send, back, send):
+    add_body((2,), False, False, at, down, others, opp_a, opp_b, before, back)
     units = down.shape[0]
-    send[:, : 4 * units] = swapped(pre[...], units)
+    send[:, : 4 * units] = pre_send[...]
     send[:, 4 * units :] = swapped(back[...], units)
 
 
-def middle_body(at, pre, back, recv, gate, up, others, d, act_rows, sums, opp_a, opp_b):
+def middle_body(at, pre, back, recv, gate, up, others, d, act_rows, values, opp_a, opp_b):
     rows = pre.shape[0]
     both = pre.shape[1] // 2
     half = rows // 2
-    experts = rows // CAP
-    owner = owner_of(rows, experts)
-    slot = slot_is(rows, CAP)
     weights = pre_weights(at, gate, up, others, 2, 0, opp_a.shape[1])
-    total = None
     for lo, out in ((0, opp_a), (half, opp_b)):
         span = slice(lo, lo + half)
         pre_all = pre[span, :] + recv[span, : 2 * both].astype(F32)
@@ -260,18 +235,10 @@
         d[span, :] = grads
         out[...] = mm(grads, weights, NT).astype(BF)
         value = jnp.sum(act * back_all, axis=1, keepdims=True)
-        part = lax.dot_general(
-            owner[span, :],
-            jnp.where(slot[span, :], value, 0.0),
-            TN,
-            preferred_element_type=F32,
-            precision=lax.Precision.HIGHEST,
-        )
-        total = part if total is None else total + part
-    sums[...] = total
-
-
-def rows_body(at, d, gate, up, others, to_right, to_left, right_later, left_later, own):
+        values[span, :] = jnp.broadcast_to(value, (half, values.shape[1]))
+
+
+def rows_body(at, d, values, gate, up, others, to_right, to_left, right_later, left_later, own, sums):
     half = d.shape[0] // 2
     block = own.shape[1]
     weights = pre_weights(at, gate, up, others, 1, 0, block)
@@ -283,6 +250,14 @@
     weights = pre_weights(at, gate, up, others, 0, 0, block)
     own[:half, :] = mm(d[:half, :], weights, NT)
     own[half:, :] = mm(d[half:, :], weights, NT)
+    rows = d.shape[0]
+    sums[...] = lax.dot_general(
+        owner_of(rows, rows // CAP),
+        jnp.where(slot_is(rows, CAP), values[:, :CAP], 0.0),
+        TN,
+        preferred_element_type=F32,
+        precision=lax.Precision.HIGHEST,
+    )
 
 
 def later_body(at, right_later, left_later, from_left, from_right, to_right, to_left):
@@ -297,29 +272,24 @@
 
 
 def grads_body(at, d, act_rows, *refs):
-    keep, send = refs[-2:]
-    messages = [refs[i : i + 5] for i in range(0, len(refs) - 2, 5)]
-    block = keep.shape[2]
-    units = keep.shape[3]
+    x, dy, (keep, send) = refs[:5], refs[5:10], refs[10:]
+    block, units = keep.shape[2:]
     half = d.shape[0] // 2
-    tokens, cotangents = plan(block)
     for r in range(CHIPS):
-        for message, column, feature, many in tokens:
-            total = None
-            for lo, part in halves_of(messages[message], r, half, slice(column, column + many)):
-                value = mm(part, d[lo : lo + half, :], TN)
-                total = value if total is None else total + value
-            for i, (out, kind) in enumerate(((keep, 0), (send, 0), (keep, 1), (send, 1))):
-                out[r, kind, feature : feature + many, :] = total[:, i * units : (i + 1) * units].astype(BF)
-        for message, column, feature, many in cotangents:
-            total = None
-            for lo, part in halves_of(messages[message], r, half, slice(column, column + many)):
-                value = mm(act_rows[lo : lo + half, :], part, TN)
-                total = value if total is None else total + value
-            total = total.astype(BF)
-            for j in range(0, many, units):
-                keep[r, 2, feature + j : feature + j + units, :] = total[:units, j : j + units]
-                send[r, 2, feature + j : feature + j + units, :] = total[units:, j : j + units]
+        total = None
+        for lo, part in halves_of(x, r, half):
+            value = mm(part, d[lo : lo + half, :], TN)
+            total = value if total is None else total + value
+        for i, (out, kind) in enumerate(((keep, 0), (send, 0), (keep, 1), (send, 1))):
+            out[r, kind] = total[:, i * units : (i + 1) * units].astype(BF)
+        total = None
+        for lo, part in halves_of(dy, r, half):
+            value = mm(act_rows[lo : lo + half, :], part, TN)
+            total = value if total is None else total + value
+        total = total.astype(BF)
+        for j in range(0, block, units):
+            keep[r, 2, j : j + units, :] = total[:units, j : j + units]
+            send[r, 2, j : j + units, :] = total[units:, j : j + units]
 
 
 def place_body(at, keep, recv, gate, up, down, token):
@@ -426,7 +396,6 @@
     units = gate.shape[1]
     both = 2 * units
     routes, gates = routes.T, gating.T
-    of_tokens, of_cotangents = plan(block)
 
     def over_experts(value):
         split = value.reshape(experts, value.shape[0] // experts, value.shape[1])
@@ -435,29 +404,24 @@
     def my_block(value):
         return lax.dynamic_slice(value, (0, hidden * block), (count, block))
 
-    my_tokens = my_block(tokens)
-    message, pick, weighted = call(
+    message, pick = call(
         functools.partial(first_body, experts),
-        (shape((rows, widths(block)[0]), BF),) + (shape((rows, count), BF),) * 2,
-        (at, routes, gates, my_tokens),
+        (shape((rows, block), BF), shape((rows, count), BF)),
+        (at, routes, my_block(tokens)),
     )
     arrived = [over_experts(message)]
     halved, token = halves(at, gate, up, down)
-    messages = call(
-        rest_body,
-        tuple(shape((rows, many), BF) for many in widths(block)[1:]),
-        (at, pick, weighted, my_tokens, my_block(grad_out)),
-        after=(token,),
-    )
-    arrived += [over_experts(message) for message in messages]
+    (message,) = call(
+        rest_body, (shape((rows, block), BF),), (at, pick, routes, gates, my_block(grad_out)), after=(token,)
+    )
+    arrived.append(over_experts(message))
     others = swap(halved)
     weights = (gate, up, others)
-    (x_piece,), (dy_piece,) = of_tokens, of_cotangents
     part = (shape((half, block), BF),)
 
     left, right = to(arrived[0], 1), to(arrived[0], -1)
     pass_a, pass_b, pre, *token = call(
-        functools.partial(turn_body, x_piece),
+        turn_body,
         part * 2 + (shape((rows, 2 * both), F32),),
         (at, arrived[0], right, left, *weights),
         token=True,
@@ -468,30 +432,30 @@
     dy = (arrived[1], right, left, to(pass_a, 1), to(pass_b, -1))
 
     narrow = shape((rows, both), F32)
-    pre, back = call(
-        functools.partial(early_body, x_piece, dy_piece),
-        (shape((rows, 2 * both), F32), narrow),
+    pre, back, pre_send = call(
+        early_body,
+        (shape((rows, 2 * both), F32), narrow, shape((rows, 2 * both), BF)),
         (at, *weights, down, *x[3:], pre, *dy[:3]),
         after=token,
     )
     back, send = call(
-        functools.partial(late_body, dy_piece),
+        late_body,
         (narrow, shape((rows, 3 * both), BF)),
-        (at, down, others, *dy[3:], back, pre),
+        (at, down, others, *dy[3:], back, pre_send),
     )
     recv = swap(send)
 
     later = (shape((half, block), F32),)
-    d, act_rows, sums, opp_a, opp_b = call(
+    d, act_rows, values, opp_a, opp_b = call(
         middle_body,
-        (shape((rows, 2 * both), BF), shape((rows, both), BF), shape((experts, CAP), F32)) + part * 2,
+        (shape((rows, 2 * both), BF), shape((rows, both), BF), shape((rows, 128), F32)) + part * 2,
         (at, pre, back, recv, *weights),
     )
     from_left, from_right = to(opp_a, 1), to(opp_b, -1)
-    to_right, to_left, right_later, left_later, own, *token = call(
+    to_right, to_left, right_later, left_later, own, sums, *token = call(
         rows_body,
-        part * 2 + later * 2 + (shape((rows, block), F32),),
-        (at, d, *weights),
+        part * 2 + later * 2 + (shape((rows, block), F32), shape((experts, CAP), F32)),
+        (at, d, values, *weights),
         token=True,
     )
     left_b, right_a = to(to_right, 1), to(to_left, -1)

time: 192 us -> 189 us (0.984)
    unnamed x30 -> x28, local copies, waits for them, and re-layouts: 11.6 us -> 10.9 us
  transfers between devices with their start and end apart: 23 -> 23, of which waited for: 11 -> 9; matrix products, arithmetic and copies ran while one was open for 0% -> 0% of each run, Pallas kernels for 16% -> 16%
where the time goes in v5:
time: 189 us; the launch traced here: 188 us
  waiting for transfers between devices  70.6 us (37%)
  starting transfers between devices  53 us (28%)
  Pallas kernels  38.6 us (20%)
  blocking collectives  13.1 us (7%)
  local copies, waits for them, and re-layouts  11.9 us (6%)
    all_to_all x3, waiting for transfers between devices, over_experts(): lax.all_to_all(split, 'expert', split_axis=0, concat_axis=0, tiled=True)  44.1 us
    pallas_call x13, Pallas kernels, call(): pl.pallas_call(run, out_shape=out_shape + ((shape((8, 128), F32),) if tok...  28 us
    ppermute x17, waiting for transfers between devices, to(): lax.ppermute(value, 'hidden', [(i, (i + 2 * shift) % size) for i in range...  24.6 us
    all_to_all x3, starting transfers between devices, over_experts(): lax.all_to_all(split, 'expert', split_axis=0, concat_axis=0, tiled=True)  22.2 us
    ppermute x17, starting transfers between devices, to(): lax.ppermute(value, 'hidden', [(i, (i + 2 * shift) % size) for i in range...  21.2 us
    all_to_all x1, blocking collectives, over_experts(): lax.all_to_all(split, 'expert', split_axis=0, concat_axis=0, tiled=True)  13.1 us
    unnamed x28, local copies, waits for them, and re-layouts  10.9 us
    ppermute x3, starting transfers between devices, swap(): return lax.ppermute(value, 'hidden', [(i, i ^ 1) for i in range(2 * CHIPS)])  9.51 us
  transfers between devices with their start and end apart: 23, of which 9 were waited for; matrix products, arithmetic and copies ran while one was open for 0% of the time, Pallas kernels for 16%

profile of v5, /device:TPU:17, one launch (start us, length us, event | category | flops | bytes accessed | tf_op | source)
XLA Modules:
  0.0 188.1 jit_solution(18239533115942955918)
XLA Ops:
  2.4 2.1 %shard_map.110 = (bf16[512,896]{1,0:T(8,128)(2,1)}, bf16[512,32]{1,0:T(8,128)(2,1)S(1)}) custom-call(s32[2]{0:T(128)S(1)} %pad_add_fusion.refs_0_.at, s32[8,32]{1,0:T(8,128)S(1)} %bitcast.41, bf16[32,896]{1,0:T(8,128)(2,1)S(1)} %get-tuple-element.88.refs_2_), custom_call_target="tpu_custom_call" | custom-call | bytes 1008640 | tf_op jit(solution)/shard_map/pallas_call | solution.py:42
  4.5 11.1 %all-to-all-start = ((bf16[32,16,896]{2,1,0:T(8,128)(2,1)}), bf16[32,16,896]{2,1,0:T(8,128)(2,1)}, u32[]{:S(2)}, u32[]{:S(2)}) async-start(bf16[32,16,896]{2,1,0:T(8,128)(2,1)} %bitcast.6), calls=%async_computation | async-start | bytes 1835008 | tf_op jit(solution)/shard_map/all_to_all | solution.py:402
  18.6 2.8 %shard_map.111 = (bf16[4,3,896,128]{3,2,1,0:T(8,128)(2,1)}, f32[8,128]{1,0:T(8,128)S(1)}) custom-call(s32[2]{0:T(128)S(1)} %pad_add_fusion.refs_0_.at, bf16[7168,128]{1,0:T(8,128)(2,1)S(1)} %bitcast.21, bf16[7168,128]{1,0:T(8,128)(2,1)S(1)} %bitcast.26, bf16[128,7168]{1,0:T(8,128)(2,1)S(1)} %bitcast.31), custom_call_target="tpu_custom_call" | custom-call | bytes 11010048 | tf_op jit(solution)/shard_map/pallas_call | solution.py:126
  24.6 15.1 %all-to-all-done = bf16[32,16,896]{2,1,0:T(8,128)(2,1)} async-done(((bf16[32,16,896]{2,1,0:T(8,128)(2,1)}), bf16[32,16,896]{2,1,0:T(8,128)(2,1)}, u32[]{:S(2)}, u32[]{:S(2)}) %all-to-all-start) | async-done | bytes 917536 | tf_op jit(solution)/shard_map/all_to_all | solution.py:402
  39.8 5.5 %all-to-all-start.1 = ((bf16[32,16,896]{2,1,0:T(8,128)(2,1)}), bf16[32,16,896]{2,1,0:T(8,128)(2,1)}, u32[]{:S(2)}, u32[]{:S(2)}) async-start(bf16[32,16,896]{2,1,0:T(8,128)(2,1)} %bitcast.35), calls=%async_computation.1 | async-start | bytes 1835008 | tf_op jit(solution)/shard_map/all_to_all | solution.py:402
  48.1 20.1 %all-to-all-done.1 = bf16[32,16,896]{2,1,0:T(8,128)(2,1)} async-done(((bf16[32,16,896]{2,1,0:T(8,128)(2,1)}), bf16[32,16,896]{2,1,0:T(8,128)(2,1)}, u32[]{:S(2)}, u32[]{:S(2)}) %all-to-all-start.1) | async-done | bytes 917536 | tf_op jit(solution)/shard_map/all_to_all | solution.py:402
  73.9 3.7 %shard_map.112 = (bf16[256,896]{1,0:T(8,128)(2,1)S(1)}, bf16[256,896]{1,0:T(8,128)(2,1)S(1)}, f32[512,512]{1,0:T(8,128)S(1)}, f32[8,128]{1,0:T(8,128)S(1)}) custom-call(s32[2]{0:T(128)S(1)} %pad_add_fusion.refs_0_.at, bf16[512,896]{1,0:T(8,128)(2,1)} %bitcast.7.refs_1_.refs_3_, bf16[512,896]{1,0:T(8,128)(2,1)} %collective-permute-done.1.refs_2_.refs_4_, ...), custom_call_target="tpu_custom_call" | custom-call | bytes 11141120 | tf_op jit(solution)/shard_map/pallas_call | solution.py:42
  77.7 2.7 %collective-permute-start.4 = (bf16[256,896]{1,0:T(8,128)(2,1)S(1)}, bf16[256,896]{1,0:T(8,128)(2,1)S(1)}, u32[]{:S(2)}, u32[]{:S(2)}) collective-permute-start(bf16[256,896]{1,0:T(8,128)(2,1)S(1)} %get-tuple-element.50), channel_id=1, source_target_pairs={{0,6},{1,7},{2,0},{3,1},{4,2},{5,3},{6,4},{7,5},{8,14},{9,15},{10,... | collective-permute-start | bytes 1376264 | tf_op jit(solution)/shard_map/ppermute | solution.py:368
  80.4 7.4 %collective-permute-done.6.refs_1_.refs_10_ = bf16[512,896]{1,0:T(8,128)(2,1)S(1)} collective-permute-done((bf16[512,896]{1,0:T(8,128)(2,1)}, bf16[512,896]{1,0:T(8,128)(2,1)S(1)}, u32[]{:S(2)}, u32[]{:S(2)}) %collective-permute-start.6) | collective-permute-done | bytes 917536 | tf_op jit(solution)/shard_map/ppermute | solution.py:368
  91.1 6.5 %collective-permute-done.3.refs_5_.refs_6_ = bf16[256,896]{1,0:T(8,128)(2,1)S(1)} collective-permute-done((bf16[256,896]{1,0:T(8,128)(2,1)S(1)}, bf16[256,896]{1,0:T(8,128)(2,1)S(1)}, u32[]{:S(2)}, u32[]{:S(2)}) %collective-permute-start.3) | collective-permute-done | bytes 458784 | tf_op jit(solution)/shard_map/ppermute | solution.py:368
  97.6 2.7 %shard_map.115 = (f32[512,512]{1,0:T(8,128)S(1)}, f32[512,256]{1,0:T(8,128)S(1)}, bf16[512,512]{1,0:T(8,128)(2,1)S(1)}) custom-call(s32[2]{0:T(128)S(1)} %pad_add_fusion.refs_0_.at, bf16[7168,128]{1,0:T(8,128)(2,1)S(1)} %bitcast.23, bf16[7168,128]{1,0:T(8,128)(2,1)S(1)} %bitcast.28, ...), custom_call_target="tpu_custom_call" | custom-call | bytes 15073280 | tf_op jit(solution)/shard_map/pallas_call | solution.py:42
  100.4 7.1 %collective-permute-done.7.refs_3_.refs_11_ = bf16[256,896]{1,0:T(8,128)(2,1)S(1)} collective-permute-done((bf16[256,896]{1,0:T(8,128)(2,1)S(1)}, bf16[256,896]{1,0:T(8,128)(2,1)S(1)}, u32[]{:S(2)}, u32[]{:S(2)}) %collective-permute-start.7) | collective-permute-done | bytes 458784 | tf_op jit(solution)/shard_map/ppermute | solution.py:368
  108.5 4.9 %collective-permute-start.9 = (bf16[512,768]{1,0:T(8,128)(2,1)S(1)}, bf16[512,768]{1,0:T(8,128)(2,1)S(1)}, u32[]{:S(2)}, u32[]{:S(2)}) collective-permute-start(bf16[512,768]{1,0:T(8,128)(2,1)S(1)} %get-tuple-element.61), channel_id=1, source_target_pairs={{0,1},{1,0},{2,3},{3,2},{4,5},{5,4},{6,7},{7,6},{8,9},{9,8},{10,11... | collective-permute-start | bytes 2359304 | tf_op jit(solution)/shard_map/ppermute | solution.py:372
  119.5 2.5 %shard_map.118 = (bf16[256,896]{1,0:T(8,128)(2,1)S(1)}, bf16[256,896]{1,0:T(8,128)(2,1)S(1)}, f32[256,896]{1,0:T(8,128)S(1)}, f32[256,896]{1,0:T(8,128)S(1)}, f3...) custom-call(s32[2]{0:T(128)S(1)} %pad_add_fusion.refs_0_.at, ...), custom_call_target="tpu_custom_call" | custom-call | bytes 11798528 | tf_op jit(solution)/shard_map/pallas_call | solution.py:42
  122.2 2.7 %collective-permute-start.14 = (bf16[256,896]{1,0:T(8,128)(2,1)S(1)}, bf16[256,896]{1,0:T(8,128)(2,1)S(1)}, u32[]{:S(2)}, u32[]{:S(2)}) collective-permute-start(bf16[256,896]{1,0:T(8,128)(2,1)S(1)} %get-tuple-element.74), channel_id=1, source_target_pairs={{0,6},{1,7},{2,0},{3,1},{4,2},{5,3},{6,4},{7,5},{8,14},{9,15},{10,... | collective-permute-start | bytes 1376264 | tf_op jit(solution)/shard_map/ppermute | solution.py:368
  124.8 6.8 %shard_map.119 = (bf16[4,3,896,128]{3,2,1,0:T(8,128)(2,1)S(1)}, bf16[4,3,896,128]{3,2,1,0:T(8,128)(2,1)}, f32[8,128]{1,0:T(8,128)S(1)}) custom-call(s32[2]{0:T(128)S(1)} %pad_add_fusion.refs_0_.at, bf16[512,512]{1,0:T(8,128)(2,1)S(1)} %get-tuple-element.62.refs_1_, bf16[512,256]{1,0:T(8,128)(2,1)S(1)} %get-tuple-element.69.refs_2_, ...), custom_call_target="tpu_custom_call" | custom-call | bytes 13631488 | tf_op jit(solution)/shard_map/pallas_call | solution.py:42
  133.9 2.7 %collective-permute-start.15 = (bf16[256,896]{1,0:T(8,128)(2,1)S(1)}, bf16[256,896]{1,0:T(8,128)(2,1)S(1)}, u32[]{:S(2)}, u32[]{:S(2)}) collective-permute-start(bf16[256,896]{1,0:T(8,128)(2,1)S(1)} %get-tuple-element.75), channel_id=1, source_target_pairs={{0,6},{1,7},{2,0},{3,1},{4,2},{5,3},{6,4},{7,5},{8,14},{9,15},{10,... | collective-permute-start | bytes 1376264 | tf_op jit(solution)/shard_map/ppermute | solution.py:368
  136.6 13.1 %all_to_all.20 = f32[32,1,16]{2,1,0:T(1,128)S(1)} all-to-all(f32[32,1,16]{2,1,0:T(1,128)S(1)} %bitcast.44), channel_id=1, replica_groups=mesh['expert'=32,'hidden'=8] {'expert'}, dimensions={0} | all-to-all | bytes 4096 | tf_op jit(solution)/shard_map/all_to_all | solution.py:402
  151.5 3.4 %collective-permute-start.19 = (bf16[4,3,896,128]{3,2,1,0:T(8,128)(2,1)}, bf16[4,3,896,128]{3,2,1,0:T(8,128)(2,1)}, u32[]{:S(2)}, u32[]{:S(2)}) collective-permute-start(bf16[4,3,896,128]{3,2,1,0:T(8,128)(2,1)} %shard_map.123), channel_id=1, source_target_pairs={{0,1},{1,0},{2,3},{3,2},{4,5},{5,4},{6,7},{7,6},{8,9},{9,8},{10,11... | collective-permute-start | bytes 8257544 | tf_op jit(solution)/shard_map/ppermute | solution.py:372
  154.9 5.6 %all-to-all-start.3 = ((bf16[32,16,896]{2,1,0:T(8,128)(2,1)}), bf16[32,16,896]{2,1,0:T(8,128)(2,1)S(1)}, u32[]{:S(2)}, u32[]{:S(2)}) async-start(bf16[32,16,896]{2,1,0:T(8,128)(2,1)} %bitcast.14), calls=%async_computation.3 | async-start | bytes 1835008 | tf_op jit(solution)/shard_map/all_to_all | solution.py:402
  163.5 2.6 %collective-permute-done.17.refs_6_ = f32[32,16]{1,0:T(8,128)S(1)} collective-permute-done((f32[32,16]{1,0:T(8,128)S(1)}, f32[32,16]{1,0:T(8,128)S(1)}, u32[]{:S(2)}, u32[]{:S(2)}) %collective-permute-start.17) | collective-permute-done | bytes 2080 | tf_op jit(solution)/shard_map/ppermute | solution.py:368
  166.1 2.0 %shard_map.122 = (f32[8,32]{1,0:T(8,128)}, f32[8,128]{1,0:T(8,128)S(1)}) custom-call(s32[2]{0:T(128)S(1)} %pad_add_fusion.refs_0_.at, bf16[512,32]{1,0:T(8,128)(2,1)S(1)} %get-tuple-element.46.refs_1_, s32[8,32]{1,0:T(8,128)S(1)} %bitcast.43, bf16[8,32]{1,0:T(8,128)(2,1)S(1)} %bitcast.46, f32[32,16]{1,0:T(8,128)S(1)} %bitcast.40, ...), custom_call_target="tpu_custom_call" | custom-call | bytes 43520 | tf_op jit(solution)/shard_map/pallas_call | solution.py:42
  169.9 7.9 %shard_map.124 = (bf16[7168,128]{1,0:T(8,128)(2,1)}, bf16[7168,128]{1,0:T(8,128)(2,1)}, bf16[128,7168]{1,0:T(8,128)(2,1)}, f32[8,128]{1,0:T(8,128)S(1)}) custom-call(s32[2]{0:T(128)S(1)} %pad_add_fusion.refs_0_.at, bf16[4,3,896,128]{3,2,1,0:T(8,128)(2,1)S(1)} %copy-done.10, bf16[4,3,896,128]{3,2,1,0:T(8,128)(2,1)} %collective-permute-done.19.recv), custom_call_target="tpu_custom_call" | custom-call | bytes 11010048 | tf_op jit(solution)/shard_map/pallas_call | solution.py:319
  177.7 8.9 %all-to-all-done.3 = bf16[32,16,896]{2,1,0:T(8,128)(2,1)S(1)} async-done(((bf16[32,16,896]{2,1,0:T(8,128)(2,1)}), bf16[32,16,896]{2,1,0:T(8,128)(2,1)S(1)}, u32[]{:S(2)}, u32[]{:S(2)}) %all-to-all-start.3) | async-done | bytes 917536 | tf_op jit(solution)/shard_map/all_to_all | solution.py:402
  (69 shorter events, 37.5 us)
Async XLA Ops:
  4.5 35.2 %all-to-all-start = ((bf16[32,16,896]{2,1,0:T(8,128)(2,1)}), bf16[32,16,896]{2,1,0:T(8,128)(2,1)}, u32[]{:S(2)}, u32[]{:S(2)}) async-start(bf16[32,16,896]{2,1,0:T(8,128)(2,1)} %bitcast.6), calls=%async_computation | async-start | bytes 1835008 | tf_op jit(solution)/shard_map/all_to_all | solution.py:402
  21.4 49.5 %collective-permute-start = (bf16[4,3,896,128]{3,2,1,0:T(8,128)(2,1)}, bf16[4,3,896,128]{3,2,1,0:T(8,128)(2,1)S(1)}, u32[]{:S(2)}, u32[]{:S(2)}) collective-permute-start(bf16[4,3,896,128]{3,2,1,0:T(8,128)(2,1)} %get-tuple-element.47), channel_id=1, source_target_pairs={{0,1},{1,0},{2,3},{3,2},{4,5},{5,4},{6,7},{7,6},{8,9},{9,8},{10,11... | collective-permute-start | bytes 8257544 | tf_op jit(solution)/shard_map/ppermute | solution.py:372
  39.8 28.4 %all-to-all-start.1 = ((bf16[32,16,896]{2,1,0:T(8,128)(2,1)}), bf16[32,16,896]{2,1,0:T(8,128)(2,1)}, u32[]{:S(2)}, u32[]{:S(2)}) async-start(bf16[32,16,896]{2,1,0:T(8,128)(2,1)} %bitcast.35), calls=%async_computation.1 | async-start | bytes 1835008 | tf_op jit(solution)/shard_map/all_to_all | solution.py:402
  45.3 25.5 %collective-permute-start.2 = (bf16[512,896]{1,0:T(8,128)(2,1)}, bf16[512,896]{1,0:T(8,128)(2,1)}, u32[]{:S(2)}, u32[]{:S(2)}) collective-permute-start(bf16[512,896]{1,0:T(8,128)(2,1)} %bitcast.7.refs_1_.refs_3_), channel_id=1, source_target_pairs={{0,2},{1,3},{2,4},{3,5},{4,6},{5,7},{6,0},{7,1},{8,10},{9,11},{10,... | collective-permute-start | bytes 2752520 | tf_op jit(solution)/shard_map/ppermute | solution.py:368
  46.6 24.3 %collective-permute-start.1 = (bf16[512,896]{1,0:T(8,128)(2,1)}, bf16[512,896]{1,0:T(8,128)(2,1)}, u32[]{:S(2)}, u32[]{:S(2)}) collective-permute-start(bf16[512,896]{1,0:T(8,128)(2,1)} %bitcast.7.refs_1_.refs_3_), channel_id=1, source_target_pairs={{0,6},{1,7},{2,0},{3,1},{4,2},{5,3},{6,4},{7,5},{8,14},{9,15},{10,... | collective-permute-start | bytes 2752520 | tf_op jit(solution)/shard_map/ppermute | solution.py:368
  68.2 19.6 %collective-permute-start.6 = (bf16[512,896]{1,0:T(8,128)(2,1)}, bf16[512,896]{1,0:T(8,128)(2,1)S(1)}, u32[]{:S(2)}, u32[]{:S(2)}) collective-permute-start(bf16[512,896]{1,0:T(8,128)(2,1)} %bitcast.10.refs_8_), channel_id=1, source_target_pairs={{0,2},{1,3},{2,4},{3,5},{4,6},{5,7},{6,0},{7,1},{8,10},{9,11},{10,... | collective-permute-start | bytes 2752520 | tf_op jit(solution)/shard_map/ppermute | solution.py:368
  69.4 18.4 %collective-permute-start.5 = (bf16[512,896]{1,0:T(8,128)(2,1)}, bf16[512,896]{1,0:T(8,128)(2,1)S(1)}, u32[]{:S(2)}, u32[]{:S(2)}) collective-permute-start(bf16[512,896]{1,0:T(8,128)(2,1)} %bitcast.10.refs_8_), channel_id=1, source_target_pairs={{0,6},{1,7},{2,0},{3,1},{4,2},{5,3},{6,4},{7,5},{8,14},{9,15},{10,... | collective-permute-start | bytes 2752520 | tf_op jit(solution)/shard_map/ppermute | solution.py:368
  73.9 23.7 %copy-start.7 = (bf16[1,128,7168]{2,1,0:T(8,128)(2,1)S(1)}, bf16[1,128,7168]{2,1,0:T(8,128)(2,1)}, u32[]{:S(2)}) copy-start(bf16[1,128,7168]{2,1,0:T(8,128)(2,1)} %param.13) | copy-start | bytes 5505028
  77.6 20.0 %collective-permute-start.3 = (bf16[256,896]{1,0:T(8,128)(2,1)S(1)}, bf16[256,896]{1,0:T(8,128)(2,1)S(1)}, u32[]{:S(2)}, u32[]{:S(2)}) collective-permute-start(bf16[256,896]{1,0:T(8,128)(2,1)S(1)} %get-tuple-element.49), channel_id=1, source_target_pairs={{0,2},{1,3},{2,4},{3,5},{4,6},{5,7},{6,0},{7,1},{8,10},{9,11},{10,... | collective-permute-start | bytes 1376264 | tf_op jit(solution)/shard_map/ppermute | solution.py:368
  77.7 19.9 %collective-permute-start.4 = (bf16[256,896]{1,0:T(8,128)(2,1)S(1)}, bf16[256,896]{1,0:T(8,128)(2,1)S(1)}, u32[]{:S(2)}, u32[]{:S(2)}) collective-permute-start(bf16[256,896]{1,0:T(8,128)(2,1)S(1)} %get-tuple-element.50), channel_id=1, source_target_pairs={{0,6},{1,7},{2,0},{3,1},{4,2},{5,3},{6,4},{7,5},{8,14},{9,15},{10,... | collective-permute-start | bytes 1376264 | tf_op jit(solution)/shard_map/ppermute | solution.py:368
  88.4 19.0 %collective-permute-start.7 = (bf16[256,896]{1,0:T(8,128)(2,1)S(1)}, bf16[256,896]{1,0:T(8,128)(2,1)S(1)}, u32[]{:S(2)}, u32[]{:S(2)}) collective-permute-start(bf16[256,896]{1,0:T(8,128)(2,1)S(1)} %get-tuple-element.56), channel_id=1, source_target_pairs={{0,2},{1,3},{2,4},{3,5},{4,6},{5,7},{6,0},{7,1},{8,10},{9,11},{10,... | collective-permute-start | bytes 1376264 | tf_op jit(solution)/shard_map/ppermute | solution.py:368
  89.4 18.0 %collective-permute-start.8 = (bf16[256,896]{1,0:T(8,128)(2,1)S(1)}, bf16[256,896]{1,0:T(8,128)(2,1)S(1)}, u32[]{:S(2)}, u32[]{:S(2)}) collective-permute-start(bf16[256,896]{1,0:T(8,128)(2,1)S(1)} %get-tuple-element.57), channel_id=1, source_target_pairs={{0,6},{1,7},{2,0},{3,1},{4,2},{5,3},{6,4},{7,5},{8,14},{9,15},{10,... | collective-permute-start | bytes 1376264 | tf_op jit(solution)/shard_map/ppermute | solution.py:368
  108.5 6.8 %collective-permute-start.9 = (bf16[512,768]{1,0:T(8,128)(2,1)S(1)}, bf16[512,768]{1,0:T(8,128)(2,1)S(1)}, u32[]{:S(2)}, u32[]{:S(2)}) collective-permute-start(bf16[512,768]{1,0:T(8,128)(2,1)S(1)} %get-tuple-element.61), channel_id=1, source_target_pairs={{0,1},{1,0},{2,3},{3,2},{4,5},{5,4},{6,7},{7,6},{8,9},{9,8},{10,11... | collective-permute-start | bytes 2359304 | tf_op jit(solution)/shard_map/ppermute | solution.py:372
  116.7 16.4 %collective-permute-start.10 = (bf16[256,896]{1,0:T(8,128)(2,1)S(1)}, bf16[256,896]{1,0:T(8,128)(2,1)S(1)}, u32[]{:S(2)}, u32[]{:S(2)}) collective-permute-start(bf16[256,896]{1,0:T(8,128)(2,1)S(1)} %get-tuple-element.67), channel_id=1, source_target_pairs={{0,2},{1,3},{2,4},{3,5},{4,6},{5,7},{6,0},{7,1},{8,10},{9,11},{10,... | collective-permute-start | bytes 1376264 | tf_op jit(solution)/shard_map/ppermute | solution.py:368
  118.0 15.2 %collective-permute-start.11 = (bf16[256,896]{1,0:T(8,128)(2,1)S(1)}, bf16[256,896]{1,0:T(8,128)(2,1)S(1)}, u32[]{:S(2)}, u32[]{:S(2)}) collective-permute-start(bf16[256,896]{1,0:T(8,128)(2,1)S(1)} %get-tuple-element.68), channel_id=1, source_target_pairs={{0,6},{1,7},{2,0},{3,1},{4,2},{5,3},{6,4},{7,5},{8,14},{9,15},{10,... | collective-permute-start | bytes 1376264 | tf_op jit(solution)/shard_map/ppermute | solution.py:368
  122.1 27.6 %collective-permute-start.13 = (bf16[256,896]{1,0:T(8,128)(2,1)S(1)}, bf16[256,896]{1,0:T(8,128)(2,1)S(1)}, u32[]{:S(2)}, u32[]{:S(2)}) collective-permute-start(bf16[256,896]{1,0:T(8,128)(2,1)S(1)} %get-tuple-element.73), channel_id=1, source_target_pairs={{0,2},{1,3},{2,4},{3,5},{4,6},{5,7},{6,0},{7,1},{8,10},{9,11},{10,... | collective-permute-start | bytes 1376264 | tf_op jit(solution)/shard_map/ppermute | solution.py:368
  122.2 27.5 %collective-permute-start.14 = (bf16[256,896]{1,0:T(8,128)(2,1)S(1)}, bf16[256,896]{1,0:T(8,128)(2,1)S(1)}, u32[]{:S(2)}, u32[]{:S(2)}) collective-permute-start(bf16[256,896]{1,0:T(8,128)(2,1)S(1)} %get-tuple-element.74), channel_id=1, source_target_pairs={{0,6},{1,7},{2,0},{3,1},{4,2},{5,3},{6,4},{7,5},{8,14},{9,15},{10,... | collective-permute-start | bytes 1376264 | tf_op jit(solution)/shard_map/ppermute | solution.py:368
  133.8 15.9 %collective-permute-start.12 = (bf16[256,896]{1,0:T(8,128)(2,1)S(1)}, bf16[256,896]{1,0:T(8,128)(2,1)S(1)}, u32[]{:S(2)}, u32[]{:S(2)}) collective-permute-start(bf16[256,896]{1,0:T(8,128)(2,1)S(1)} %get-tuple-element.72), channel_id=1, source_target_pairs={{0,2},{1,3},{2,4},{3,5},{4,6},{5,7},{6,0},{7,1},{8,10},{9,11},{10,... | collective-permute-start | bytes 1376264 | tf_op jit(solution)/shard_map/ppermute | solution.py:368
  133.9 15.8 %collective-permute-start.15 = (bf16[256,896]{1,0:T(8,128)(2,1)S(1)}, bf16[256,896]{1,0:T(8,128)(2,1)S(1)}, u32[]{:S(2)}, u32[]{:S(2)}) collective-permute-start(bf16[256,896]{1,0:T(8,128)(2,1)S(1)} %get-tuple-element.75), channel_id=1, source_target_pairs={{0,6},{1,7},{2,0},{3,1},{4,2},{5,3},{6,4},{7,5},{8,14},{9,15},{10,... | collective-permute-start | bytes 1376264 | tf_op jit(solution)/shard_map/ppermute | solution.py:368
  151.5 16.6 %collective-permute-start.19 = (bf16[4,3,896,128]{3,2,1,0:T(8,128)(2,1)}, bf16[4,3,896,128]{3,2,1,0:T(8,128)(2,1)}, u32[]{:S(2)}, u32[]{:S(2)}) collective-permute-start(bf16[4,3,896,128]{3,2,1,0:T(8,128)(2,1)} %shard_map.123), channel_id=1, source_target_pairs={{0,1},{1,0},{2,3},{3,2},{4,5},{5,4},{6,7},{7,6},{8,9},{9,8},{10,11... | collective-permute-start | bytes 8257544 | tf_op jit(solution)/shard_map/ppermute | solution.py:372
  154.9 31.8 %all-to-all-start.3 = ((bf16[32,16,896]{2,1,0:T(8,128)(2,1)}), bf16[32,16,896]{2,1,0:T(8,128)(2,1)S(1)}, u32[]{:S(2)}, u32[]{:S(2)}) async-start(bf16[32,16,896]{2,1,0:T(8,128)(2,1)} %bitcast.14), calls=%async_computation.3 | async-start | bytes 1835008 | tf_op jit(solution)/shard_map/all_to_all | solution.py:402
  160.5 3.0 %collective-permute-start.18 = (f32[32,16]{1,0:T(8,128)S(1)}, f32[32,16]{1,0:T(8,128)S(1)}, u32[]{:S(2)}, u32[]{:S(2)}) collective-permute-start(f32[32,16]{1,0:T(8,128)S(1)} %bitcast.37), channel_id=1, source_target_pairs={{0,6},{1,7},{2,0},{3,1},{4,2},{5,3},{6,4},{7,5},{8,14},{9,15},{10,... | collective-permute-start | bytes 6152 | tf_op jit(solution)/shard_map/ppermute | solution.py:368
  161.7 4.4 %collective-permute-start.17 = (f32[32,16]{1,0:T(8,128)S(1)}, f32[32,16]{1,0:T(8,128)S(1)}, u32[]{:S(2)}, u32[]{:S(2)}) collective-permute-start(f32[32,16]{1,0:T(8,128)S(1)} %bitcast.38), channel_id=1, source_target_pairs={{0,4},{1,5},{2,6},{3,7},{4,0},{5,1},{6,2},{7,3},{8,12},{9,13},{10,... | collective-permute-start | bytes 6152 | tf_op jit(solution)/shard_map/ppermute | solution.py:368
  161.7 4.4 %collective-permute-start.16 = (f32[32,16]{1,0:T(8,128)S(1)}, f32[32,16]{1,0:T(8,128)S(1)}, u32[]{:S(2)}, u32[]{:S(2)}) collective-permute-start(f32[32,16]{1,0:T(8,128)S(1)} %bitcast.39), channel_id=1, source_target_pairs={{0,2},{1,3},{2,4},{3,5},{4,6},{5,7},{6,0},{7,1},{8,10},{9,11},{10,... | collective-permute-start | bytes 6152 | tf_op jit(solution)/shard_map/ppermute | solution.py:368
  (13 other events, 77.7 us)

commit v6 on v5

--- a/solution.py
+++ b/solution.py
@@ -207,22 +207,20 @@
     add_body((0, 1, 3), True, False, at, down, others, *dy, back)
 
 
-def late_body(at, down, others, opp_a, opp_b, before, pre_send, back, send):
+def late_body(at, down, others, opp_a, opp_b, before, back, send):
     add_body((2,), False, False, at, down, others, opp_a, opp_b, before, back)
-    units = down.shape[0]
-    send[:, : 4 * units] = pre_send[...]
-    send[:, 4 * units :] = swapped(back[...], units)
-
-
-def middle_body(at, pre, back, recv, gate, up, others, d, act_rows, values, opp_a, opp_b):
+    send[...] = swapped(back[...], down.shape[0])
+
+
+def middle_body(at, pre, back, pre_recv, back_recv, gate, up, others, d, act_rows, values, opp_a, opp_b):
     rows = pre.shape[0]
     both = pre.shape[1] // 2
     half = rows // 2
     weights = pre_weights(at, gate, up, others, 2, 0, opp_a.shape[1])
     for lo, out in ((0, opp_a), (half, opp_b)):
         span = slice(lo, lo + half)
-        pre_all = pre[span, :] + recv[span, : 2 * both].astype(F32)
-        back_all = back[span, :] + recv[span, 2 * both :].astype(F32)
+        pre_all = pre[span, :] + pre_recv[span, :].astype(F32)
+        back_all = back[span, :] + back_recv[span, :].astype(F32)
         pre_gate = pre_all[:, :both]
         pre_up = pre_all[:, both:]
         sig = jax.nn.sigmoid(pre_gate)
@@ -440,16 +438,16 @@
     )
     back, send = call(
         late_body,
-        (narrow, shape((rows, 3 * both), BF)),
-        (at, down, others, *dy[3:], back, pre_send),
-    )
-    recv = swap(send)
+        (narrow, shape((rows, both), BF)),
+        (at, down, others, *dy[3:], back),
+    )
+    pre_recv, back_recv = swap(pre_send), swap(send)
 
     later = (shape((half, block), F32),)
     d, act_rows, values, opp_a, opp_b = call(
         middle_body,
         (shape((rows, 2 * both), BF), shape((rows, both), BF), shape((rows, 128), F32)) + part * 2,
-        (at, pre, back, recv, *weights),
+        (at, pre, back, pre_recv, back_recv, *weights),
     )
     from_left, from_right = to(opp_a, 1), to(opp_b, -1)
     to_right, to_left, right_later, left_later, own, sums, *token = call(

time: 189 us -> 188 us (level)
  waiting for transfers between devices: 70.6 us -> 62.6 us
  starting transfers between devices: 53 us -> 60.2 us
    ppermute x17, waiting for transfers between devices: 24.6 us -> 17.5 us  [to(): lax.ppermute(value, 'hidden', [(i, (i + 2 * shift) % size) for i in range...]
    ppermute x3 -> x4, starting transfers between devices: 9.51 us -> 16.6 us  [swap(): return lax.ppermute(value, 'hidden', [(i, i ^ 1) for i in range(2 * CHIPS)])]
  transfers between devices with their start and end apart: 23 -> 24, of which waited for: 9 -> 8; matrix products, arithmetic and copies ran while one was open for 0% -> 0% of each run, Pallas kernels for 16% -> 17%
where the time goes in v6:
time: 188 us; the launch traced here: 187 us
  waiting for transfers between devices  62.6 us (33%)
  starting transfers between devices  60.2 us (32%)
  Pallas kernels  38.6 us (21%)
  blocking collectives  13.1 us (7%)
  local copies, waits for them, and re-layouts  11.9 us (6%)
    all_to_all x3, waiting for transfers between devices, over_experts(): lax.all_to_all(split, 'expert', split_axis=0, concat_axis=0, tiled=True)  43.9 us
    pallas_call x13, Pallas kernels, call(): pl.pallas_call(run, out_shape=out_shape + ((shape((8, 128), F32),) if tok...  28 us
    all_to_all x3, starting transfers between devices, over_experts(): lax.all_to_all(split, 'expert', split_axis=0, concat_axis=0, tiled=True)  22.2 us
    ppermute x17, starting transfers between devices, to(): lax.ppermute(value, 'hidden', [(i, (i + 2 * shift) % size) for i in range...  21.4 us
    ppermute x17, waiting for transfers between devices, to(): lax.ppermute(value, 'hidden', [(i, (i + 2 * shift) % size) for i in range...  17.5 us
    ppermute x4, starting transfers between devices, swap(): return lax.ppermute(value, 'hidden', [(i, i ^ 1) for i in range(2 * CHIPS)])  16.6 us
    all_to_all x1, blocking collectives, over_experts(): lax.all_to_all(split, 'expert', split_axis=0, concat_axis=0, tiled=True)  13.1 us
    unnamed x28, local copies, waits for them, and re-layouts  10.9 us
  transfers between devices with their start and end apart: 24, of which 8 were waited for; matrix products, arithmetic and copies ran while one was open for 0% of the time, Pallas kernels for 17%

profile of v6, /device:TPU:17, one launch (start us, length us, event | category | flops | bytes accessed | tf_op | source)
XLA Modules:
  0.0 187.3 jit_solution(11954399416104867009)
XLA Ops:
  2.4 2.1 %shard_map.110 = (bf16[512,896]{1,0:T(8,128)(2,1)}, bf16[512,32]{1,0:T(8,128)(2,1)S(1)}) custom-call(s32[2]{0:T(128)S(1)} %pad_add_fusion.refs_0_.at, s32[8,32]{1,0:T(8,128)S(1)} %bitcast.41, bf16[32,896]{1,0:T(8,128)(2,1)S(1)} %get-tuple-element.88.refs_2_), custom_call_target="tpu_custom_call" | custom-call | bytes 1008640 | tf_op jit(solution)/shard_map/pallas_call | solution.py:42
  4.5 11.1 %all-to-all-start = ((bf16[32,16,896]{2,1,0:T(8,128)(2,1)}), bf16[32,16,896]{2,1,0:T(8,128)(2,1)}, u32[]{:S(2)}, u32[]{:S(2)}) async-start(bf16[32,16,896]{2,1,0:T(8,128)(2,1)} %bitcast.6), calls=%async_computation | async-start | bytes 1835008 | tf_op jit(solution)/shard_map/all_to_all | solution.py:400
  18.6 2.8 %shard_map.111 = (bf16[4,3,896,128]{3,2,1,0:T(8,128)(2,1)}, f32[8,128]{1,0:T(8,128)S(1)}) custom-call(s32[2]{0:T(128)S(1)} %pad_add_fusion.refs_0_.at, bf16[7168,128]{1,0:T(8,128)(2,1)S(1)} %bitcast.21, bf16[7168,128]{1,0:T(8,128)(2,1)S(1)} %bitcast.26, bf16[128,7168]{1,0:T(8,128)(2,1)S(1)} %bitcast.31), custom_call_target="tpu_custom_call" | custom-call | bytes 11010048 | tf_op jit(solution)/shard_map/pallas_call | solution.py:126
  24.6 15.1 %all-to-all-done = bf16[32,16,896]{2,1,0:T(8,128)(2,1)} async-done(((bf16[32,16,896]{2,1,0:T(8,128)(2,1)}), bf16[32,16,896]{2,1,0:T(8,128)(2,1)}, u32[]{:S(2)}, u32[]{:S(2)}) %all-to-all-start) | async-done | bytes 917536 | tf_op jit(solution)/shard_map/all_to_all | solution.py:400
  39.8 5.5 %all-to-all-start.1 = ((bf16[32,16,896]{2,1,0:T(8,128)(2,1)}), bf16[32,16,896]{2,1,0:T(8,128)(2,1)}, u32[]{:S(2)}, u32[]{:S(2)}) async-start(bf16[32,16,896]{2,1,0:T(8,128)(2,1)} %bitcast.35), calls=%async_computation.1 | async-start | bytes 1835008 | tf_op jit(solution)/shard_map/all_to_all | solution.py:400
  48.1 20.1 %all-to-all-done.1 = bf16[32,16,896]{2,1,0:T(8,128)(2,1)} async-done(((bf16[32,16,896]{2,1,0:T(8,128)(2,1)}), bf16[32,16,896]{2,1,0:T(8,128)(2,1)}, u32[]{:S(2)}, u32[]{:S(2)}) %all-to-all-start.1) | async-done | bytes 917536 | tf_op jit(solution)/shard_map/all_to_all | solution.py:400
  73.9 3.7 %shard_map.112 = (bf16[256,896]{1,0:T(8,128)(2,1)S(1)}, bf16[256,896]{1,0:T(8,128)(2,1)S(1)}, f32[512,512]{1,0:T(8,128)S(1)}, f32[8,128]{1,0:T(8,128)S(1)}) custom-call(s32[2]{0:T(128)S(1)} %pad_add_fusion.refs_0_.at, bf16[512,896]{1,0:T(8,128)(2,1)} %bitcast.7.refs_1_.refs_3_, bf16[512,896]{1,0:T(8,128)(2,1)} %collective-permute-done.1.refs_2_.refs_4_, ...), custom_call_target="tpu_custom_call" | custom-call | bytes 11141120 | tf_op jit(solution)/shard_map/pallas_call | solution.py:42
  77.7 2.7 %collective-permute-start.4 = (bf16[256,896]{1,0:T(8,128)(2,1)S(1)}, bf16[256,896]{1,0:T(8,128)(2,1)S(1)}, u32[]{:S(2)}, u32[]{:S(2)}) collective-permute-start(bf16[256,896]{1,0:T(8,128)(2,1)S(1)} %get-tuple-element.50), channel_id=1, source_target_pairs={{0,6},{1,7},{2,0},{3,1},{4,2},{5,3},{6,4},{7,5},{8,14},{9,15},{10,... | collective-permute-start | bytes 1376264 | tf_op jit(solution)/shard_map/ppermute | solution.py:366
  80.4 7.4 %collective-permute-done.6.refs_1_.refs_10_ = bf16[512,896]{1,0:T(8,128)(2,1)S(1)} collective-permute-done((bf16[512,896]{1,0:T(8,128)(2,1)}, bf16[512,896]{1,0:T(8,128)(2,1)S(1)}, u32[]{:S(2)}, u32[]{:S(2)}) %collective-permute-start.6) | collective-permute-done | bytes 917536 | tf_op jit(solution)/shard_map/ppermute | solution.py:366
  91.1 6.5 %collective-permute-done.3.refs_5_.refs_6_ = bf16[256,896]{1,0:T(8,128)(2,1)S(1)} collective-permute-done((bf16[256,896]{1,0:T(8,128)(2,1)S(1)}, bf16[256,896]{1,0:T(8,128)(2,1)S(1)}, u32[]{:S(2)}, u32[]{:S(2)}) %collective-permute-start.3) | collective-permute-done | bytes 458784 | tf_op jit(solution)/shard_map/ppermute | solution.py:366
  97.6 2.7 %shard_map.115 = (f32[512,512]{1,0:T(8,128)S(1)}, f32[512,256]{1,0:T(8,128)S(1)}, bf16[512,512]{1,0:T(8,128)(2,1)S(1)}) custom-call(s32[2]{0:T(128)S(1)} %pad_add_fusion.refs_0_.at, bf16[7168,128]{1,0:T(8,128)(2,1)S(1)} %bitcast.23, bf16[7168,128]{1,0:T(8,128)(2,1)S(1)} %bitcast.28, ...), custom_call_target="tpu_custom_call" | custom-call | bytes 15073280 | tf_op jit(solution)/shard_map/pallas_call | solution.py:42
  100.4 9.2 %collective-permute-start.9 = (bf16[512,512]{1,0:T(8,128)(2,1)S(1)}, bf16[512,512]{1,0:T(8,128)(2,1)S(1)}, u32[]{:S(2)}, u32[]{:S(2)}) collective-permute-start(bf16[512,512]{1,0:T(8,128)(2,1)S(1)} %get-tuple-element.60), channel_id=1, source_target_pairs={{0,1},{1,0},{2,3},{3,2},{4,5},{5,4},{6,7},{7,6},{8,9},{9,8},{10,11... | collective-permute-start | bytes 1572872 | tf_op jit(solution)/shard_map/ppermute | solution.py:370
  110.6 2.8 %collective-permute-start.10 = (bf16[512,256]{1,0:T(8,128)(2,1)S(1)}, bf16[512,256]{1,0:T(8,128)(2,1)S(1)}, u32[]{:S(2)}, u32[]{:S(2)}) collective-permute-start(bf16[512,256]{1,0:T(8,128)(2,1)S(1)} %get-tuple-element.61), channel_id=1, source_target_pairs={{0,1},{1,0},{2,3},{3,2},{4,5},{5,4},{6,7},{7,6},{8,9},{9,8},{10,11... | collective-permute-start | bytes 786440 | tf_op jit(solution)/shard_map/ppermute | solution.py:370
  118.8 2.5 %shard_map.118 = (bf16[256,896]{1,0:T(8,128)(2,1)S(1)}, bf16[256,896]{1,0:T(8,128)(2,1)S(1)}, f32[256,896]{1,0:T(8,128)S(1)}, f32[256,896]{1,0:T(8,128)S(1)}, f3...) custom-call(s32[2]{0:T(128)S(1)} %pad_add_fusion.refs_0_.at, ...), custom_call_target="tpu_custom_call" | custom-call | bytes 11798528 | tf_op jit(solution)/shard_map/pallas_call | solution.py:42
  121.4 2.7 %collective-permute-start.15 = (bf16[256,896]{1,0:T(8,128)(2,1)S(1)}, bf16[256,896]{1,0:T(8,128)(2,1)S(1)}, u32[]{:S(2)}, u32[]{:S(2)}) collective-permute-start(bf16[256,896]{1,0:T(8,128)(2,1)S(1)} %get-tuple-element.74), channel_id=1, source_target_pairs={{0,6},{1,7},{2,0},{3,1},{4,2},{5,3},{6,4},{7,5},{8,14},{9,15},{10,... | collective-permute-start | bytes 1376264 | tf_op jit(solution)/shard_map/ppermute | solution.py:366
  124.1 6.8 %shard_map.119 = (bf16[4,3,896,128]{3,2,1,0:T(8,128)(2,1)S(1)}, bf16[4,3,896,128]{3,2,1,0:T(8,128)(2,1)}, f32[8,128]{1,0:T(8,128)S(1)}) custom-call(s32[2]{0:T(128)S(1)} %pad_add_fusion.refs_0_.at, bf16[512,512]{1,0:T(8,128)(2,1)S(1)} %get-tuple-element.62.refs_1_, bf16[512,256]{1,0:T(8,128)(2,1)S(1)} %get-tuple-element.69.refs_2_, ...), custom_call_target="tpu_custom_call" | custom-call | bytes 13631488 | tf_op jit(solution)/shard_map/pallas_call | solution.py:42
  133.2 2.7 %collective-permute-start.16 = (bf16[256,896]{1,0:T(8,128)(2,1)S(1)}, bf16[256,896]{1,0:T(8,128)(2,1)S(1)}, u32[]{:S(2)}, u32[]{:S(2)}) collective-permute-start(bf16[256,896]{1,0:T(8,128)(2,1)S(1)} %get-tuple-element.75), channel_id=1, source_target_pairs={{0,6},{1,7},{2,0},{3,1},{4,2},{5,3},{6,4},{7,5},{8,14},{9,15},{10,... | collective-permute-start | bytes 1376264 | tf_op jit(solution)/shard_map/ppermute | solution.py:366
  135.8 13.1 %all_to_all.20 = f32[32,1,16]{2,1,0:T(1,128)S(1)} all-to-all(f32[32,1,16]{2,1,0:T(1,128)S(1)} %bitcast.44), channel_id=1, replica_groups=mesh['expert'=32,'hidden'=8] {'expert'}, dimensions={0} | all-to-all | bytes 4096 | tf_op jit(solution)/shard_map/all_to_all | solution.py:400
  150.7 3.4 %collective-permute-start.20 = (bf16[4,3,896,128]{3,2,1,0:T(8,128)(2,1)}, bf16[4,3,896,128]{3,2,1,0:T(8,128)(2,1)}, u32[]{:S(2)}, u32[]{:S(2)}) collective-permute-start(bf16[4,3,896,128]{3,2,1,0:T(8,128)(2,1)} %shard_map.123), channel_id=1, source_target_pairs={{0,1},{1,0},{2,3},{3,2},{4,5},{5,4},{6,7},{7,6},{8,9},{9,8},{10,11... | collective-permute-start | bytes 8257544 | tf_op jit(solution)/shard_map/ppermute | solution.py:370
  154.1 5.6 %all-to-all-start.3 = ((bf16[32,16,896]{2,1,0:T(8,128)(2,1)}), bf16[32,16,896]{2,1,0:T(8,128)(2,1)S(1)}, u32[]{:S(2)}, u32[]{:S(2)}) async-start(bf16[32,16,896]{2,1,0:T(8,128)(2,1)} %bitcast.14), calls=%async_computation.3 | async-start | bytes 1835008 | tf_op jit(solution)/shard_map/all_to_all | solution.py:400
  162.9 2.6 %collective-permute-done.18.refs_6_ = f32[32,16]{1,0:T(8,128)S(1)} collective-permute-done((f32[32,16]{1,0:T(8,128)S(1)}, f32[32,16]{1,0:T(8,128)S(1)}, u32[]{:S(2)}, u32[]{:S(2)}) %collective-permute-start.18) | collective-permute-done | bytes 2080 | tf_op jit(solution)/shard_map/ppermute | solution.py:366
  165.6 2.0 %shard_map.122 = (f32[8,32]{1,0:T(8,128)}, f32[8,128]{1,0:T(8,128)S(1)}) custom-call(s32[2]{0:T(128)S(1)} %pad_add_fusion.refs_0_.at, bf16[512,32]{1,0:T(8,128)(2,1)S(1)} %get-tuple-element.46.refs_1_, s32[8,32]{1,0:T(8,128)S(1)} %bitcast.43, bf16[8,32]{1,0:T(8,128)(2,1)S(1)} %bitcast.46, f32[32,16]{1,0:T(8,128)S(1)} %bitcast.40, ...), custom_call_target="tpu_custom_call" | custom-call | bytes 43520 | tf_op jit(solution)/shard_map/pallas_call | solution.py:42
  169.3 7.9 %shard_map.124 = (bf16[7168,128]{1,0:T(8,128)(2,1)}, bf16[7168,128]{1,0:T(8,128)(2,1)}, bf16[128,7168]{1,0:T(8,128)(2,1)}, f32[8,128]{1,0:T(8,128)S(1)}) custom-call(s32[2]{0:T(128)S(1)} %pad_add_fusion.refs_0_.at, bf16[4,3,896,128]{3,2,1,0:T(8,128)(2,1)S(1)} %copy-done.10, bf16[4,3,896,128]{3,2,1,0:T(8,128)(2,1)} %collective-permute-done.20.recv), custom_call_target="tpu_custom_call" | custom-call | bytes 11010048 | tf_op jit(solution)/shard_map/pallas_call | solution.py:317
  177.2 8.7 %all-to-all-done.3 = bf16[32,16,896]{2,1,0:T(8,128)(2,1)S(1)} async-done(((bf16[32,16,896]{2,1,0:T(8,128)(2,1)}), bf16[32,16,896]{2,1,0:T(8,128)(2,1)S(1)}, u32[]{:S(2)}, u32[]{:S(2)}) %all-to-all-start.3) | async-done | bytes 917536 | tf_op jit(solution)/shard_map/all_to_all | solution.py:400
  (71 shorter events, 37.0 us)
Async XLA Ops:
  4.5 35.2 %all-to-all-start = ((bf16[32,16,896]{2,1,0:T(8,128)(2,1)}), bf16[32,16,896]{2,1,0:T(8,128)(2,1)}, u32[]{:S(2)}, u32[]{:S(2)}) async-start(bf16[32,16,896]{2,1,0:T(8,128)(2,1)} %bitcast.6), calls=%async_computation | async-start | bytes 1835008 | tf_op jit(solution)/shard_map/all_to_all | solution.py:400
  21.4 49.5 %collective-permute-start = (bf16[4,3,896,128]{3,2,1,0:T(8,128)(2,1)}, bf16[4,3,896,128]{3,2,1,0:T(8,128)(2,1)S(1)}, u32[]{:S(2)}, u32[]{:S(2)}) collective-permute-start(bf16[4,3,896,128]{3,2,1,0:T(8,128)(2,1)} %get-tuple-element.47), channel_id=1, source_target_pairs={{0,1},{1,0},{2,3},{3,2},{4,5},{5,4},{6,7},{7,6},{8,9},{9,8},{10,11... | collective-permute-start | bytes 8257544 | tf_op jit(solution)/shard_map/ppermute | solution.py:370
  39.8 28.4 %all-to-all-start.1 = ((bf16[32,16,896]{2,1,0:T(8,128)(2,1)}), bf16[32,16,896]{2,1,0:T(8,128)(2,1)}, u32[]{:S(2)}, u32[]{:S(2)}) async-start(bf16[32,16,896]{2,1,0:T(8,128)(2,1)} %bitcast.35), calls=%async_computation.1 | async-start | bytes 1835008 | tf_op jit(solution)/shard_map/all_to_all | solution.py:400
  45.3 25.5 %collective-permute-start.2 = (bf16[512,896]{1,0:T(8,128)(2,1)}, bf16[512,896]{1,0:T(8,128)(2,1)}, u32[]{:S(2)}, u32[]{:S(2)}) collective-permute-start(bf16[512,896]{1,0:T(8,128)(2,1)} %bitcast.7.refs_1_.refs_3_), channel_id=1, source_target_pairs={{0,2},{1,3},{2,4},{3,5},{4,6},{5,7},{6,0},{7,1},{8,10},{9,11},{10,... | collective-permute-start | bytes 2752520 | tf_op jit(solution)/shard_map/ppermute | solution.py:366
  46.6 24.3 %collective-permute-start.1 = (bf16[512,896]{1,0:T(8,128)(2,1)}, bf16[512,896]{1,0:T(8,128)(2,1)}, u32[]{:S(2)}, u32[]{:S(2)}) collective-permute-start(bf16[512,896]{1,0:T(8,128)(2,1)} %bitcast.7.refs_1_.refs_3_), channel_id=1, source_target_pairs={{0,6},{1,7},{2,0},{3,1},{4,2},{5,3},{6,4},{7,5},{8,14},{9,15},{10,... | collective-permute-start | bytes 2752520 | tf_op jit(solution)/shard_map/ppermute | solution.py:366
  68.2 19.6 %collective-permute-start.6 = (bf16[512,896]{1,0:T(8,128)(2,1)}, bf16[512,896]{1,0:T(8,128)(2,1)S(1)}, u32[]{:S(2)}, u32[]{:S(2)}) collective-permute-start(bf16[512,896]{1,0:T(8,128)(2,1)} %bitcast.10.refs_8_), channel_id=1, source_target_pairs={{0,2},{1,3},{2,4},{3,5},{4,6},{5,7},{6,0},{7,1},{8,10},{9,11},{10,... | collective-permute-start | bytes 2752520 | tf_op jit(solution)/shard_map/ppermute | solution.py:366
  69.4 18.4 %collective-permute-start.5 = (bf16[512,896]{1,0:T(8,128)(2,1)}, bf16[512,896]{1,0:T(8,128)(2,1)S(1)}, u32[]{:S(2)}, u32[]{:S(2)}) collective-permute-start(bf16[512,896]{1,0:T(8,128)(2,1)} %bitcast.10.refs_8_), channel_id=1, source_target_pairs={{0,6},{1,7},{2,0},{3,1},{4,2},{5,3},{6,4},{7,5},{8,14},{9,15},{10,... | collective-permute-start | bytes 2752520 | tf_op jit(solution)/shard_map/ppermute | solution.py:366
  77.6 20.0 %collective-permute-start.3 = (bf16[256,896]{1,0:T(8,128)(2,1)S(1)}, bf16[256,896]{1,0:T(8,128)(2,1)S(1)}, u32[]{:S(2)}, u32[]{:S(2)}) collective-permute-start(bf16[256,896]{1,0:T(8,128)(2,1)S(1)} %get-tuple-element.49), channel_id=1, source_target_pairs={{0,2},{1,3},{2,4},{3,5},{4,6},{5,7},{6,0},{7,1},{8,10},{9,11},{10,... | collective-permute-start | bytes 1376264 | tf_op jit(solution)/shard_map/ppermute | solution.py:366
  77.7 19.9 %collective-permute-start.4 = (bf16[256,896]{1,0:T(8,128)(2,1)S(1)}, bf16[256,896]{1,0:T(8,128)(2,1)S(1)}, u32[]{:S(2)}, u32[]{:S(2)}) collective-permute-start(bf16[256,896]{1,0:T(8,128)(2,1)S(1)} %get-tuple-element.50), channel_id=1, source_target_pairs={{0,6},{1,7},{2,0},{3,1},{4,2},{5,3},{6,4},{7,5},{8,14},{9,15},{10,... | collective-permute-start | bytes 1376264 | tf_op jit(solution)/shard_map/ppermute | solution.py:366
  88.4 21.1 %collective-permute-start.7 = (bf16[256,896]{1,0:T(8,128)(2,1)S(1)}, bf16[256,896]{1,0:T(8,128)(2,1)S(1)}, u32[]{:S(2)}, u32[]{:S(2)}) collective-permute-start(bf16[256,896]{1,0:T(8,128)(2,1)S(1)} %get-tuple-element.56), channel_id=1, source_target_pairs={{0,2},{1,3},{2,4},{3,5},{4,6},{5,7},{6,0},{7,1},{8,10},{9,11},{10,... | collective-permute-start | bytes 1376264 | tf_op jit(solution)/shard_map/ppermute | solution.py:366
  89.4 20.1 %collective-permute-start.8 = (bf16[256,896]{1,0:T(8,128)(2,1)S(1)}, bf16[256,896]{1,0:T(8,128)(2,1)S(1)}, u32[]{:S(2)}, u32[]{:S(2)}) collective-permute-start(bf16[256,896]{1,0:T(8,128)(2,1)S(1)} %get-tuple-element.57), channel_id=1, source_target_pairs={{0,6},{1,7},{2,0},{3,1},{4,2},{5,3},{6,4},{7,5},{8,14},{9,15},{10,... | collective-permute-start | bytes 1376264 | tf_op jit(solution)/shard_map/ppermute | solution.py:366
  100.4 14.1 %collective-permute-start.9 = (bf16[512,512]{1,0:T(8,128)(2,1)S(1)}, bf16[512,512]{1,0:T(8,128)(2,1)S(1)}, u32[]{:S(2)}, u32[]{:S(2)}) collective-permute-start(bf16[512,512]{1,0:T(8,128)(2,1)S(1)} %get-tuple-element.60), channel_id=1, source_target_pairs={{0,1},{1,0},{2,3},{3,2},{4,5},{5,4},{6,7},{7,6},{8,9},{9,8},{10,11... | collective-permute-start | bytes 1572872 | tf_op jit(solution)/shard_map/ppermute | solution.py:370
  110.6 3.9 %collective-permute-start.10 = (bf16[512,256]{1,0:T(8,128)(2,1)S(1)}, bf16[512,256]{1,0:T(8,128)(2,1)S(1)}, u32[]{:S(2)}, u32[]{:S(2)}) collective-permute-start(bf16[512,256]{1,0:T(8,128)(2,1)S(1)} %get-tuple-element.61), channel_id=1, source_target_pairs={{0,1},{1,0},{2,3},{3,2},{4,5},{5,4},{6,7},{7,6},{8,9},{9,8},{10,11... | collective-permute-start | bytes 786440 | tf_op jit(solution)/shard_map/ppermute | solution.py:370
  115.9 16.4 %collective-permute-start.11 = (bf16[256,896]{1,0:T(8,128)(2,1)S(1)}, bf16[256,896]{1,0:T(8,128)(2,1)S(1)}, u32[]{:S(2)}, u32[]{:S(2)}) collective-permute-start(bf16[256,896]{1,0:T(8,128)(2,1)S(1)} %get-tuple-element.67), channel_id=1, source_target_pairs={{0,2},{1,3},{2,4},{3,5},{4,6},{5,7},{6,0},{7,1},{8,10},{9,11},{10,... | collective-permute-start | bytes 1376264 | tf_op jit(solution)/shard_map/ppermute | solution.py:366
  117.2 15.2 %collective-permute-start.12 = (bf16[256,896]{1,0:T(8,128)(2,1)S(1)}, bf16[256,896]{1,0:T(8,128)(2,1)S(1)}, u32[]{:S(2)}, u32[]{:S(2)}) collective-permute-start(bf16[256,896]{1,0:T(8,128)(2,1)S(1)} %get-tuple-element.68), channel_id=1, source_target_pairs={{0,6},{1,7},{2,0},{3,1},{4,2},{5,3},{6,4},{7,5},{8,14},{9,15},{10,... | collective-permute-start | bytes 1376264 | tf_op jit(solution)/shard_map/ppermute | solution.py:366
  121.3 27.6 %collective-permute-start.14 = (bf16[256,896]{1,0:T(8,128)(2,1)S(1)}, bf16[256,896]{1,0:T(8,128)(2,1)S(1)}, u32[]{:S(2)}, u32[]{:S(2)}) collective-permute-start(bf16[256,896]{1,0:T(8,128)(2,1)S(1)} %get-tuple-element.73), channel_id=1, source_target_pairs={{0,2},{1,3},{2,4},{3,5},{4,6},{5,7},{6,0},{7,1},{8,10},{9,11},{10,... | collective-permute-start | bytes 1376264 | tf_op jit(solution)/shard_map/ppermute | solution.py:366
  121.4 27.5 %collective-permute-start.15 = (bf16[256,896]{1,0:T(8,128)(2,1)S(1)}, bf16[256,896]{1,0:T(8,128)(2,1)S(1)}, u32[]{:S(2)}, u32[]{:S(2)}) collective-permute-start(bf16[256,896]{1,0:T(8,128)(2,1)S(1)} %get-tuple-element.74), channel_id=1, source_target_pairs={{0,6},{1,7},{2,0},{3,1},{4,2},{5,3},{6,4},{7,5},{8,14},{9,15},{10,... | collective-permute-start | bytes 1376264 | tf_op jit(solution)/shard_map/ppermute | solution.py:366
  133.1 15.8 %collective-permute-start.13 = (bf16[256,896]{1,0:T(8,128)(2,1)S(1)}, bf16[256,896]{1,0:T(8,128)(2,1)S(1)}, u32[]{:S(2)}, u32[]{:S(2)}) collective-permute-start(bf16[256,896]{1,0:T(8,128)(2,1)S(1)} %get-tuple-element.72), channel_id=1, source_target_pairs={{0,2},{1,3},{2,4},{3,5},{4,6},{5,7},{6,0},{7,1},{8,10},{9,11},{10,... | collective-permute-start | bytes 1376264 | tf_op jit(solution)/shard_map/ppermute | solution.py:366
  133.2 15.8 %collective-permute-start.16 = (bf16[256,896]{1,0:T(8,128)(2,1)S(1)}, bf16[256,896]{1,0:T(8,128)(2,1)S(1)}, u32[]{:S(2)}, u32[]{:S(2)}) collective-permute-start(bf16[256,896]{1,0:T(8,128)(2,1)S(1)} %get-tuple-element.75), channel_id=1, source_target_pairs={{0,6},{1,7},{2,0},{3,1},{4,2},{5,3},{6,4},{7,5},{8,14},{9,15},{10,... | collective-permute-start | bytes 1376264 | tf_op jit(solution)/shard_map/ppermute | solution.py:366
  150.7 16.8 %collective-permute-start.20 = (bf16[4,3,896,128]{3,2,1,0:T(8,128)(2,1)}, bf16[4,3,896,128]{3,2,1,0:T(8,128)(2,1)}, u32[]{:S(2)}, u32[]{:S(2)}) collective-permute-start(bf16[4,3,896,128]{3,2,1,0:T(8,128)(2,1)} %shard_map.123), channel_id=1, source_target_pairs={{0,1},{1,0},{2,3},{3,2},{4,5},{5,4},{6,7},{7,6},{8,9},{9,8},{10,11... | collective-permute-start | bytes 8257544 | tf_op jit(solution)/shard_map/ppermute | solution.py:370
  154.1 31.8 %all-to-all-start.3 = ((bf16[32,16,896]{2,1,0:T(8,128)(2,1)}), bf16[32,16,896]{2,1,0:T(8,128)(2,1)S(1)}, u32[]{:S(2)}, u32[]{:S(2)}) async-start(bf16[32,16,896]{2,1,0:T(8,128)(2,1)} %bitcast.14), calls=%async_computation.3 | async-start | bytes 1835008 | tf_op jit(solution)/shard_map/all_to_all | solution.py:400
  159.7 3.2 %collective-permute-start.19 = (f32[32,16]{1,0:T(8,128)S(1)}, f32[32,16]{1,0:T(8,128)S(1)}, u32[]{:S(2)}, u32[]{:S(2)}) collective-permute-start(f32[32,16]{1,0:T(8,128)S(1)} %bitcast.37), channel_id=1, source_target_pairs={{0,6},{1,7},{2,0},{3,1},{4,2},{5,3},{6,4},{7,5},{8,14},{9,15},{10,... | collective-permute-start | bytes 6152 | tf_op jit(solution)/shard_map/ppermute | solution.py:366
  161.2 4.4 %collective-permute-start.18 = (f32[32,16]{1,0:T(8,128)S(1)}, f32[32,16]{1,0:T(8,128)S(1)}, u32[]{:S(2)}, u32[]{:S(2)}) collective-permute-start(f32[32,16]{1,0:T(8,128)S(1)} %bitcast.38), channel_id=1, source_target_pairs={{0,4},{1,5},{2,6},{3,7},{4,0},{5,1},{6,2},{7,3},{8,12},{9,13},{10,... | collective-permute-start | bytes 6152 | tf_op jit(solution)/shard_map/ppermute | solution.py:366
  161.2 4.4 %collective-permute-start.17 = (f32[32,16]{1,0:T(8,128)S(1)}, f32[32,16]{1,0:T(8,128)S(1)}, u32[]{:S(2)}, u32[]{:S(2)}) collective-permute-start(f32[32,16]{1,0:T(8,128)S(1)} %bitcast.39), channel_id=1, source_target_pairs={{0,2},{1,3},{2,4},{3,5},{4,6},{5,7},{6,0},{7,1},{8,10},{9,11},{10,... | collective-permute-start | bytes 6152 | tf_op jit(solution)/shard_map/ppermute | solution.py:366
  (14 other events, 101.4 us)

commit v7 on v6

--- a/solution.py
+++ b/solution.py
@@ -269,9 +269,9 @@
         out[span, :] = (own[span, :] + left[...].astype(F32) + right[...].astype(F32)).astype(BF)
 
 
-def grads_body(at, d, act_rows, *refs):
-    x, dy, (keep, send) = refs[:5], refs[5:10], refs[10:]
-    block, units = keep.shape[2:]
+def grads_body(at, d, *refs):
+    x, (keep, send) = refs[:5], refs[5:]
+    units = keep.shape[3]
     half = d.shape[0] // 2
     for r in range(CHIPS):
         total = None
@@ -280,40 +280,45 @@
             total = value if total is None else total + value
         for i, (out, kind) in enumerate(((keep, 0), (send, 0), (keep, 1), (send, 1))):
             out[r, kind] = total[:, i * units : (i + 1) * units].astype(BF)
+
+
+def down_body(at, act_rows, *refs):
+    dy, (keep, send) = refs[:5], refs[5:]
+    units = keep.shape[1]
+    half = act_rows.shape[0] // 2
+    for r in range(CHIPS):
         total = None
         for lo, part in halves_of(dy, r, half):
             value = mm(act_rows[lo : lo + half, :], part, TN)
             total = value if total is None else total + value
-        total = total.astype(BF)
-        for j in range(0, block, units):
-            keep[r, 2, j : j + units, :] = total[:units, j : j + units]
-            send[r, 2, j : j + units, :] = total[units:, j : j + units]
-
-
-def place_body(at, keep, recv, gate, up, down, token):
+        keep[r] = total[:units, :].astype(BF)
+        send[r] = total[units:, :].astype(BF)
+
+
+def place_body(at, keep, recv, down_keep, down_recv, gate, up, down, token):
     token[...] = jnp.zeros((8, 128), F32)
-    units = gate.shape[1]
     mine = lax.rem(pl.program_id(0), 2) == at[1]
 
-    def put(held):
-        gate[...] = held[0, 0]
-        up[...] = held[0, 1]
-        for j in range(0, gate.shape[0], units):
-            down[:, j : j + units] = held[0, 2, j : j + units, :]
+    def put(tall, wide):
+        gate[...] = tall[0, 0]
+        up[...] = tall[0, 1]
+        down[...] = wide[0]
 
     @pl.when(mine)
     def _():
-        put(keep)
+        put(keep, down_keep)
 
     @pl.when(jnp.logical_not(mine))
     def _():
-        put(recv)
-
-
-def place(at, keep, recv):
+        put(recv, down_recv)
+
+
+def place(at, keep, recv, down_keep, down_recv):
     _, _, block, units = keep.shape
     depth = 2 * CHIPS * block
-    source = pl.BlockSpec((1, 3, block, units), lambda b, at: ((b // 2 + CHIPS - at[0]) % CHIPS, 0, 0, 0))
+    where = lambda b, at: (b // 2 + CHIPS - at[0]) % CHIPS
+    source = pl.BlockSpec((1, 2, block, units), lambda b, at: (where(b, at), 0, 0, 0))
+    wide = pl.BlockSpec((1, units, block), lambda b, at: (where(b, at), 0, 0))
     return pl.pallas_call(
         place_body,
         out_shape=(
@@ -327,7 +332,7 @@
         grid_spec=pltpu.PrefetchScalarGridSpec(
             num_scalar_prefetch=1,
             grid=(2 * CHIPS,),
-            in_specs=[source, source],
+            in_specs=[source, source, wide, wide],
             out_specs=[
                 pl.BlockSpec((block, units), lambda b, at: (b, 0)),
                 pl.BlockSpec((block, units), lambda b, at: (b, 0)),
@@ -335,7 +340,7 @@
                 pl.BlockSpec((8, 128), lambda b, at: (0, 0)),
             ],
         ),
-    )(at, keep, recv)
+    )(at, keep, recv, down_keep, down_recv)
 
 
 def finish_body(at, pick, back, grad):
@@ -459,8 +464,8 @@
     left_b, right_a = to(to_right, 1), to(to_left, -1)
     keep, send, *token = call(
         grads_body,
-        (shape((CHIPS, 3, block, units), BF),) * 2,
-        (at, d, act_rows, *x, *dy),
+        (shape((CHIPS, 2, block, units), BF),) * 2,
+        (at, d, *x),
         after=token,
         token=True,
     )
@@ -475,7 +480,10 @@
         token=True,
     )
     returned = over_experts(total)
-    *grads, placed = place(at, keep, swap(behind(send, token[0])))
+    down_keep, down_send = call(
+        down_body, (shape((CHIPS, units, block), BF),) * 2, (at, act_rows, *dy), after=token
+    )
+    *grads, placed = place(at, keep, swap(behind(send, token[0])), down_keep, swap(down_send))
     grad_gating, gated = call(
         gating_body,
         (shape((topk, count), F32),),

time: 188 us -> 186 us (0.989); the launches traced: 187 us -> 183 us
  waiting for transfers between devices: 62.6 us -> 57 us
    all_to_all x3, waiting for transfers between devices: 43.9 us -> 36.9 us  [over_experts(): lax.all_to_all(split, 'expert', split_axis=0, concat_axis=0, tiled=True)]
    unnamed x28 -> x46, local copies, waits for them, and re-layouts: 10.9 us -> 11.5 us
    ppermute x4 -> x5, starting transfers between devices: 16.6 us -> 16.6 us  [swap(): return lax.ppermute(value, 'hidden', [(i, i ^ 1) for i in range(2 * CHIPS)])]
    pallas_call x13 -> x14, Pallas kernels: 28 us -> 28 us  [call(): pl.pallas_call(run, out_shape=out_shape + ((shape((8, 128), F32),) if tok...]
  transfers between devices with their start and end apart: 24 -> 25, of which waited for: 8 -> 8; matrix products, arithmetic and copies ran while one was open for 0% -> 0% of each run, Pallas kernels for 17% -> 17%
where the time goes in v7:
time: 186 us; the launch traced here: 183 us
  starting transfers between devices  61.9 us (33%)
  waiting for transfers between devices  57 us (31%)
  Pallas kernels  37.9 us (20%)
  blocking collectives  13.1 us (7%)
  local copies, waits for them, and re-layouts  12.5 us (7%)
    all_to_all x3, waiting for transfers between devices, over_experts(): lax.all_to_all(split, 'expert', split_axis=0, concat_axis=0, tiled=True)  36.9 us
    pallas_call x14, Pallas kernels, call(): pl.pallas_call(run, out_shape=out_shape + ((shape((8, 128), F32),) if tok...  28 us
    all_to_all x3, starting transfers between devices, over_experts(): lax.all_to_all(split, 'expert', split_axis=0, concat_axis=0, tiled=True)  22.6 us
    ppermute x17, starting transfers between devices, to(): lax.ppermute(value, 'hidden', [(i, (i + 2 * shift) % size) for i in range...  22.6 us
    ppermute x17, waiting for transfers between devices, to(): lax.ppermute(value, 'hidden', [(i, (i + 2 * shift) % size) for i in range...  19 us
    ppermute x5, starting transfers between devices, swap(): return lax.ppermute(value, 'hidden', [(i, i ^ 1) for i in range(2 * CHIPS)])  16.6 us
    all_to_all x1, blocking collectives, over_experts(): lax.all_to_all(split, 'expert', split_axis=0, concat_axis=0, tiled=True)  13.1 us
    unnamed x46, local copies, waits for them, and re-layouts  11.5 us
  transfers between devices with their start and end apart: 25, of which 8 were waited for; matrix products, arithmetic and copies ran while one was open for 0% of the time, Pallas kernels for 17%

profile of v7, /device:TPU:17, one launch (start us, length us, event | category | flops | bytes accessed | tf_op | source)
XLA Modules:
  0.0 183.4 jit_solution(15397688492529330075)
XLA Ops:
  2.4 2.1 %shard_map.110 = (bf16[512,896]{1,0:T(8,128)(2,1)}, bf16[512,32]{1,0:T(8,128)(2,1)S(1)}) custom-call(s32[2]{0:T(128)S(1)} %pad_add_fusion.refs_0_.at, s32[8,32]{1,0:T(8,128)S(1)} %bitcast.42, bf16[32,896]{1,0:T(8,128)(2,1)S(1)} %get-tuple-element.92.refs_2_), custom_call_target="tpu_custom_call" | custom-call | bytes 1008640 | tf_op jit(solution)/shard_map/pallas_call | solution.py:42
  4.5 11.1 %all-to-all-start = ((bf16[32,16,896]{2,1,0:T(8,128)(2,1)}), bf16[32,16,896]{2,1,0:T(8,128)(2,1)}, u32[]{:S(2)}, u32[]{:S(2)}) async-start(bf16[32,16,896]{2,1,0:T(8,128)(2,1)} %bitcast.6), calls=%async_computation | async-start | bytes 1835008 | tf_op jit(solution)/shard_map/all_to_all | solution.py:405
  18.6 2.8 %shard_map.111 = (bf16[4,3,896,128]{3,2,1,0:T(8,128)(2,1)}, f32[8,128]{1,0:T(8,128)S(1)}) custom-call(s32[2]{0:T(128)S(1)} %pad_add_fusion.refs_0_.at, bf16[7168,128]{1,0:T(8,128)(2,1)S(1)} %bitcast.21, bf16[7168,128]{1,0:T(8,128)(2,1)S(1)} %bitcast.26, bf16[128,7168]{1,0:T(8,128)(2,1)S(1)} %bitcast.31), custom_call_target="tpu_custom_call" | custom-call | bytes 11010048 | tf_op jit(solution)/shard_map/pallas_call | solution.py:126
  24.7 15.1 %all-to-all-done = bf16[32,16,896]{2,1,0:T(8,128)(2,1)} async-done(((bf16[32,16,896]{2,1,0:T(8,128)(2,1)}), bf16[32,16,896]{2,1,0:T(8,128)(2,1)}, u32[]{:S(2)}, u32[]{:S(2)}) %all-to-all-start) | async-done | bytes 917536 | tf_op jit(solution)/shard_map/all_to_all | solution.py:405
  39.8 5.5 %all-to-all-start.1 = ((bf16[32,16,896]{2,1,0:T(8,128)(2,1)}), bf16[32,16,896]{2,1,0:T(8,128)(2,1)}, u32[]{:S(2)}, u32[]{:S(2)}) async-start(bf16[32,16,896]{2,1,0:T(8,128)(2,1)} %bitcast.35), calls=%async_computation.1 | async-start | bytes 1835008 | tf_op jit(solution)/shard_map/all_to_all | solution.py:405
  48.1 20.1 %all-to-all-done.1 = bf16[32,16,896]{2,1,0:T(8,128)(2,1)} async-done(((bf16[32,16,896]{2,1,0:T(8,128)(2,1)}), bf16[32,16,896]{2,1,0:T(8,128)(2,1)}, u32[]{:S(2)}, u32[]{:S(2)}) %all-to-all-start.1) | async-done | bytes 917536 | tf_op jit(solution)/shard_map/all_to_all | solution.py:405
  73.9 3.8 %shard_map.112 = (bf16[256,896]{1,0:T(8,128)(2,1)S(1)}, bf16[256,896]{1,0:T(8,128)(2,1)S(1)}, f32[512,512]{1,0:T(8,128)S(1)}, f32[8,128]{1,0:T(8,128)S(1)}) custom-call(s32[2]{0:T(128)S(1)} %pad_add_fusion.refs_0_.at, bf16[512,896]{1,0:T(8,128)(2,1)} %bitcast.7.refs_1_.refs_2_, bf16[512,896]{1,0:T(8,128)(2,1)} %collective-permute-done.1.refs_2_.refs_3_, ...), custom_call_target="tpu_custom_call" | custom-call | bytes 11141120 | tf_op jit(solution)/shard_map/pallas_call | solution.py:42
  77.8 2.7 %collective-permute-start.4 = (bf16[256,896]{1,0:T(8,128)(2,1)S(1)}, bf16[256,896]{1,0:T(8,128)(2,1)S(1)}, u32[]{:S(2)}, u32[]{:S(2)}) collective-permute-start(bf16[256,896]{1,0:T(8,128)(2,1)S(1)} %get-tuple-element.52), channel_id=1, source_target_pairs={{0,6},{1,7},{2,0},{3,1},{4,2},{5,3},{6,4},{7,5},{8,14},{9,15},{10,... | collective-permute-start | bytes 1376264 | tf_op jit(solution)/shard_map/ppermute | solution.py:371
  80.5 7.3 %collective-permute-done.6.refs_1_.refs_10_.refs_4_ = bf16[512,896]{1,0:T(8,128)(2,1)S(1)} collective-permute-done((bf16[512,896]{1,0:T(8,128)(2,1)}, bf16[512,896]{1,0:T(8,128)(2,1)S(1)}, u32[]{:S(2)}, u32[]{:S(2)}) %collective-permute-start.6) | collective-permute-done | bytes 917536 | tf_op jit(solution)/shard_map/ppermute | solution.py:371
  91.1 6.5 %collective-permute-done.3.refs_5_ = bf16[256,896]{1,0:T(8,128)(2,1)S(1)} collective-permute-done((bf16[256,896]{1,0:T(8,128)(2,1)S(1)}, bf16[256,896]{1,0:T(8,128)(2,1)S(1)}, u32[]{:S(2)}, u32[]{:S(2)}) %collective-permute-start.3) | collective-permute-done | bytes 458784 | tf_op jit(solution)/shard_map/ppermute | solution.py:371
  97.6 2.7 %shard_map.115 = (f32[512,512]{1,0:T(8,128)S(1)}, f32[512,256]{1,0:T(8,128)S(1)}, bf16[512,512]{1,0:T(8,128)(2,1)S(1)}) custom-call(s32[2]{0:T(128)S(1)} %pad_add_fusion.refs_0_.at, bf16[7168,128]{1,0:T(8,128)(2,1)S(1)} %bitcast.23, bf16[7168,128]{1,0:T(8,128)(2,1)S(1)} %bitcast.28, ...), custom_call_target="tpu_custom_call" | custom-call | bytes 15073280 | tf_op jit(solution)/shard_map/pallas_call | solution.py:42
  100.4 9.2 %collective-permute-start.9 = (bf16[512,512]{1,0:T(8,128)(2,1)S(1)}, bf16[512,512]{1,0:T(8,128)(2,1)S(1)}, u32[]{:S(2)}, u32[]{:S(2)}) collective-permute-start(bf16[512,512]{1,0:T(8,128)(2,1)S(1)} %get-tuple-element.62), channel_id=1, source_target_pairs={{0,1},{1,0},{2,3},{3,2},{4,5},{5,4},{6,7},{7,6},{8,9},{9,8},{10,11... | collective-permute-start | bytes 1572872 | tf_op jit(solution)/shard_map/ppermute | solution.py:375
  110.6 2.7 %collective-permute-start.10 = (bf16[512,256]{1,0:T(8,128)(2,1)S(1)}, bf16[512,256]{1,0:T(8,128)(2,1)S(1)}, u32[]{:S(2)}, u32[]{:S(2)}) collective-permute-start(bf16[512,256]{1,0:T(8,128)(2,1)S(1)} %get-tuple-element.63), channel_id=1, source_target_pairs={{0,1},{1,0},{2,3},{3,2},{4,5},{5,4},{6,7},{7,6},{8,9},{9,8},{10,11... | collective-permute-start | bytes 786440 | tf_op jit(solution)/shard_map/ppermute | solution.py:375
  119.3 2.5 %shard_map.118 = (bf16[256,896]{1,0:T(8,128)(2,1)S(1)}, bf16[256,896]{1,0:T(8,128)(2,1)S(1)}, f32[256,896]{1,0:T(8,128)S(1)}, f32[256,896]{1,0:T(8,128)S(1)}, f3...) custom-call(s32[2]{0:T(128)S(1)} %pad_add_fusion.refs_0_.at, ...), custom_call_target="tpu_custom_call" | custom-call | bytes 11798528 | tf_op jit(solution)/shard_map/pallas_call | solution.py:42
  121.9 2.7 %collective-permute-start.15 = (bf16[256,896]{1,0:T(8,128)(2,1)S(1)}, bf16[256,896]{1,0:T(8,128)(2,1)S(1)}, u32[]{:S(2)}, u32[]{:S(2)}) collective-permute-start(bf16[256,896]{1,0:T(8,128)(2,1)S(1)} %get-tuple-element.75), channel_id=1, source_target_pairs={{0,6},{1,7},{2,0},{3,1},{4,2},{5,3},{6,4},{7,5},{8,14},{9,15},{10,... | collective-permute-start | bytes 1376264 | tf_op jit(solution)/shard_map/ppermute | solution.py:371
  124.6 5.1 %shard_map.119 = (bf16[4,2,896,128]{3,2,1,0:T(8,128)(2,1)S(1)}, bf16[4,2,896,128]{3,2,1,0:T(8,128)(2,1)}, f32[8,128]{1,0:T(8,128)S(1)}) custom-call(s32[2]{0:T(128)S(1)} %pad_add_fusion.refs_0_.at, bf16[512,512]{1,0:T(8,128)(2,1)S(1)} %get-tuple-element.64.refs_1_, bf16[512,896]{1,0:T(8,128)(2,1)} %bitcast.7.refs_1_.refs_2_, ...), custom_call_target="tpu_custom_call" | custom-call | bytes 7864320 | tf_op jit(solution)/shard_map/pallas_call | solution.py:42
  131.7 2.7 %collective-permute-start.16 = (bf16[256,896]{1,0:T(8,128)(2,1)S(1)}, bf16[256,896]{1,0:T(8,128)(2,1)S(1)}, u32[]{:S(2)}, u32[]{:S(2)}) collective-permute-start(bf16[256,896]{1,0:T(8,128)(2,1)S(1)} %get-tuple-element.76), channel_id=1, source_target_pairs={{0,6},{1,7},{2,0},{3,1},{4,2},{5,3},{6,4},{7,5},{8,14},{9,15},{10,... | collective-permute-start | bytes 1376264 | tf_op jit(solution)/shard_map/ppermute | solution.py:371
  134.4 13.1 %all_to_all.20 = f32[32,1,16]{2,1,0:T(1,128)S(1)} all-to-all(f32[32,1,16]{2,1,0:T(1,128)S(1)} %bitcast.45), channel_id=1, replica_groups=mesh['expert'=32,'hidden'=8] {'expert'}, dimensions={0} | all-to-all | bytes 4096 | tf_op jit(solution)/shard_map/all_to_all | solution.py:405
  151.9 6.0 %all-to-all-start.3 = ((bf16[32,16,896]{2,1,0:T(8,128)(2,1)}), bf16[32,16,896]{2,1,0:T(8,128)(2,1)S(1)}, u32[]{:S(2)}, u32[]{:S(2)}) async-start(bf16[32,16,896]{2,1,0:T(8,128)(2,1)} %bitcast.36), calls=%async_computation.3 | async-start | bytes 1835008 | tf_op jit(solution)/shard_map/all_to_all | solution.py:405
  159.9 2.6 %shard_map.124 = (bf16[4,128,896]{2,1,0:T(8,128)(2,1)S(1)}, bf16[4,128,896]{2,1,0:T(8,128)(2,1)S(1)}) custom-call(s32[2]{0:T(128)S(1)} %pad_add_fusion.refs_0_.at, bf16[512,256]{1,0:T(8,128)(2,1)S(1)} %copy-done.19, bf16[512,896]{1,0:T(8,128)(2,1)} %bitcast.10.refs_8_.refs_2_, bf16[512,896]{1,0:T(8,128)(2,1)S(1)} %copy-done.11, ...), custom_call_target="tpu_custom_call" | custom-call | bytes 5767168 | tf_op jit(solution)/shard_map/pallas_call | solution.py:42
  164.2 2.7 %collective-permute-start.19 = (f32[32,16]{1,0:T(8,128)S(1)}, f32[32,16]{1,0:T(8,128)S(1)}, u32[]{:S(2)}, u32[]{:S(2)}) collective-permute-start(f32[32,16]{1,0:T(8,128)S(1)} %bitcast.38), channel_id=1, source_target_pairs={{0,6},{1,7},{2,0},{3,1},{4,2},{5,3},{6,4},{7,5},{8,14},{9,15},{10,... | collective-permute-start | bytes 6152 | tf_op jit(solution)/shard_map/ppermute | solution.py:371
  167.8 3.4 %collective-permute-done.18.refs_6_ = f32[32,16]{1,0:T(8,128)S(1)} collective-permute-done((f32[32,16]{1,0:T(8,128)S(1)}, f32[32,16]{1,0:T(8,128)S(1)}, u32[]{:S(2)}, u32[]{:S(2)}) %collective-permute-start.18) | collective-permute-done | bytes 2080 | tf_op jit(solution)/shard_map/ppermute | solution.py:371
  171.2 2.0 %shard_map.122 = (f32[8,32]{1,0:T(8,128)}, f32[8,128]{1,0:T(8,128)S(1)}) custom-call(s32[2]{0:T(128)S(1)} %pad_add_fusion.refs_0_.at, bf16[512,32]{1,0:T(8,128)(2,1)S(1)} %get-tuple-element.48.refs_1_, s32[8,32]{1,0:T(8,128)S(1)} %bitcast.44, bf16[8,32]{1,0:T(8,128)(2,1)S(1)} %bitcast.47, f32[32,16]{1,0:T(8,128)S(1)} %bitcast.41, ...), custom_call_target="tpu_custom_call" | custom-call | bytes 43520 | tf_op jit(solution)/shard_map/pallas_call | solution.py:42
  173.1 7.1 %shard_map.125 = (bf16[7168,128]{1,0:T(8,128)(2,1)}, bf16[7168,128]{1,0:T(8,128)(2,1)}, bf16[128,7168]{1,0:T(8,128)(2,1)}, f32[8,128]{1,0:T(8,128)S(1)}) custom-call(s32[2]{0:T(128)S(1)} %pad_add_fusion.refs_0_.at, bf16[4,2,896,128]{3,2,1,0:T(8,128)(2,1)S(1)} %copy-done.16, bf16[4,2,896,128]{3,2,1,0:T(8,128)(2,1)} %collective-permute-done.20.recv, ...), custom_call_target="tpu_custom_call" | custom-call | bytes 11010048 | tf_op jit(solution)/shard_map/pallas_call | solution.py:322
  (92 shorter events, 41.1 us)
Async XLA Ops:
  4.5 35.2 %all-to-all-start = ((bf16[32,16,896]{2,1,0:T(8,128)(2,1)}), bf16[32,16,896]{2,1,0:T(8,128)(2,1)}, u32[]{:S(2)}, u32[]{:S(2)}) async-start(bf16[32,16,896]{2,1,0:T(8,128)(2,1)} %bitcast.6), calls=%async_computation | async-start | bytes 1835008 | tf_op jit(solution)/shard_map/all_to_all | solution.py:405
  21.4 49.5 %collective-permute-start = (bf16[4,3,896,128]{3,2,1,0:T(8,128)(2,1)}, bf16[4,3,896,128]{3,2,1,0:T(8,128)(2,1)S(1)}, u32[]{:S(2)}, u32[]{:S(2)}) collective-permute-start(bf16[4,3,896,128]{3,2,1,0:T(8,128)(2,1)} %get-tuple-element.49), channel_id=1, source_target_pairs={{0,1},{1,0},{2,3},{3,2},{4,5},{5,4},{6,7},{7,6},{8,9},{9,8},{10,11... | collective-permute-start | bytes 8257544 | tf_op jit(solution)/shard_map/ppermute | solution.py:375
  39.8 28.4 %all-to-all-start.1 = ((bf16[32,16,896]{2,1,0:T(8,128)(2,1)}), bf16[32,16,896]{2,1,0:T(8,128)(2,1)}, u32[]{:S(2)}, u32[]{:S(2)}) async-start(bf16[32,16,896]{2,1,0:T(8,128)(2,1)} %bitcast.35), calls=%async_computation.1 | async-start | bytes 1835008 | tf_op jit(solution)/shard_map/all_to_all | solution.py:405
  45.3 25.5 %collective-permute-start.2 = (bf16[512,896]{1,0:T(8,128)(2,1)}, bf16[512,896]{1,0:T(8,128)(2,1)}, u32[]{:S(2)}, u32[]{:S(2)}) collective-permute-start(bf16[512,896]{1,0:T(8,128)(2,1)} %bitcast.7.refs_1_.refs_2_), channel_id=1, source_target_pairs={{0,2},{1,3},{2,4},{3,5},{4,6},{5,7},{6,0},{7,1},{8,10},{9,11},{10,... | collective-permute-start | bytes 2752520 | tf_op jit(solution)/shard_map/ppermute | solution.py:371
  46.6 24.3 %collective-permute-start.1 = (bf16[512,896]{1,0:T(8,128)(2,1)}, bf16[512,896]{1,0:T(8,128)(2,1)}, u32[]{:S(2)}, u32[]{:S(2)}) collective-permute-start(bf16[512,896]{1,0:T(8,128)(2,1)} %bitcast.7.refs_1_.refs_2_), channel_id=1, source_target_pairs={{0,6},{1,7},{2,0},{3,1},{4,2},{5,3},{6,4},{7,5},{8,14},{9,15},{10,... | collective-permute-start | bytes 2752520 | tf_op jit(solution)/shard_map/ppermute | solution.py:371
  68.2 19.6 %collective-permute-start.6 = (bf16[512,896]{1,0:T(8,128)(2,1)}, bf16[512,896]{1,0:T(8,128)(2,1)S(1)}, u32[]{:S(2)}, u32[]{:S(2)}) collective-permute-start(bf16[512,896]{1,0:T(8,128)(2,1)} %bitcast.10.refs_8_.refs_2_), channel_id=1, source_target_pairs={{0,2},{1,3},{2,4},{3,5},{4,6},{5,7},{6,0},{7,1},{8,10},{9,11},{10,... | collective-permute-start | bytes 2752520 | tf_op jit(solution)/shard_map/ppermute | solution.py:371
  69.4 18.4 %collective-permute-start.5 = (bf16[512,896]{1,0:T(8,128)(2,1)}, bf16[512,896]{1,0:T(8,128)(2,1)S(1)}, u32[]{:S(2)}, u32[]{:S(2)}) collective-permute-start(bf16[512,896]{1,0:T(8,128)(2,1)} %bitcast.10.refs_8_.refs_2_), channel_id=1, source_target_pairs={{0,6},{1,7},{2,0},{3,1},{4,2},{5,3},{6,4},{7,5},{8,14},{9,15},{10,... | collective-permute-start | bytes 2752520 | tf_op jit(solution)/shard_map/ppermute | solution.py:371
  77.7 19.9 %collective-permute-start.3 = (bf16[256,896]{1,0:T(8,128)(2,1)S(1)}, bf16[256,896]{1,0:T(8,128)(2,1)S(1)}, u32[]{:S(2)}, u32[]{:S(2)}) collective-permute-start(bf16[256,896]{1,0:T(8,128)(2,1)S(1)} %get-tuple-element.51), channel_id=1, source_target_pairs={{0,2},{1,3},{2,4},{3,5},{4,6},{5,7},{6,0},{7,1},{8,10},{9,11},{10,... | collective-permute-start | bytes 1376264 | tf_op jit(solution)/shard_map/ppermute | solution.py:371
  77.8 19.8 %collective-permute-start.4 = (bf16[256,896]{1,0:T(8,128)(2,1)S(1)}, bf16[256,896]{1,0:T(8,128)(2,1)S(1)}, u32[]{:S(2)}, u32[]{:S(2)}) collective-permute-start(bf16[256,896]{1,0:T(8,128)(2,1)S(1)} %get-tuple-element.52), channel_id=1, source_target_pairs={{0,6},{1,7},{2,0},{3,1},{4,2},{5,3},{6,4},{7,5},{8,14},{9,15},{10,... | collective-permute-start | bytes 1376264 | tf_op jit(solution)/shard_map/ppermute | solution.py:371
  88.4 21.2 %collective-permute-start.7 = (bf16[256,896]{1,0:T(8,128)(2,1)S(1)}, bf16[256,896]{1,0:T(8,128)(2,1)S(1)}, u32[]{:S(2)}, u32[]{:S(2)}) collective-permute-start(bf16[256,896]{1,0:T(8,128)(2,1)S(1)} %get-tuple-element.58), channel_id=1, source_target_pairs={{0,2},{1,3},{2,4},{3,5},{4,6},{5,7},{6,0},{7,1},{8,10},{9,11},{10,... | collective-permute-start | bytes 1376264 | tf_op jit(solution)/shard_map/ppermute | solution.py:371
  89.4 20.2 %collective-permute-start.8 = (bf16[256,896]{1,0:T(8,128)(2,1)S(1)}, bf16[256,896]{1,0:T(8,128)(2,1)S(1)}, u32[]{:S(2)}, u32[]{:S(2)}) collective-permute-start(bf16[256,896]{1,0:T(8,128)(2,1)S(1)} %get-tuple-element.59), channel_id=1, source_target_pairs={{0,6},{1,7},{2,0},{3,1},{4,2},{5,3},{6,4},{7,5},{8,14},{9,15},{10,... | collective-permute-start | bytes 1376264 | tf_op jit(solution)/shard_map/ppermute | solution.py:371
  100.4 14.1 %collective-permute-start.9 = (bf16[512,512]{1,0:T(8,128)(2,1)S(1)}, bf16[512,512]{1,0:T(8,128)(2,1)S(1)}, u32[]{:S(2)}, u32[]{:S(2)}) collective-permute-start(bf16[512,512]{1,0:T(8,128)(2,1)S(1)} %get-tuple-element.62), channel_id=1, source_target_pairs={{0,1},{1,0},{2,3},{3,2},{4,5},{5,4},{6,7},{7,6},{8,9},{9,8},{10,11... | collective-permute-start | bytes 1572872 | tf_op jit(solution)/shard_map/ppermute | solution.py:375
  110.6 3.9 %collective-permute-start.10 = (bf16[512,256]{1,0:T(8,128)(2,1)S(1)}, bf16[512,256]{1,0:T(8,128)(2,1)S(1)}, u32[]{:S(2)}, u32[]{:S(2)}) collective-permute-start(bf16[512,256]{1,0:T(8,128)(2,1)S(1)} %get-tuple-element.63), channel_id=1, source_target_pairs={{0,1},{1,0},{2,3},{3,2},{4,5},{5,4},{6,7},{7,6},{8,9},{9,8},{10,11... | collective-permute-start | bytes 786440 | tf_op jit(solution)/shard_map/ppermute | solution.py:375
  116.6 14.2 %collective-permute-start.11 = (bf16[256,896]{1,0:T(8,128)(2,1)S(1)}, bf16[256,896]{1,0:T(8,128)(2,1)S(1)}, u32[]{:S(2)}, u32[]{:S(2)}) collective-permute-start(bf16[256,896]{1,0:T(8,128)(2,1)S(1)} %get-tuple-element.69), channel_id=1, source_target_pairs={{0,2},{1,3},{2,4},{3,5},{4,6},{5,7},{6,0},{7,1},{8,10},{9,11},{10,... | collective-permute-start | bytes 1376264 | tf_op jit(solution)/shard_map/ppermute | solution.py:371
  117.8 13.0 %collective-permute-start.12 = (bf16[256,896]{1,0:T(8,128)(2,1)S(1)}, bf16[256,896]{1,0:T(8,128)(2,1)S(1)}, u32[]{:S(2)}, u32[]{:S(2)}) collective-permute-start(bf16[256,896]{1,0:T(8,128)(2,1)S(1)} %get-tuple-element.70), channel_id=1, source_target_pairs={{0,6},{1,7},{2,0},{3,1},{4,2},{5,3},{6,4},{7,5},{8,14},{9,15},{10,... | collective-permute-start | bytes 1376264 | tf_op jit(solution)/shard_map/ppermute | solution.py:371
  121.8 25.7 %collective-permute-start.14 = (bf16[256,896]{1,0:T(8,128)(2,1)S(1)}, bf16[256,896]{1,0:T(8,128)(2,1)S(1)}, u32[]{:S(2)}, u32[]{:S(2)}) collective-permute-start(bf16[256,896]{1,0:T(8,128)(2,1)S(1)} %get-tuple-element.74), channel_id=1, source_target_pairs={{0,2},{1,3},{2,4},{3,5},{4,6},{5,7},{6,0},{7,1},{8,10},{9,11},{10,... | collective-permute-start | bytes 1376264 | tf_op jit(solution)/shard_map/ppermute | solution.py:371
  121.9 25.6 %collective-permute-start.15 = (bf16[256,896]{1,0:T(8,128)(2,1)S(1)}, bf16[256,896]{1,0:T(8,128)(2,1)S(1)}, u32[]{:S(2)}, u32[]{:S(2)}) collective-permute-start(bf16[256,896]{1,0:T(8,128)(2,1)S(1)} %get-tuple-element.75), channel_id=1, source_target_pairs={{0,6},{1,7},{2,0},{3,1},{4,2},{5,3},{6,4},{7,5},{8,14},{9,15},{10,... | collective-permute-start | bytes 1376264 | tf_op jit(solution)/shard_map/ppermute | solution.py:371
  131.6 17.6 %collective-permute-start.13 = (bf16[256,896]{1,0:T(8,128)(2,1)S(1)}, bf16[256,896]{1,0:T(8,128)(2,1)S(1)}, u32[]{:S(2)}, u32[]{:S(2)}) collective-permute-start(bf16[256,896]{1,0:T(8,128)(2,1)S(1)} %get-tuple-element.73), channel_id=1, source_target_pairs={{0,2},{1,3},{2,4},{3,5},{4,6},{5,7},{6,0},{7,1},{8,10},{9,11},{10,... | collective-permute-start | bytes 1376264 | tf_op jit(solution)/shard_map/ppermute | solution.py:371
  131.7 17.5 %collective-permute-start.16 = (bf16[256,896]{1,0:T(8,128)(2,1)S(1)}, bf16[256,896]{1,0:T(8,128)(2,1)S(1)}, u32[]{:S(2)}, u32[]{:S(2)}) collective-permute-start(bf16[256,896]{1,0:T(8,128)(2,1)S(1)} %get-tuple-element.76), channel_id=1, source_target_pairs={{0,6},{1,7},{2,0},{3,1},{4,2},{5,3},{6,4},{7,5},{8,14},{9,15},{10,... | collective-permute-start | bytes 1376264 | tf_op jit(solution)/shard_map/ppermute | solution.py:371
  150.1 23.0 %collective-permute-start.20 = (bf16[4,2,896,128]{3,2,1,0:T(8,128)(2,1)}, bf16[4,2,896,128]{3,2,1,0:T(8,128)(2,1)}, u32[]{:S(2)}, u32[]{:S(2)}) collective-permute-start(bf16[4,2,896,128]{3,2,1,0:T(8,128)(2,1)} %shard_map.123), channel_id=1, source_target_pairs={{0,1},{1,0},{2,3},{3,2},{4,5},{5,4},{6,7},{7,6},{8,9},{9,8},{10,11... | collective-permute-start | bytes 5505032 | tf_op jit(solution)/shard_map/ppermute | solution.py:375
  151.9 29.9 %all-to-all-start.3 = ((bf16[32,16,896]{2,1,0:T(8,128)(2,1)}), bf16[32,16,896]{2,1,0:T(8,128)(2,1)S(1)}, u32[]{:S(2)}, u32[]{:S(2)}) async-start(bf16[32,16,896]{2,1,0:T(8,128)(2,1)} %bitcast.36), calls=%async_computation.3 | async-start | bytes 1835008 | tf_op jit(solution)/shard_map/all_to_all | solution.py:405
  162.5 10.6 %collective-permute-start.21 = (bf16[4,128,896]{2,1,0:T(8,128)(2,1)S(1)}, bf16[4,128,896]{2,1,0:T(8,128)(2,1)S(1)}, u32[]{:S(2)}, u32[]{:S(2)}) collective-permute-start(bf16[4,128,896]{2,1,0:T(8,128)(2,1)S(1)} %get-tuple-element.85), channel_id=1, source_target_pairs={{0,1},{1,0},{2,3},{3,2},{4,5},{5,4},{6,7},{7,6},{8,9},{9,8},{10,11... | collective-permute-start | bytes 2752520 | tf_op jit(solution)/shard_map/ppermute | solution.py:375
  166.9 4.2 %collective-permute-start.18 = (f32[32,16]{1,0:T(8,128)S(1)}, f32[32,16]{1,0:T(8,128)S(1)}, u32[]{:S(2)}, u32[]{:S(2)}) collective-permute-start(f32[32,16]{1,0:T(8,128)S(1)} %bitcast.39), channel_id=1, source_target_pairs={{0,4},{1,5},{2,6},{3,7},{4,0},{5,1},{6,2},{7,3},{8,12},{9,13},{10,... | collective-permute-start | bytes 6152 | tf_op jit(solution)/shard_map/ppermute | solution.py:371
  167.0 4.2 %collective-permute-start.17 = (f32[32,16]{1,0:T(8,128)S(1)}, f32[32,16]{1,0:T(8,128)S(1)}, u32[]{:S(2)}, u32[]{:S(2)}) collective-permute-start(f32[32,16]{1,0:T(8,128)S(1)} %bitcast.40), channel_id=1, source_target_pairs={{0,2},{1,3},{2,4},{3,5},{4,6},{5,7},{6,0},{7,1},{8,10},{9,11},{10,... | collective-permute-start | bytes 6152 | tf_op jit(solution)/shard_map/ppermute | solution.py:371
  (24 other events, 162.5 us)
